TPU v7x, 256 devices: a whole 4x4x8 slice. The times are simulated.
256 devices in a mesh: prow: 8 (over z), pcol: 32 (over x, y, core).
Axes of the slice: x: 4, y: 4, z: 8, core: 2. Of those that a mesh axis runs over, the one named last changes fastest.
Arguments:
- hamiltonian: float32 [8, 2048, 2, 8192], P(None, 'prow', None, 'pcol'), may hold values from -7 to 7, as said below
Outputs:
- reduced: float32 [8, 2048, 2, 8192], P(None, 'prow', None, 'pcol')
Inputs may be any that keep to these rules, and one draw needn't show every extreme that they name: `hamiltonian`: symmetric; the panel A[256:, :256] has full column rank and I + K^T is invertible.
All inputs are finite; a program needn't handle non-finite values.
Results may differ from a plain program's by a relative error of at most 0.00011.
Values sent between devices are 32-bit elements; how exact they have to be, the bound alone decides.
No kernel may reach another device: no remote copies, remote signals or barrier semaphores. Data moves between devices by JAX's collectives and lax.ppermute only.
A program may use at most 128 MiB of HBM per device.

v0:
```python
import jax
import jax.numpy as jnp
from jax import lax
from jax.sharding import PartitionSpec as P


def spread(shard, axis, root):
    mine = lax.axis_index(axis) == root
    return lax.psum(jnp.where(mine, shard, jnp.zeros_like(shard)), axis)


def small_inverse(k_top, ident):
    hp = lax.Precision.HIGHEST
    matrix = ident + k_top.T
    normal = jnp.dot(matrix.T, matrix, precision=hp, preferred_element_type=jnp.float32)
    factor = jnp.linalg.cholesky(normal)
    return jax.scipy.linalg.cho_solve((factor, True), matrix.T)


def body(hamiltonian):
    hp = lax.Precision.HIGHEST
    rows_loc, width, cols_loc, _ = hamiltonian.shape
    prow_count = lax.axis_size("prow")
    pcol_count = lax.axis_size("pcol")
    prow_at = lax.axis_index("prow")
    pcol_at = lax.axis_index("pcol")
    row_block = jnp.arange(rows_loc, dtype=jnp.int32) * prow_count + prow_at
    col_block = jnp.arange(cols_loc, dtype=jnp.int32) * pcol_count + pcol_at
    ident = jnp.eye(width, dtype=jnp.float32)
    panel = spread(hamiltonian[:, :, 0, :], "pcol", 0)
    panel = jnp.where((row_block >= 1)[:, None, None], panel, 0.0)
    flat = panel.reshape(rows_loc * width, width)
    gram_part = jnp.dot(flat.T, flat, precision=hp, preferred_element_type=jnp.float32)
    top_part = jnp.sum(jnp.where((row_block == 1)[:, None, None], panel, 0.0), axis=0)
    gram, top = lax.psum((gram_part, top_part), "prow")
    lower = jnp.linalg.cholesky(gram)
    basis = jax.scipy.linalg.solve_triangular(lower, flat.T, lower=True).T
    k_top = jax.scipy.linalg.solve_triangular(lower, top.T, lower=True).T
    mixer = small_inverse(k_top, ident)
    y_rows = basis.reshape(rows_loc, width, width) + jnp.where(
        (row_block == 1)[:, None, None], ident[None], 0.0
    )
    picked = (
        jnp.arange(cols_loc, dtype=jnp.int32) * (pcol_count // prow_count) + pcol_at // prow_count
    )
    source = pcol_at % prow_count
    y_cols = spread(y_rows[picked], "prow", source)
    y_flat = y_rows.reshape(rows_loc * width, width)
    yc_flat = y_cols.reshape(cols_loc * width, width)
    matrix = hamiltonian.reshape(rows_loc * width, cols_loc * width)
    applied_part = jnp.dot(matrix, yc_flat, precision=hp, preferred_element_type=jnp.float32)
    applied = lax.psum(applied_part, "pcol")
    proj = lax.psum(
        jnp.dot(y_flat.T, applied, precision=hp, preferred_element_type=jnp.float32), "prow"
    )
    core = jnp.dot(jnp.dot(mixer.T, proj, precision=hp), mixer, precision=hp)
    live_rows = jnp.repeat(row_block >= 1, width)[:, None]
    shifted = jnp.dot(applied, mixer, precision=hp, preferred_element_type=jnp.float32)
    w_rows = jnp.where(
        live_rows,
        shifted - 0.5 * jnp.dot(y_flat, core, precision=hp, preferred_element_type=jnp.float32),
        0.0,
    )
    w_cols = spread(w_rows.reshape(rows_loc, width, width)[picked], "prow", source).reshape(
        cols_loc * width, width
    )
    updated = (
        matrix - jnp.dot(y_flat, w_cols.T, precision=hp) - jnp.dot(w_rows, yc_flat.T, precision=hp)
    )
    updated = updated.reshape(rows_loc, width, cols_loc, width)
    band_col = jnp.where((row_block == 1)[:, None, None], -lower.T[None], 0.0)
    in_col = (col_block == 0)[None, None, :, None] & (row_block >= 1)[:, None, None, None]
    updated = jnp.where(in_col, band_col[:, :, None, :], updated)
    band_row = jnp.where((col_block == 1)[None, :, None], -lower[:, None, :], 0.0)
    in_row = (row_block == 0)[:, None, None, None] & (col_block >= 1)[None, None, :, None]
    return jnp.where(in_row, band_row[None], updated)


def solution(mesh):
    return jax.shard_map(
        body,
        mesh=mesh,
        in_specs=(P(None, "prow", None, "pcol"),),
        out_specs=P(None, "prow", None, "pcol"),
        check_vma=False,
    )
```

profile of v0, /device:TPU:1, one launch (start us, length us, event | category | flops | bytes accessed | tf_op | source)
XLA Modules:
  0.0 751.5 jit_solution(12954962271223460986)
XLA Ops:
  6.5 1.6 slice-done
  8.1 1.5 fusion.2
  9.8 122.0 %all-reduce.9.cloned.1.call-done = f32[8,256,256]{2,1,0:T(8,128)} async-done(((f32[8,256,256]{2,1,0:T(8,128)}), f32[8,256,256]{2,1,0:T(8,128)}) %all-reduce.9.cloned.1.call-update) | async-done | bytes 2097168 | tf_op jit(solution)/shard_map/psum | solution.py:9
  131.8 2.7 select_reduce_fusion
  134.4 4.2 convolution_bitcast_fusion.1
  139.0 67.6 %all-reduce.11.cloned.1.call-done = f32[256,256]{0,1:T(8,128)} async-done(((f32[256,256]{0,1:T(8,128)}), f32[256,256]{0,1:T(8,128)}) %all-reduce.11.cloned.1.call-update) | async-done | bytes 262160 | tf_op jit(solution)/shard_map/psum | solution.py:35
  206.6 1.1 copy.14
  208.7 11.7 %cholesky.130 = f32[128,128]{1,0:T(8,128)S(1)} custom-call(f32[128,128]{1,0:T(8,128)S(1)} %cholesky.194), custom_call_target="Cholesky" | custom-call | tf_op jit(solution)/shard_map/jit(cholesky)/cholesky | solution.py:36
  220.5 9.8 %custom-call.23 = f32[1,128,128]{1,2,0:T(8,128)S(1)} custom-call(f32[1,128,128]{2,1,0:T(8,128)S(1)} %get-tuple-element.72), custom_call_target="InvertDiagBlocksLowerTriangular" | custom-call | tf_op jit(solution)/shard_map/jit(cholesky)/cholesky | solution.py:36
  230.7 11.7 %cholesky.147 = f32[128,128]{1,0:T(8,128)S(1)} custom-call(f32[128,128]{1,0:T(8,128)S(1)} %convolution_subtract_fusion.5), custom_call_target="Cholesky" | custom-call | tf_op jit(solution)/shard_map/jit(cholesky)/cholesky | solution.py:36
  246.0 4.4 while.6
  246.9 1.4 bitcast_dynamic-update-slice_fusion.4
  248.9 1.4 bitcast_dynamic-update-slice_fusion.4
  251.0 19.7 %custom-call.19 = f32[2,128,128]{1,2,0:T(8,128)S(1)} custom-call(f32[2,128,128]{2,1,0:T(8,128)S(1)} %get-tuple-element.22), custom_call_target="InvertDiagBlocksLowerTriangular" | custom-call | tf_op jit(solution)/shard_map/jit(_solve_triangular)/triangular_solve | solution.py:37
  270.6 1.1 fusion.3
  271.7 2.6 convolution_subtract_fusion
  274.4 1.1 fusion.26
  275.5 1.0 copy.15
  276.5 1.5 maximum_bitcast_fusion
  278.0 2.9 copy.28
  280.9 3.5 broadcast_select_fusion
  284.4 1.4 gather_fusion
  287.2 4.6 copy.31
  291.8 67.8 %all-reduce.13.cloned.1.call-done = f32[512,256]{1,0:T(8,128)} async-done(((f32[512,256]{1,0:T(8,128)}), f32[512,256]{1,0:T(8,128)}) %all-reduce.13.cloned.1.call-update) | async-done | bytes 524304 | tf_op jit(solution)/shard_map/psum | solution.py:9
  359.7 10.4 %convolution_bitcast_fusion = f32[2048,256]{0,1:T(8,128)} fusion(f32[512,256]{1,0:T(8,128)} %all-reduce.13.cloned.1.call-done, f32[2048,512]{1,0:T(8,128)} %bitcast.123), kind=kOutput, calls=%fused_computation.8 | convolution fusion | flops 3221225472 | bytes 6815744 | tf_op jit(solution)/shard_map/dot_general | solution.py:51
  370.4 1.9 copy.27
  372.3 2.2 select_add_fusion.1
  374.5 116.2 %all-reduce.15.cloned.1.call-done = f32[2048,256]{0,1:T(8,128)} async-done(((f32[2048,256]{0,1:T(8,128)}), f32[2048,256]{0,1:T(8,128)}) %all-reduce.15.cloned.1.call-update) | async-done | bytes 2097168 | tf_op jit(solution)/shard_map/psum | solution.py:52
  490.7 4.2 fusion.41
  496.3 67.7 %all-reduce.19.cloned.1.call-done = (f32[256,256]{0,1:T(8,128)}, f32[256,256]{1,0:T(8,128)}) async-done(((f32[256,256]{0,1:T(8,128)}, f32[256,256]{1,0:T(8,128)}), (f32[256,256]{0,1:T(8,128)}, f32[256,256]{1,0:T(8,128)})) %all-reduce.19.cloned.1.call-update) | async-done | bytes 524304 | tf_op jit(solution)/shard_map/psum | solution.py:35
  563.9 1.2 fusion.15
  565.2 1.3 convolution_subtract_fusion.3
  567.7 11.7 %cholesky.164 = f32[128,128]{1,0:T(8,128)S(1)} custom-call(f32[128,128]{1,0:T(8,128)S(1)} %cholesky.197), custom_call_target="Cholesky" | custom-call | tf_op jit(solution)/shard_map/jit(cholesky)/cholesky | solution.py:16
  579.4 9.8 %custom-call.25 = f32[1,128,128]{1,2,0:T(8,128)S(1)} custom-call(f32[1,128,128]{2,1,0:T(8,128)S(1)} %get-tuple-element.68), custom_call_target="InvertDiagBlocksLowerTriangular" | custom-call | tf_op jit(solution)/shard_map/jit(cholesky)/cholesky | solution.py:16
  589.7 11.7 %cholesky.181 = f32[128,128]{1,0:T(8,128)S(1)} custom-call(f32[128,128]{1,0:T(8,128)S(1)} %convolution_subtract_fusion.4), custom_call_target="Cholesky" | custom-call | tf_op jit(solution)/shard_map/jit(cholesky)/cholesky | solution.py:16
  604.3 4.3 while.7
  605.1 1.4 bitcast_dynamic-update-slice_fusion.5
  607.2 1.4 bitcast_dynamic-update-slice_fusion.5
  608.6 19.7 %custom-call.20 = f32[2,128,128]{1,2,0:T(8,128)S(1)} custom-call(f32[2,128,128]{2,1,0:T(8,128)S(1)} %get-tuple-element.30), custom_call_target="InvertDiagBlocksLowerTriangular" | custom-call | tf_op jit(solution)/shard_map/jit(_cho_solve)/triangular_solve | solution.py:17
  631.2 2.0 fusion.12
  633.2 3.6 fusion.1
  636.8 3.1 copy.29
  640.0 2.2 gather_fusion.1
  643.5 71.6 %all-reduce.17.cloned.1.call-done = f32[512,256]{1,0:T(8,128)} async-done(((f32[512,256]{1,0:T(8,128)}), f32[512,256]{1,0:T(8,128)}) %all-reduce.17.cloned.1.call-update) | async-done | bytes 524304 | tf_op jit(solution)/shard_map/psum | solution.py:9
  715.1 7.9 %fusion.42 = f32[2048,512]{1,0:T(8,128)S(1)} fusion(f32[2048,256]{0,1:T(8,128)S(1)} %select_add_fusion.1, f32[512,256]{1,0:T(8,128)} %all-reduce.17.cloned.1.call-done), kind=kOutput, calls=%fused_computation.110 | convolution fusion | flops 3221225472 | bytes 6815744 | tf_op jit(solution)/shard_map/dot_general | solution.py:68
  723.0 8.3 %subtract_subtract_fusion = f32[2048,512]{1,0:T(8,128)} fusion(f32[2048,512]{1,0:T(8,128)S(1)} %bitcast.124, f32[2048,512]{1,0:T(8,128)S(1)} %fusion.42, f32[2048,256]{0,1:T(8,128)S(1)} %copy-done.1, f32[512,256]{1,0:T(8,128)S(1)} %copy-done.7), kind=kOutput, calls=%fused_computation.7 | convolution fusion | flops 3223322624 | bytes 15204352 | tf_op jit(solution)/shard_map/dot_general | solution.py:68
  731.3 6.3 reshape.195
  737.6 6.5 select_select_fusion
  (102 shorter events, 17.4 us)
Async XLA Ops:
  6.5 125.3 %all-reduce.9.cloned.1.call-start = ((), (), s32[]{:S(2)}) async-start(), calls=%async_computation | async-start | bytes 4194304 | tf_op jit(solution)/shard_map/psum | solution.py:9
  6.5 1.6 slice-start
  9.7 196.9 %all-reduce.11.cloned.1.call-start = ((), (), s32[]{:S(2)}) async-start(), calls=%async_computation.1 | async-start | bytes 524288 | tf_op jit(solution)/shard_map/psum | solution.py:35
  138.6 221.0 %all-reduce.13.cloned.1.call-start = ((), (), s32[]{:S(2)}) async-start(), calls=%async_computation.2 | async-start | bytes 1048576 | tf_op jit(solution)/shard_map/psum | solution.py:9
  250.4 0.6 copy-start.12
  251.0 19.7 %copy-start.8 = (f32[256,256]{1,0:T(8,128)}, f32[256,256]{1,0:T(8,128)S(1)}, u32[]{:S(2)}) copy-start(f32[256,256]{1,0:T(8,128)S(1)} %get-tuple-element.192) | copy-start | bytes 786436
  274.4 1.1 copy-start.5
  275.5 2.5 copy-start.2
  286.7 204.0 %all-reduce.15.cloned.1.call-start = ((), (), s32[]{:S(2)}) async-start(), calls=%async_computation.3 | async-start | bytes 4194304 | tf_op jit(solution)/shard_map/psum | solution.py:52
  370.1 193.8 %all-reduce.19.cloned.1.call-start = ((), (), s32[]{:S(2)}) async-start(), calls=%async_computation.5 | async-start | bytes 1048576 | tf_op jit(solution)/shard_map/psum | solution.py:35
  494.9 220.2 %all-reduce.17.cloned.1.call-start = ((), (), s32[]{:S(2)}) async-start(), calls=%async_computation.4 | async-start | bytes 1048576 | tf_op jit(solution)/shard_map/psum | solution.py:9
  566.8 37.4 %copy-start.13 = (s32[2,2]{1,0:T(2,128)S(1)}, s32[2,2]{1,0:T(2,128)}, u32[]{:S(2)}) copy-start(s32[2,2]{1,0:T(2,128)} %copy-done.12) | copy-start | bytes 52
  589.5 40.7 %copy-start.9 = (f32[256,256]{1,0:T(8,128)S(1)}, f32[256,256]{1,0:T(8,128)}, u32[]{:S(2)}) copy-start(f32[256,256]{1,0:T(8,128)} %get-tuple-element.56) | copy-start | bytes 786436
  628.3 2.9 copy-start.3
  640.0 3.1 copy-start.10
  640.0 3.2 copy-start.6
  640.0 3.2 copy-start.11
  643.5 79.5 %copy-start.7 = (f32[512,256]{1,0:T(8,128)S(1)}, f32[512,256]{1,0:T(8,128)}, u32[]{:S(2)}) copy-start(f32[512,256]{1,0:T(8,128)} %all-reduce.13.cloned.1.call-done) | copy-start | bytes 1572868
  715.1 7.9 %copy-start = (f32[256,8,2,256]{3,1,2,0:T(8,128)S(1)}, f32[256,8,2,256]{3,1,2,0:T(8,128)}, u32[]{:S(2)}) copy-start(f32[256,8,2,256]{3,1,2,0:T(8,128)} %copy.31) | copy-start | bytes 12582916
  715.1 7.9 %copy-start.1 = (f32[2048,256]{0,1:T(8,128)S(1)}, f32[2048,256]{0,1:T(8,128)}, u32[]{:S(2)}) copy-start(f32[2048,256]{0,1:T(8,128)} %fusion.1) | copy-start | bytes 6291460
  731.3 6.3 copy-start.4
Sparse Core Ops, SparseCore 0:
  10.6 121.1 all-reduce.8
  138.7 67.7 all-reduce.10
  286.8 72.8 all-reduce.12
  370.2 120.3 all-reduce.14
  495.0 68.8 all-reduce.18
  643.2 71.8 all-reduce.16
where the time goes:
time: 759 us; the launch traced here: 751 us
  waiting for transfers between devices  513 us (68%)
  other arithmetic  132 us (17%)
  matrix products  52.5 us (7%)
  local copies, waits for them, and re-layouts  35.5 us (5%)
  between operations  17.2 us (2%)
    psum x3, waiting for transfers between devices, spread(): return lax.psum(jnp.where(mine, shard, jnp.zeros_like(shard)), axis)  261 us
    psum x2, waiting for transfers between devices, body(): gram, top = lax.psum((gram_part, top_part), 'prow')  135 us
    psum x1, waiting for transfers between devices, body(): applied = lax.psum(applied_part, 'pcol')  116 us
    another operation x7, other arithmetic, small_inverse(): factor = jnp.linalg.cholesky(normal)  34.7 us
    another operation x7, other arithmetic, body(): lower = jnp.linalg.cholesky(gram)  34.7 us
    another operation x2, other arithmetic, small_inverse(): return jax.scipy.linalg.cho_solve((factor, True), matrix.T)  19.7 us
    another operation x2, other arithmetic, body(): basis = jax.scipy.linalg.solve_triangular(lower, flat.T, lower=True).T  19.7 us
  transfers between devices with their start and end apart: 6, of which 6 were waited for; matrix products, arithmetic and copies ran while one was open for 1% of the time, Pallas kernels for 0%

commit v1 on v0

v1 whole, which is shorter than its diff:
```python
import jax
import jax.numpy as jnp
from jax import lax
from jax.sharding import PartitionSpec as P

HP = lax.Precision.HIGHEST
XS, YS, CORES = 4, 4, 2
CHIPS = XS * YS
PLANE = [[q * CORES + k for q in range(CHIPS)] for k in range(CORES)]
YLINE = [[(x * YS + y) * CORES + k for y in range(YS)] for x in range(XS) for k in range(CORES)]
SWAP = [(i, i ^ 1) for i in range(CHIPS * CORES)]


def mm(a, b):
    return jnp.dot(a, b, precision=HP, preferred_element_type=jnp.float32)


def mm_tn(a, b):
    return lax.dot_general(a, b, (((0,), (0,)), ((), ())), precision=HP, preferred_element_type=jnp.float32)


def mm_nt(a, b):
    return lax.dot_general(a, b, (((1,), (1,)), ((), ())), precision=HP, preferred_element_type=jnp.float32)


def share(piece, axis, count, groups=None):
    copies = jnp.broadcast_to(piece[None], (count,) + piece.shape)
    return lax.all_to_all(copies, axis, 0, 0, axis_index_groups=groups)


def both_halves(half, core):
    other = lax.ppermute(half, "pcol", SWAP)
    first = core == 0
    return jnp.stack([jnp.where(first, half, other), jnp.where(first, other, half)])


def small_math(gram, top, ident):
    lower = jnp.linalg.cholesky(gram)
    inv = jax.scipy.linalg.solve_triangular(lower, ident, lower=True)
    matrix = ident + mm_nt(inv, top)
    normal = mm_tn(matrix, matrix)
    factor = jnp.linalg.cholesky(normal)
    mixer = jax.scipy.linalg.cho_solve((factor, True), matrix.T)
    return lower, inv, mixer


def body(hamiltonian):
    nl, nb, nm, _ = hamiltonian.shape
    nz = lax.axis_size("prow")
    prow = lax.axis_index("prow")
    pcol = lax.axis_index("pcol")
    core = pcol % CORES
    yat = (pcol // CORES) % YS
    row_block = jnp.arange(nl, dtype=jnp.int32) * nz + prow
    col_block = jnp.arange(nm, dtype=jnp.int32) * (CHIPS * CORES) + pcol
    ident = jnp.eye(nb, dtype=jnp.float32)
    sub = nb // (CHIPS * CORES)
    matrix = hamiltonian.reshape(nl * nb, nm * nb)

    top_row = jnp.where((col_block >= 1)[None, :, None] & (prow == 0), hamiltonian[0], 0.0)
    p_cols_t = lax.psum(top_row, "prow").reshape(nb, nm * nb)

    panel = jnp.where((row_block >= 1)[:, None, None], hamiltonian[:, :, 0, :], 0.0)
    flat = panel.reshape(nl * nb, nb)
    gram_part = mm_tn(flat, flat)
    packet = jnp.concatenate(
        [
            panel.reshape(nl, CORES, CHIPS, sub, nb).transpose(1, 2, 0, 3, 4),
            gram_part.reshape(CORES, CHIPS, 1, sub, nb),
        ],
        axis=2,
    )
    given = lax.ppermute(packet[1], "pcol", [(0, 1)])
    outgoing = jnp.where(pcol == 0, packet[0], given)
    mine = lax.all_to_all(outgoing, "pcol", 0, 0, axis_index_groups=PLANE)[0]
    stacked = share(jnp.stack([mine[nl], mine[0]]), "prow", nz)
    gram_piece = jnp.sum(stacked[:, 0], axis=0)
    top_piece = stacked[1, 1]
    half = share(
        jnp.concatenate([mine[:nl], gram_piece[None], top_piece[None]]), "pcol", CHIPS, PLANE
    )
    whole = both_halves(half, core)
    p_rows = whole[:, :, :nl].transpose(2, 0, 1, 3, 4).reshape(nl * nb, nb)
    gram = whole[:, :, nl].reshape(nb, nb)
    top = whole[:, :, nl + 1].reshape(nb, nb)

    lower, inv, mixer = small_math(gram, top, ident)

    y_rows = mm_nt(p_rows, inv).reshape(nl, nb, nb)
    y_rows = y_rows + jnp.where((row_block == 1)[:, None, None], ident[None], 0.0)
    y_rows = y_rows.reshape(nl * nb, nb)
    y_cols = mm_nt(p_cols_t.T, inv).reshape(nm, nb, nb)
    y_cols = y_cols + jnp.where((col_block == 1)[:, None, None], ident[None], 0.0)
    y_cols = y_cols.reshape(nm * nb, nb)

    live = jnp.where((row_block >= 1)[:, None, None], y_rows.reshape(nl, nb, nb), 0.0)
    part = mm_tn(matrix, live.reshape(nl * nb, nb))
    part = jnp.where((col_block >= 1)[:, None, None], part.reshape(nm, nb, nb), 0.0)
    piece = jnp.sum(
        lax.all_to_all(part.reshape(nz, nm * nb // nz, nb), "prow", 0, 0), axis=0
    )
    ay_cols = share(piece, "prow", nz).reshape(nm * nb, nb)
    proj_part = mm_tn(y_cols, ay_cols)

    hb = nb // CORES
    qb = hb // YS
    pack = jnp.concatenate(
        [ay_cols.reshape(nm, CORES, hb, nb), proj_part.reshape(1, CORES, hb, nb)]
    ).transpose(1, 0, 2, 3)
    first = core == 0
    keep = jnp.where(first, pack[0], pack[1])
    got = lax.ppermute(jnp.where(first, pack[1], pack[0]), "pcol", SWAP)
    ay_half = jnp.where(core == prow % CORES, keep[:nm], got[:nm])
    proj_half = keep[nm:] + got[nm:]
    lines = jnp.concatenate([ay_half, proj_half]).reshape(nm + 1, YS, qb, nb).transpose(1, 0, 2, 3)
    lines = lax.all_to_all(lines, "pcol", 0, 0, axis_index_groups=YLINE)
    ay_piece = lax.dynamic_index_in_dim(lines[:, :nm], prow // CORES, 0, keepdims=False)
    proj_piece = jnp.sum(lines[:, nm:], axis=0)
    half = share(jnp.concatenate([ay_piece, proj_piece]), "pcol", CHIPS, PLANE)
    half = half.reshape(XS, YS, nm + 1, qb, nb)
    half = jnp.concatenate(
        [
            half[:, :, :nm].transpose(2, 0, 1, 3, 4).reshape(nm * XS, hb, nb),
            jnp.sum(half[:, :, nm], axis=0).reshape(1, hb, nb),
        ]
    )
    whole = both_halves(half, core).transpose(1, 0, 2, 3)
    ay_rows = whole[: nm * XS].reshape(nl * nb, nb)
    proj = whole[nm * XS].reshape(nb, nb)

    core_matrix = mm(mm_tn(mixer, proj), mixer)
    w_cols = mm(ay_cols, mixer) - mm(y_cols, core_matrix)
    v_cols = mm_nt(y_cols, mixer)
    live = jnp.where((row_block >= 1)[:, None, None], y_rows.reshape(nl, nb, nb), 0.0)
    left = jnp.concatenate([live.reshape(nl * nb, nb), ay_rows], axis=1)
    right = jnp.concatenate([w_cols, v_cols], axis=1)
    updated = (matrix - mm_nt(left, right)).reshape(nl, nb, nm, nb)
    band_col = jnp.where((row_block == 1)[:, None, None], -lower.T[None], 0.0)
    in_col = (col_block == 0)[None, None, :, None] & (row_block >= 1)[:, None, None, None]
    updated = jnp.where(in_col, band_col[:, :, None, :], updated)
    band_row = jnp.where((col_block == 1)[None, :, None], -lower[:, None, :], 0.0)
    in_row = (row_block == 0)[:, None, None, None] & (col_block >= 1)[None, None, :, None]
    return jnp.where(in_row, band_row[None], updated)


def solution(mesh):
    return jax.shard_map(
        body,
        mesh=mesh,
        in_specs=(P(None, "prow", None, "pcol"),),
        out_specs=P(None, "prow", None, "pcol"),
        check_vma=False,
    )
```

time: 759 us -> 343 us (0.45)
  waiting for transfers between devices: 513 us -> 33.4 us
  blocking collectives: 0 us -> 40.1 us
  starting transfers between devices: 1.06 us -> 29.7 us
  matrix products: 52.5 us -> 35.9 us
    psum x6 -> x1, waiting for transfers between devices: 513 us -> 0.01 us  [body(): p_cols_t = lax.psum(top_row, 'prow').reshape(nb, nm * nb)]
    all_to_all x0 -> x2, blocking collectives: none -> 40.1 us  [the longest x1 20.7 us: body(): mine = lax.all_to_all(outgoing, 'pcol', 0, 0, axis_index_groups=PLANE)[0]]
    all_to_all x0 -> x5, waiting for transfers between devices: none -> 27.6 us  [the longest x1 15.9 us: body(): lax.all_to_all(part.reshape(nz, nm * nb // nz, nb), 'prow', 0, 0)]
    all_to_all x0 -> x5, starting transfers between devices: none -> 21.5 us  [the longest x3 14.5 us: share(): return lax.all_to_all(copies, axis, 0, 0, axis_index_groups=groups)]
    dot_general x10 -> x13, matrix products: 42.1 us -> 26.4 us  [the longest x5 15.4 us: mm_nt(): lax.dot_general(a, b, (((1,), (1,)), ((), ())), precision=HP, preferred_e...]
    ppermute x0 -> x4, starting transfers between devices: none -> 8.24 us  [the longest x2 6.43 us: both_halves(): other = lax.ppermute(half, 'pcol', SWAP)]
    another operation x18 -> x23, other arithmetic: 109 us -> 117 us  [the longest x7 37 us: small_math(): factor = jnp.linalg.cholesky(normal)]
  transfers between devices with their start and end apart: 6 -> 10, of which waited for: 6 -> 4; matrix products, arithmetic and copies ran while one was open for 1% -> 50% of each run, Pallas kernels for 0% -> 0%
where the time goes in v1:
time: 343 us; the launch traced here: 337 us
  other arithmetic  139 us (41%)
  local copies, waits for them, and re-layouts  42.1 us (12%)
  blocking collectives  40.1 us (12%)
  matrix products  35.9 us (10%)
  waiting for transfers between devices  33.4 us (10%)
  starting transfers between devices  29.7 us (9%)
  between operations  16.8 us (5%)
    another operation x7, other arithmetic, small_math(): factor = jnp.linalg.cholesky(normal)  37 us
    another operation x7, other arithmetic, small_math(): lower = jnp.linalg.cholesky(gram)  34.6 us
    another operation x2, other arithmetic, small_math(): mixer = jax.scipy.linalg.cho_solve((factor, True), matrix.T)  22.2 us
    all_to_all x1, blocking collectives, body(): mine = lax.all_to_all(outgoing, 'pcol', 0, 0, axis_index_groups=PLANE)[0]  20.7 us
    another operation x2, other arithmetic, small_math(): inv = jax.scipy.linalg.solve_triangular(lower, ident, lower=True)  19.7 us
    all_to_all x1, blocking collectives, share(): return lax.all_to_all(copies, axis, 0, 0, axis_index_groups=groups)  19.3 us
    all_to_all x1, waiting for transfers between devices, body(): lax.all_to_all(part.reshape(nz, nm * nb // nz, nb), 'prow', 0, 0)  15.9 us
    dot_general x5, matrix products, mm_nt(): lax.dot_general(a, b, (((1,), (1,)), ((), ())), precision=HP, preferred_e...  15.4 us
  transfers between devices with their start and end apart: 10, of which 4 were waited for; matrix products, arithmetic and copies ran while one was open for 50% of the time, Pallas kernels for 0%

profile of v1, /device:TPU:1, one launch (start us, length us, event | category | flops | bytes accessed | tf_op | source)
XLA Modules:
  0.0 337.1 jit_solution(3155374550102982408)
XLA Ops:
  6.5 1.6 slice-done
  8.1 1.7 broadcast_select_fusion.1
  10.0 1.9 bitcast_select_fusion
  11.9 2.9 copy.90
  14.7 2.1 select_bitcast_fusion
  17.6 1.9 convolution_bitcast_fusion.2
  21.9 5.8 %collective-permute-done = f32[16,9,8,256]{3,2,0,1:T(8,128)S(1)} collective-permute-done((f32[16,9,8,256]{3,2,0,1:T(8,128)}, f32[16,9,8,256]{3,2,0,1:T(8,128)S(1)}, u32[]{:S(2)}, u32[]{:S(2)}) %collective-permute-start) | collective-permute-done | bytes 1179680 | tf_op jit(solution)/shard_map/ppermute | solution.py:73
  27.9 20.7 %all_to_all.35 = f32[16,9,8,256]{3,2,1,0:T(8,128)S(1)} all-to-all(f32[16,9,8,256]{3,2,1,0:T(8,128)S(1)} %copy.92), channel_id=1, replica_groups={{0,2,4,6,8,10,12,14,16,18,20,22,24,26,28,30},{1,3,5,7,9,11,13,15,17,19,..., dimensions={0} | all-to-all | bytes 2359296 | tf_op jit(solution)/shard_map/all_to_all | solution.py:75
  49.3 6.3 %all-to-all-start.1 = ((f32[8,2,8,256]{3,2,1,0:T(8,128)}), f32[8,2,8,256]{3,2,1,0:T(8,128)S(1)}, u32[]{:S(2)}, u32[]{:S(2)}) async-start(f32[8,2,8,256]{3,2,1,0:T(8,128)} %broadcast_in_dim.218), calls=%async_computation.1 | async-start | bytes 262144 | tf_op jit(solution)/shard_map/all_to_all | solution.py:28
  55.7 8.0 %all-to-all-done.1 = f32[8,2,8,256]{3,2,1,0:T(8,128)S(1)} async-done(((f32[8,2,8,256]{3,2,1,0:T(8,128)}), f32[8,2,8,256]{3,2,1,0:T(8,128)S(1)}, u32[]{:S(2)}, u32[]{:S(2)}) %all-to-all-start.1) | async-done | bytes 131104 | tf_op jit(solution)/shard_map/all_to_all | solution.py:28
  63.8 19.3 %all_to_all.36 = f32[16,10,8,256]{3,2,1,0:T(8,128)S(1)} all-to-all(f32[16,10,8,256]{3,2,1,0:T(8,128)S(1)} %broadcast_in_dim.220), channel_id=1, replica_groups={{0,2,4,6,8,10,12,14,16,18,20,22,24,26,28,30},{1,3,5,7,9,11,13,15,17,19,..., dimensions={0} | all-to-all | bytes 2621440 | tf_op jit(solution)/shard_map/all_to_all | solution.py:28
  83.3 4.9 %collective-permute-start.1 = (f32[16,10,8,256]{3,2,0,1:T(8,128)S(1)}, f32[16,10,8,256]{3,2,0,1:T(8,128)}, u32[]{:S(2)}, u32[]{:S(2)}) collective-permute-start(f32[16,10,8,256]{3,2,0,1:T(8,128)S(1)} %copy.94), channel_id=1, source_target_pairs={{0,1},{1,0},{2,3},{3,2},{4,5},{5,4},{6,7},{7,6},{8,9},{9,8},{10,11... | collective-permute-start | bytes 3932168 | tf_op jit(solution)/shard_map/ppermute | solution.py:32
  90.6 4.6 %copy.117 = f32[256,8,2,256]{3,1,2,0:T(8,128)} copy(f32[256,8,2,256]{3,2,1,0:T(2,128)} %bitcast.206) | data formatting | bytes 8388608
  97.1 1.6 select_bitcast_fusion.2
  98.7 1.6 fusion.7
  100.4 11.7 %cholesky.130 = f32[128,128]{1,0:T(8,128)S(1)} custom-call(f32[128,128]{1,0:T(8,128)S(1)} %cholesky.194), custom_call_target="Cholesky" | custom-call | tf_op jit(solution)/shard_map/jit(cholesky)/cholesky | solution.py:38
  112.2 9.8 %custom-call.18 = f32[1,128,128]{1,2,0:T(8,128)S(1)} custom-call(f32[1,128,128]{2,1,0:T(8,128)S(1)} %get-tuple-element.70), custom_call_target="InvertDiagBlocksLowerTriangular" | custom-call | tf_op jit(solution)/shard_map/jit(cholesky)/cholesky | solution.py:38
  122.5 11.7 %cholesky.147 = f32[128,128]{1,0:T(8,128)S(1)} custom-call(f32[128,128]{1,0:T(8,128)S(1)} %convolution_subtract_fusion.5), custom_call_target="Cholesky" | custom-call | tf_op jit(solution)/shard_map/jit(cholesky)/cholesky | solution.py:38
  137.7 4.5 %while.6 = (s32[]{:T(128)}, f32[256,256]{1,0:T(8,128)S(1)}, s32[2,2]{1,0:T(2,128)S(1)}, f32[2,128,128]{2,1,0:T(8,128)S(1)}, s32[]{:T(128)}) while((s32[]{:T(128)}, f32[256,256]{1,0:T(8,128)S(1)}, s32[2,2]{1,0:T(2,128)S(1)}, f32[2,128,128]{2,1,0:T(8,128)S(1)}, s32[]{:T(128)}) %tuple.54), condition=%wide.while_cond, body=%wide.while_body.sunk | while | flops 2 | bytes 131181 | solution.py:39
  138.8 1.3 bitcast_dynamic-update-slice_fusion.5
  140.8 1.3 bitcast_dynamic-update-slice_fusion.5
  142.7 19.7 %custom-call.19 = f32[2,128,128]{1,2,0:T(8,128)S(1)} custom-call(f32[2,128,128]{2,1,0:T(8,128)S(1)} %get-tuple-element.29), custom_call_target="InvertDiagBlocksLowerTriangular" | custom-call | tf_op jit(solution)/shard_map/jit(_solve_triangular)/triangular_solve/custom-call.1 | solution.py:39
  163.3 3.6 %add_select_fusion = f32[8,256,256]{2,1,0:T(8,128)S(1)} fusion(f32[8,256,256]{2,1,0:T(8,128)} %bitcast.210, f32[256,256]{1,0:T(8,128)S(1)} %fusion.22, pred[8]{0:T(512)(128)(4,1)S(1)} %get-tuple-element.78, pred[8]{0:T(512)(128)(4,1)S(1)} %get-tuple-element.77, f32[128,256]{1,0:T(8,128)S(1)} %fusion.37, f32[128,256]{1,0:T(8,128)S(1)} %fusion.27), kind=kOutput, calls=%fused_computation.17 | convolution fusion | flops 1612251136 | bytes 4718608 | tf_op jit(solution)/shard_map/dot_general | solution.py:23
  166.9 4.5 %convolution_bitcast_fusion = f32[512,256]{0,1:T(8,128)} fusion(f32[2048,256]{1,0:T(8,128)S(1)} %bitcast.204, f32[2048,512]{1,0:T(8,128)S(1)} %bitcast.201), kind=kOutput, calls=%fused_computation.21 | convolution fusion | flops 3221225472 | bytes 6815744 | tf_op jit(solution)/shard_map/dot_general | solution.py:19
  173.6 3.5 %all-to-all-start.3 = ((f32[8,64,256]{2,1,0:T(8,128)}), f32[8,64,256]{2,1,0:T(8,128)S(1)}, u32[]{:S(2)}, u32[]{:S(2)}) async-start(f32[8,64,256]{2,1,0:T(8,128)} %broadcast_select_fusion.3), calls=%async_computation.3 | async-start | bytes 1048576 | tf_op jit(solution)/shard_map/all_to_all | solution.py:100
  179.1 15.9 %all-to-all-done.3 = f32[8,64,256]{2,1,0:T(8,128)S(1)} async-done(((f32[8,64,256]{2,1,0:T(8,128)}), f32[8,64,256]{2,1,0:T(8,128)S(1)}, u32[]{:S(2)}, u32[]{:S(2)}) %all-to-all-start.3) | async-done | bytes 524320 | tf_op jit(solution)/shard_map/all_to_all | solution.py:100
  195.7 1.7 broadcast_in_dim.235
  197.4 3.7 %all-to-all-start.4 = ((f32[8,64,256]{2,1,0:T(8,128)}), f32[8,64,256]{2,1,0:T(8,128)S(1)}, u32[]{:S(2)}, u32[]{:S(2)}) async-start(f32[8,64,256]{2,1,0:T(8,128)} %broadcast_in_dim.235), calls=%async_computation.4 | async-start | bytes 1048576 | tf_op jit(solution)/shard_map/all_to_all | solution.py:28
  201.8 11.7 %cholesky.164 = f32[128,128]{1,0:T(8,128)S(1)} custom-call(f32[128,128]{1,0:T(8,128)S(1)} %cholesky.197), custom_call_target="Cholesky" | custom-call | tf_op jit(solution)/shard_map/jit(cholesky)/cholesky | solution.py:42
  214.1 9.8 %custom-call.20 = f32[1,128,128]{1,2,0:T(8,128)S(1)} custom-call(f32[1,128,128]{2,1,0:T(8,128)S(1)} %get-tuple-element.66), custom_call_target="InvertDiagBlocksLowerTriangular" | custom-call | tf_op jit(solution)/shard_map/jit(cholesky)/cholesky | solution.py:42
  226.2 12.3 %cholesky.181 = f32[128,128]{1,0:T(8,128)} custom-call(f32[128,128]{1,0:T(8,128)S(1)} %convolution_subtract_fusion.4), custom_call_target="Cholesky" | custom-call | tf_op jit(solution)/shard_map/jit(cholesky)/cholesky | solution.py:42
  238.5 1.7 convolution_add_fusion
  241.2 1.7 convolution_bitcast_fusion.1
  245.7 3.5 %all-to-all-start.5 = ((f32[4,3,32,256]{3,2,1,0:T(8,128)}), f32[4,3,32,256]{3,2,1,0:T(8,128)S(1)}, u32[]{:S(2)}, u32[]{:S(2)}) async-start(f32[4,3,32,256]{3,2,1,0:T(8,128)} %copy.106), calls=%async_computation.5 | async-start | bytes 786432 | tf_op jit(solution)/shard_map/all_to_all | solution.py:116
  251.7 1.7 select_select_fusion.1
  253.3 3.7 %all-to-all-done.5 = f32[4,3,32,256]{3,2,1,0:T(8,128)S(1)} async-done(((f32[4,3,32,256]{3,2,1,0:T(8,128)}), f32[4,3,32,256]{3,2,1,0:T(8,128)S(1)}, u32[]{:S(2)}, u32[]{:S(2)}) %all-to-all-start.5) | async-done | bytes 393248 | tf_op jit(solution)/shard_map/all_to_all | solution.py:116
  258.4 4.5 %all-to-all-start.6 = ((f32[16,3,32,256]{3,2,1,0:T(8,128)}), f32[16,3,32,256]{3,2,1,0:T(8,128)}, u32[]{:S(2)}, u32[]{:S(2)}) async-start(f32[16,3,32,256]{3,2,1,0:T(8,128)} %broadcast_in_dim.240), calls=%async_computation.6 | async-start | bytes 3145728 | tf_op jit(solution)/shard_map/all_to_all | solution.py:28
  263.0 6.9 %while.5 = (s32[]{:T(128)}, f32[256,256]{1,0:T(8,128)}, s32[2,2]{1,0:T(2,128)}, f32[2,128,128]{2,1,0:T(8,128)S(1)}, s32[]{:T(128)}) while((s32[]{:T(128)}, f32[256,256]{1,0:T(8,128)}, s32[2,2]{1,0:T(2,128)}, f32[2,128,128]{2,1,0:T(8,128)S(1)}, s32[]{:T(128)}) %tuple.62), condition=%wide.while_cond.1, body=%wide.while_body.1.sunk | while | flops 2 | bytes 131181 | solution.py:43
  264.2 2.2 bitcast_dynamic-update-slice_fusion.4
  267.7 2.2 bitcast_dynamic-update-slice_fusion.4
  270.6 20.5 %custom-call.15 = f32[2,128,128]{1,2,0:T(8,128)S(1)} custom-call(f32[2,128,128]{2,1,0:T(8,128)} %copy-done.15), custom_call_target="InvertDiagBlocksLowerTriangular" | custom-call | tf_op jit(solution)/shard_map/jit(_cho_solve)/triangular_solve | solution.py:43
  295.9 1.8 convolution_subtract_fusion.1
  297.7 1.5 copy.107
  299.5 1.5 collective-permute-start.3
  303.0 1.6 broadcast_select_fusion
  309.0 8.4 %fusion.4 = f32[2048,512]{1,0:T(8,128)} fusion(f32[2048,512]{1,0:T(8,128)S(1)} %bitcast.202, f32[2048,256]{1,0:T(8,128)S(1)} %bitcast.219, f32[2048,256]{1,0:T(8,128)S(1)} %bitcast.205, f32[512,256]{0,1:T(8,128)S(1)} %fusion.29, f32[512,256]{0,1:T(8,128)S(1)} %convolution_subtract_fusion), kind=kOutput, calls=%fused_computation.9 | convolution fusion | flops 6444810240 | bytes 13631488 | tf_op jit(solution)/shard_map/dot_general | solution.py:23
  317.4 6.0 %reshape.248 = f32[8,256,2,256]{3,2,1,0:T(2,128)} reshape(f32[2048,512]{1,0:T(8,128)} %fusion.4) | data formatting | bytes 8388608 | tf_op jit(solution)/shard_map/reshape | solution.py:137
  323.4 6.5 %select_select_fusion = f32[8,256,2,256]{3,2,1,0:T(2,128)} fusion(f32[8,256,2,256]{3,2,1,0:T(2,128)} %reshape.248, pred[8,2]{1,0:T(8,128)(4,1)S(1)} %broadcast_and_fusion, pred[8,2]{1,0:T(8,128)(4,1)S(1)} %broadcast_and_fusion.1, f32[8,256,256]{2,1,0:T(8,128)S(1)} %copy-done.4, f32[256,2,256]{2,1,0:T(2,128)S(1)} %copy-done.7), kind=kLoop, calls=%fused_computation.8 | loop fusion | flops 2097152 | bytes 11010080 | tf_op jit(solution)/shard_map/jit(_where)/select_n | solution.py:143
  (156 shorter events, 43.7 us)
Async XLA Ops:
  6.5 1.6 slice-start
  9.9 2.0 copy-start.2
  14.7 2.2 copy-start.3
  14.7 2.9 copy-start.5
  20.6 7.1 %collective-permute-start = (f32[16,9,8,256]{3,2,0,1:T(8,128)}, f32[16,9,8,256]{3,2,0,1:T(8,128)S(1)}, u32[]{:S(2)}, u32[]{:S(2)}) collective-permute-start(f32[16,9,8,256]{3,2,0,1:T(8,128)} %fusion.11), channel_id=1, source_target_pairs={{0,1},{32,33},{64,65},{96,97},{128,129},{160,161},{192,193},{224,2... | collective-permute-start | bytes 3538952 | tf_op jit(solution)/shard_map/ppermute | solution.py:73
  49.3 14.3 %all-to-all-start.1 = ((f32[8,2,8,256]{3,2,1,0:T(8,128)}), f32[8,2,8,256]{3,2,1,0:T(8,128)S(1)}, u32[]{:S(2)}, u32[]{:S(2)}) async-start(f32[8,2,8,256]{3,2,1,0:T(8,128)} %broadcast_in_dim.218), calls=%async_computation.1 | async-start | bytes 262144 | tf_op jit(solution)/shard_map/all_to_all | solution.py:28
  55.7 182.9 %all-reduce.3.cloned.1.call-start = ((), (), s32[]{:S(2)}) async-start(), calls=%async_computation.7 | async-start | bytes 1048576 | tf_op jit(solution)/shard_map/psum | solution.py:61
  83.3 13.8 %collective-permute-start.1 = (f32[16,10,8,256]{3,2,0,1:T(8,128)S(1)}, f32[16,10,8,256]{3,2,0,1:T(8,128)}, u32[]{:S(2)}, u32[]{:S(2)}) collective-permute-start(f32[16,10,8,256]{3,2,0,1:T(8,128)S(1)} %copy.94), channel_id=1, source_target_pairs={{0,1},{1,0},{2,3},{3,2},{4,5},{5,4},{6,7},{7,6},{8,9},{9,8},{10,11... | collective-permute-start | bytes 3932168 | tf_op jit(solution)/shard_map/ppermute | solution.py:32
  95.8 0.5 copy-start.17
  142.2 0.5 copy-start.21
  163.3 14.0 %copy-start.8 = (f32[128,256]{1,0:T(8,128)}, f32[128,256]{1,0:T(8,128)S(1)}, u32[]{:S(2)}) copy-start(f32[128,256]{1,0:T(8,128)S(1)} %fusion.37) | copy-start | bytes 393220
  163.3 3.6 %copy-start = (f32[256,8,2,256]{3,1,2,0:T(8,128)S(1)}, f32[256,8,2,256]{3,1,2,0:T(8,128)}, u32[]{:S(2)}) copy-start(f32[256,8,2,256]{3,1,2,0:T(8,128)} %copy.117) | copy-start | bytes 12582916
  171.4 5.7 %copy-start.19 = (pred[2]{0:T(512)(128)(4,1)S(1)}, pred[2]{0:T(512)(128)(4,1)}, u32[]{:S(2)}) copy-start(pred[2]{0:T(512)(128)(4,1)} %get-tuple-element.79) | copy-start | bytes 10
  171.4 5.8 %copy-start.18 = (pred[2]{0:T(512)(128)(4,1)S(1)}, pred[2]{0:T(512)(128)(4,1)}, u32[]{:S(2)}) copy-start(pred[2]{0:T(512)(128)(4,1)} %copy-done.17) | copy-start | bytes 10
  171.4 5.8 %copy-start.20 = (pred[8]{0:T(512)(128)(4,1)S(1)}, pred[8]{0:T(512)(128)(4,1)}, u32[]{:S(2)}) copy-start(pred[8]{0:T(512)(128)(4,1)} %broadcast_compare_fusion.5) | copy-start | bytes 28
  173.6 21.5 %all-to-all-start.3 = ((f32[8,64,256]{2,1,0:T(8,128)}), f32[8,64,256]{2,1,0:T(8,128)S(1)}, u32[]{:S(2)}, u32[]{:S(2)}) async-start(f32[8,64,256]{2,1,0:T(8,128)} %broadcast_select_fusion.3), calls=%async_computation.3 | async-start | bytes 1048576 | tf_op jit(solution)/shard_map/all_to_all | solution.py:100
  197.4 43.8 %all-to-all-start.4 = ((f32[8,64,256]{2,1,0:T(8,128)}), f32[8,64,256]{2,1,0:T(8,128)S(1)}, u32[]{:S(2)}, u32[]{:S(2)}) async-start(f32[8,64,256]{2,1,0:T(8,128)} %broadcast_in_dim.235), calls=%async_computation.4 | async-start | bytes 1048576 | tf_op jit(solution)/shard_map/all_to_all | solution.py:28
  201.1 0.7 copy-start.11
  225.0 13.5 %copy-start.10 = (f32[256,256]{1,0:T(8,128)}, f32[256,256]{1,0:T(8,128)S(1)}, u32[]{:S(2)}) copy-start(f32[256,256]{1,0:T(8,128)S(1)} %get-tuple-element.75) | copy-start | bytes 786436
  241.2 2.3 copy-start.16
  243.0 1.9 collective-permute-start.2
  245.7 11.3 %all-to-all-start.5 = ((f32[4,3,32,256]{3,2,1,0:T(8,128)}), f32[4,3,32,256]{3,2,1,0:T(8,128)S(1)}, u32[]{:S(2)}, u32[]{:S(2)}) async-start(f32[4,3,32,256]{3,2,1,0:T(8,128)} %copy.106), calls=%async_computation.5 | async-start | bytes 786432 | tf_op jit(solution)/shard_map/all_to_all | solution.py:116
  258.4 32.7 %copy-start.6 = (f32[256,256]{1,0:T(8,128)S(1)}, f32[256,256]{1,0:T(8,128)}, u32[]{:S(2)}) copy-start(f32[256,256]{1,0:T(8,128)} %get-tuple-element.61) | copy-start | bytes 786436
  258.4 39.3 %all-to-all-start.6 = ((f32[16,3,32,256]{3,2,1,0:T(8,128)}), f32[16,3,32,256]{3,2,1,0:T(8,128)}, u32[]{:S(2)}, u32[]{:S(2)}) async-start(f32[16,3,32,256]{3,2,1,0:T(8,128)} %broadcast_in_dim.240), calls=%async_computation.6 | async-start | bytes 3145728 | tf_op jit(solution)/shard_map/all_to_all | solution.py:28
  269.9 0.6 copy-start.15
  291.0 3.4 %copy-start.12 = (f32[2,128,128]{1,2,0:T(8,128)}, f32[2,128,128]{1,2,0:T(8,128)S(1)}, u32[]{:S(2)}) copy-start(f32[2,128,128]{1,2,0:T(8,128)S(1)} %custom-call.15) | copy-start | bytes 393220
  299.2 1.7 copy-start.13
  299.2 1.7 copy-start.14
  299.4 3.6 %copy-start.9 = (f32[256,256]{1,0:T(8,128)S(1)}, f32[256,256]{1,0:T(8,128)}, u32[]{:S(2)}) copy-start(f32[256,256]{1,0:T(8,128)} %copy.98) | copy-start | bytes 786436
  299.5 5.8 %collective-permute-start.3 = (f32[9,128,256]{2,1,0:T(8,128)S(1)}, f32[9,128,256]{2,1,0:T(8,128)S(1)}, u32[]{:S(2)}, u32[]{:S(2)}) collective-permute-start(f32[9,128,256]{2,1,0:T(8,128)S(1)} %pad_maximum_fusion.1), channel_id=1, source_target_pairs={{0,1},{1,0},{2,3},{3,2},{4,5},{5,4},{6,7},{7,6},{8,9},{9,8},{10,11... | collective-permute-start | bytes 3538952 | tf_op jit(solution)/shard_map/ppermute | solution.py:32
  306.9 2.2 copy-start.1
  317.4 6.0 %copy-start.4 = (f32[8,256,256]{2,1,0:T(8,128)S(1)}, f32[8,256,256]{2,1,0:T(8,128)}, u32[]{:S(2)}) copy-start(f32[8,256,256]{2,1,0:T(8,128)} %broadcast_select_fusion) | copy-start | bytes 6291460
  317.4 6.0 %copy-start.7 = (f32[256,2,256]{2,1,0:T(2,128)S(1)}, f32[256,2,256]{2,1,0:T(2,128)}, u32[]{:S(2)}) copy-start(f32[256,2,256]{2,1,0:T(2,128)} %broadcast_select_fusion.2) | copy-start | bytes 1572868
Sparse Core Ops, SparseCore 0:
  90.7 61.7 all-reduce.2

commit v2 on v0

v2 whole, which is shorter than its diff:
```python
import functools
import jax
import jax.numpy as jnp
from jax import lax
from jax.experimental import pallas as pl
from jax.experimental.pallas import tpu as pltpu
from jax.sharding import PartitionSpec as P

HP = lax.Precision.HIGHEST
XS, YS, CORES = 4, 4, 2
CHIPS = XS * YS
LANES = 128
BASE = 64
GROUP = 8
PLANE = [[q * CORES + k for q in range(CHIPS)] for k in range(CORES)]
YLINE = [[(x * YS + y) * CORES + k for y in range(YS)] for x in range(XS) for k in range(CORES)]
SWAP = [(i, i ^ 1) for i in range(CHIPS * CORES)]
VMEM = pl.BlockSpec(memory_space=pltpu.VMEM)
SMEM = pl.BlockSpec(memory_space=pltpu.SMEM)


def mm(a, b):
    return jnp.dot(a, b, precision=HP, preferred_element_type=jnp.float32)


def mm_tn(a, b):
    return lax.dot_general(a, b, (((0,), (0,)), ((), ())), precision=HP, preferred_element_type=jnp.float32)


def mm_nt(a, b):
    return lax.dot_general(a, b, (((1,), (1,)), ((), ())), precision=HP, preferred_element_type=jnp.float32)


def eliminate(block, jordan):
    n = block.shape[0]
    eye = (lax.broadcasted_iota(jnp.int32, (n, n), 0) == lax.broadcasted_iota(jnp.int32, (n, n), 1))
    wide = jnp.concatenate([block, eye.astype(jnp.float32)], axis=1)
    shape = (GROUP, 2 * n)
    groups = n // GROUP
    at = lax.broadcasted_iota(jnp.int32, shape, 0)
    w = [wide[g * GROUP : (g + 1) * GROUP] for g in range(groups)]
    for p in range(groups):
        live = [g for g in range(groups) if jordan or g >= p]
        cols = {
            g: [
                jnp.broadcast_to(w[g][:, p * GROUP + b : p * GROUP + b + 1], shape)
                for b in range(GROUP)
            ]
            for g in live
        }
        for a in range(GROUP):
            inv = 1.0 / cols[p][a][a : a + 1]
            row = w[p][a : a + 1]
            heads = [cols[p][b][a : a + 1] for b in range(GROUP)]
            for g in live:
                m = cols[g][a] * inv
                if g == p:
                    m = jnp.where(at != a if jordan else at > a, m, 0.0)
                for b in range(a + 1, GROUP):
                    cols[g][b] = cols[g][b] - m * heads[b]
                w[g] = w[g] - m * row
    return jnp.concatenate(w, axis=0)


def diagonal(wide):
    n = wide.shape[0]
    shape = wide.shape
    eye = lax.broadcasted_iota(jnp.int32, shape, 0) == lax.broadcasted_iota(jnp.int32, shape, 1)
    return jnp.sum(jnp.where(eye, wide, 0.0), axis=1, keepdims=True)


def factor(a):
    n = a.shape[0]
    if n <= BASE:
        wide = eliminate(a, False)
        wide = wide * (1.0 / jnp.sqrt(diagonal(wide)))
        left = wide[:, :n]
        upper = lax.broadcasted_iota(jnp.int32, (n, n), 0) <= lax.broadcasted_iota(jnp.int32, (n, n), 1)
        return jnp.where(upper, left, 0.0), wide[:, n:]
    h = n // 2
    u11, i11 = factor(a[:h, :h])
    u12 = mm(i11, a[:h, h:])
    u22, i22 = factor(a[h:, h:] - mm_tn(u12, u12))
    i21 = -mm(i22, mm_tn(u12, i11))
    zero = jnp.zeros((h, h), jnp.float32)
    upper = jnp.concatenate([jnp.concatenate([u11, u12], 1), jnp.concatenate([zero, u22], 1)], 0)
    inv = jnp.concatenate([jnp.concatenate([i11, zero], 1), jnp.concatenate([i21, i22], 1)], 0)
    return upper, inv


def inverse(a):
    n = a.shape[0]
    if n <= BASE:
        wide = eliminate(a, True)
        return (wide * (1.0 / diagonal(wide)))[:, n:]
    h = n // 2
    i11 = inverse(a[:h, :h])
    x = mm(i11, a[:h, h:])
    y = mm(a[h:, :h], i11)
    s = inverse(a[h:, h:] - mm(a[h:, :h], x))
    xs = mm(x, s)
    top = jnp.concatenate([i11 + mm(xs, y), -xs], 1)
    return jnp.concatenate([top, jnp.concatenate([-mm(s, y), s], 1)], 0)


def split(a):
    high = a.astype(jnp.bfloat16)
    return high, (a - high.astype(jnp.float32)).astype(jnp.bfloat16)


def dot3(a, b, dims):
    one = functools.partial(
        lax.dot_general, dimension_numbers=(dims, ((), ())), preferred_element_type=jnp.float32
    )
    return one(a[0], b[0]) + (one(a[0], b[1]) + one(a[1], b[0]))


def identity(n):
    rows = lax.broadcasted_iota(jnp.int32, (n, n), 0)
    return (rows == lax.broadcasted_iota(jnp.int32, (n, n), 1)).astype(jnp.float32)


def tile(ref, m, t, nm, nt):
    return ref[pl.ds(t * nm + m, ref.shape[0] // (nm * nt), stride=nm * nt), :]


def in_order(at_ref, own, other):
    first = at_ref[2] == 0
    return jnp.concatenate([jnp.where(first, own, other), jnp.where(first, other, own)], axis=0)


def rows_of(ref):
    return ref[...].reshape(-1, ref.shape[-1])


def pack_kernel(nm, nt, at_ref, x_ref, packet_ref, gram_ref):
    step = pl.program_id(0)
    last = pl.num_programs(0) - 1

    @pl.when(step < last)
    def _():
        panel = jnp.concatenate([tile(x_ref, 0, t, nm, nt) for t in range(nt)], axis=1)
        panel = jnp.where((step == 0) & (at_ref[0] == 0), 0.0, panel)
        packet_ref[...] = panel.reshape(packet_ref.shape)
        more = mm_tn(panel, panel)

        @pl.when(step == 0)
        def _():
            gram_ref[...] = more

        @pl.when(step > 0)
        def _():
            gram_ref[...] += more

    @pl.when(step == last)
    def _():
        packet_ref[...] = gram_ref[...].reshape(packet_ref.shape)


def factor_kernel(at_ref, own_ref, other_ref, upper_ref, inv_ref, inv_t_ref):
    upper, inv = factor(in_order(at_ref, rows_of(own_ref), rows_of(other_ref)))
    upper_ref[...] = upper
    inv_ref[...] = inv
    inv_t_ref[...] = inv.T


def mixer_kernel(at_ref, own_ref, other_ref, inv_ref, after_ref, mixer_ref):
    top = in_order(at_ref, rows_of(own_ref), rows_of(other_ref))
    mixer_ref[...] = inverse(identity(top.shape[0]) + mm_nt(inv_ref[...], top))


def apply_kernel(nm, nt, at_ref, x_ref, own_ref, other_ref, inv_t_ref, y_ref, part_ref, sum_ref):
    step = pl.program_id(0)
    nb = inv_t_ref.shape[0]
    y = mm(in_order(at_ref, rows_of(own_ref), rows_of(other_ref)), inv_t_ref[...])
    y += jnp.where((step == 0) & (at_ref[0] == 1), identity(nb), 0.0)
    y_ref[0] = y
    block = jnp.concatenate(
        [tile(x_ref, m, t, nm, nt) for m in range(nm) for t in range(nt)], axis=1
    )
    more = dot3(split(y.T), split(block), ((1,), (0,)))

    @pl.when(step == 0)
    def _():
        sum_ref[...] = more

    @pl.when(step > 0)
    def _():
        sum_ref[...] += more

    @pl.when(step == pl.num_programs(0) - 1)
    def _():
        total = sum_ref[...].T
        part_ref[:nb] = jnp.where(at_ref[1] == 0, 0.0, total[:nb])
        part_ref[nb:] = total[nb:]


def cols_kernel(nm, nt, at_ref, top_ref, inv_ref, y_ref):
    nb = inv_ref.shape[0]
    parts = [
        mm(inv_ref[...], jnp.concatenate([tile(top_ref, m, t, nm, nt) for t in range(nt)], axis=1))
        for m in range(nm)
    ]
    parts[0] += jnp.where(at_ref[1] == 1, identity(nb), 0.0)
    y_ref[...] = jnp.concatenate(parts, axis=1)


def proj_kernel(at_ref, y_ref, ay_ref, keep_ref, send_ref):
    nb = y_ref.shape[0]
    hb = nb // CORES
    ay = ay_ref[...]
    proj = mm(y_ref[...], ay)
    parts = [ay[i * nb : (i + 1) * nb] for i in range(ay.shape[0] // nb)] + [proj]
    first = at_ref[2] == 0
    for i, p in enumerate(parts):
        keep_ref[i] = jnp.where(first, p[:hb], p[hb:])
        send_ref[i] = jnp.where(first, p[hb:], p[:hb])


def sides_kernel(mixer_ref, y_ref, ay_ref, z_ref, v_ref):
    mixer = mixer_ref[...]
    z_ref[...] = lax.dot_general(
        mixer, ay_ref[...], (((0,), (1,)), ((), ())), precision=HP, preferred_element_type=jnp.float32
    )
    v_ref[...] = mm(mixer, y_ref[...])


def update_kernel(
    nm, nt, at_ref, x_ref, left_ref, own_ref, other_ref, own_proj_ref, other_proj_ref,
    mixer_ref, y_ref, z_ref, v_ref, upper_ref, out_ref, high_ref, low_ref,
):
    step = pl.program_id(0)
    nb = mixer_ref.shape[0]

    @pl.when(step == 0)
    def _():
        halves = [
            jnp.sum(ref[...].reshape(XS, nb // CORES, nb), axis=0)
            for ref in (own_proj_ref, other_proj_ref)
        ]
        mixer = mixer_ref[...]
        core = mm(mm_tn(mixer, in_order(at_ref, *halves)), mixer)
        w = split(z_ref[...] - mm_tn(core, y_ref[...]))
        v = split(v_ref[...])
        for i, ref in enumerate((high_ref, low_ref)):
            ref[:nb] = w[i]
            ref[nb:] = v[i]

    ay = in_order(at_ref, rows_of(own_ref), rows_of(other_ref))
    left = split(jnp.concatenate([left_ref[0], ay], axis=1))
    change = dot3(left, (high_ref[...], low_ref[...]), ((1,), (0,)))
    rows = nb
    for m in range(nm):
        for t in range(nt):
            at = m * nb + t * LANES
            out_ref[pl.ds(t * nm + m, rows, stride=nm * nt), :] = (
                tile(x_ref, m, t, nm, nt) - change[:, at : at + LANES]
            )

    @pl.when(at_ref[1] == 0)
    def _():
        keep = (step == 0) & (at_ref[0] == 0)
        band = jnp.where((step == 0) & (at_ref[0] == 1), -upper_ref[...], 0.0)
        for t in range(nt):
            old = tile(x_ref, 0, t, nm, nt)
            out_ref[pl.ds(t * nm, rows, stride=nm * nt), :] = jnp.where(
                keep, old, band[:, t * LANES : (t + 1) * LANES]
            )

    @pl.when((step == 0) & (at_ref[0] == 0))
    def _():
        band = jnp.where(at_ref[1] == 1, -upper_ref[...].T, 0.0)
        for m in range(nm):
            for t in range(nt):
                new = band[:, t * LANES : (t + 1) * LANES] if m == 0 else jnp.zeros((rows, LANES))
                if m == 0:
                    new = jnp.where(at_ref[1] == 0, tile(x_ref, m, t, nm, nt), new)
                out_ref[pl.ds(t * nm + m, rows, stride=nm * nt), :] = new


def call(kernel, outs, ins, grid=(), flops=0, moved=1 << 20, scratch=()):
    return pl.pallas_call(
        kernel,
        grid=grid,
        out_shape=[jax.ShapeDtypeStruct(s, jnp.float32) for s, _ in outs],
        in_specs=ins,
        out_specs=[spec for _, spec in outs],
        scratch_shapes=list(scratch),
        compiler_params=pltpu.CompilerParams(vmem_limit_bytes=40 << 20),
        cost_estimate=pl.CostEstimate(flops=flops, bytes_accessed=moved, transcendentals=0),
    )


def share(piece, axis, count, groups=None):
    copies = jnp.broadcast_to(piece[None], (count,) + piece.shape)
    return lax.all_to_all(copies, axis, 0, 0, axis_index_groups=groups)


def doubled(block, reach, nz):
    pairs = [(i, i + reach) for i in range(0, nz, 2 * reach)]
    return block + lax.ppermute(block, "prow", pairs)


def body(hamiltonian):
    nl, nb, nm, _ = hamiltonian.shape
    nt = nb // LANES
    nz = lax.axis_size("prow")
    prow = lax.axis_index("prow")
    pcol = lax.axis_index("pcol")
    core = pcol % CORES
    at = jnp.stack([prow, pcol, core]).astype(jnp.int32)
    sub = nb // (CHIPS * CORES)
    hb = nb // CORES
    qb = hb // YS
    nc = nm * nb
    square, wide, tall = (nb, nb), (nb, nc), (nc, nb)

    x = hamiltonian.reshape(nl, nb, nm, nt, LANES).transpose(0, 1, 3, 2, 4)
    x = x.reshape(nl * nb * nt * nm, LANES)
    x_rows = nb * nt * nm
    x_spec = pl.BlockSpec((x_rows, LANES), lambda l: (l, 0))

    first_rows = x[:x_rows].reshape(nb * nt, nm, LANES)
    live = (jnp.arange(nm, dtype=jnp.int32) * (CHIPS * CORES) + pcol >= 1) & (prow == 0)
    p_cols = jnp.where(live[None, :, None], first_rows, 0.0).reshape(x_rows, LANES)

    packet = call(
        functools.partial(pack_kernel, nm, nt),
        [((CORES, CHIPS, nl + 1, sub, nb),
          pl.BlockSpec((CORES, CHIPS, 1, sub, nb), lambda l: (0, 0, l, 0, 0)))],
        [SMEM, pl.BlockSpec((x_rows, LANES), lambda l: (jnp.minimum(l, nl - 1), 0))],
        grid=(nl + 1,),
        flops=12 * nl * nb**3,
        moved=6 << 20,
        scratch=[pltpu.VMEM(square, jnp.float32)],
    )(at, x)[0]
    given = lax.ppermute(packet[1], "pcol", [(0, 1)])
    outgoing = jnp.where(pcol == 0, packet[0], given)
    mine = lax.all_to_all(outgoing, "pcol", 0, 0, axis_index_groups=PLANE)[0]
    p_cols, mine = lax.optimization_barrier((doubled(p_cols, 4, nz), mine))
    stacked = share(jnp.stack([mine[nl], mine[0]]), "prow", nz)
    p_cols, stacked = lax.optimization_barrier((doubled(p_cols, 2, nz), stacked))
    gram_piece = jnp.sum(stacked[:, 0], axis=0)
    own = share(
        jnp.concatenate([mine[:nl], gram_piece[None], stacked[1, 1][None]]), "pcol", CHIPS, PLANE
    )
    p_cols, own = lax.optimization_barrier((doubled(p_cols, 1, nz), own))
    other = lax.ppermute(own, "pcol", SWAP)

    def chunk(index):
        return pl.BlockSpec((CHIPS, 1, sub, nb), index)

    gram_spec = chunk(lambda l: (0, nl, 0, 0))
    upper, inv, inv_t = call(
        factor_kernel, [(square, VMEM)] * 3, [SMEM, gram_spec, gram_spec], grid=(1,), flops=10**10
    )(at, own, other)

    whole = lambda shape: pl.BlockSpec(shape, lambda l: (0,) * len(shape))
    row_spec = chunk(lambda l: (0, l, 0, 0))
    y_rows, part = call(
        functools.partial(apply_kernel, nm, nt),
        [((nl, nb, nb), pl.BlockSpec((1, nb, nb), lambda l: (l, 0, 0))), (tall, whole(tall))],
        [SMEM, x_spec, row_spec, row_spec, whole(square)],
        grid=(nl,),
        flops=12 * nl * nb**2 * (nb + nc),
        moved=9 << 20,
        scratch=[pltpu.VMEM(wide, jnp.float32)],
    )(at, x, own, other, inv_t)
    top_spec = chunk(lambda l: (0, nl + 1, 0, 0))
    mixer = call(
        mixer_kernel,
        [(square, VMEM)],
        [SMEM, top_spec, top_spec, VMEM, pl.BlockSpec(memory_space=pl.ANY)],
        grid=(1,),
        flops=10**10,
    )(at, own, other, inv, part)[0]
    y_cols = call(
        functools.partial(cols_kernel, nm, nt), [(wide, VMEM)], [SMEM, VMEM, VMEM], flops=10**9
    )(at, p_cols, inv)[0]
    parts = lax.all_to_all(part.reshape(nz, nc // nz, nb), "prow", 0, 0)
    parts, mixer = lax.optimization_barrier((parts, mixer))
    ay_cols = share(jnp.sum(parts, axis=0), "prow", nz).reshape(nc, nb)
    ay_cols, y_cols = lax.optimization_barrier((ay_cols, y_cols))

    half_shape = (nm + 1, hb, nb)
    keep, send = call(proj_kernel, [(half_shape, VMEM)] * 2, [SMEM, VMEM, VMEM], flops=10**9)(
        at, y_cols, ay_cols
    )
    got = lax.ppermute(send, "pcol", SWAP)
    lines = jnp.concatenate([jnp.where(core == prow % CORES, keep[:nm], got[:nm]), keep[nm:] + got[nm:]])
    lines = lines.reshape(nm + 1, YS, qb, nb).transpose(1, 0, 2, 3)
    lines = lax.all_to_all(lines, "pcol", 0, 0, axis_index_groups=YLINE)
    z_cols, v_cols = call(sides_kernel, [(wide, VMEM)] * 2, [VMEM] * 3, flops=3 * 10**9)(
        mixer, y_cols, ay_cols
    )
    lines, z_cols, v_cols = lax.optimization_barrier((lines, z_cols, v_cols))
    ay_piece = lax.dynamic_index_in_dim(lines[:, :nm], prow // CORES, 0, keepdims=False)
    half = share(
        jnp.concatenate([ay_piece, jnp.sum(lines[:, nm:], axis=0)]), "pcol", CHIPS, PLANE
    ).reshape(XS, YS, nm + 1, qb, nb)
    other_half = lax.ppermute(half, "pcol", SWAP)
    ay_spec = pl.BlockSpec((1, YS, 1, qb, nb), lambda l: (l % XS, 0, l // XS, 0, 0))
    proj_spec = pl.BlockSpec((XS, YS, 1, qb, nb), lambda l: (0, 0, nm, 0, 0))
    out = call(
        functools.partial(update_kernel, nm, nt),
        [(x.shape, x_spec)],
        [SMEM, x_spec, pl.BlockSpec((1, nb, nb), lambda l: (l, 0, 0)), ay_spec, ay_spec,
         proj_spec, proj_spec, whole(square), whole(wide), whole(wide), whole(wide), whole(square)],
        grid=(nl,),
        flops=12 * nl * nb**2 * nc,
        moved=12 << 20,
        scratch=[pltpu.VMEM((2 * nb, nc), jnp.bfloat16)] * 2,
    )(at, x, y_rows, half, other_half, half, other_half, mixer, y_cols, z_cols, v_cols, upper)[0]
    out = out.reshape(nl, nb, nt, nm, LANES).transpose(0, 1, 3, 2, 4)
    return out.reshape(hamiltonian.shape)


def solution(mesh):
    return jax.shard_map(
        body,
        mesh=mesh,
        in_specs=(P(None, "prow", None, "pcol"),),
        out_specs=P(None, "prow", None, "pcol"),
        check_vma=False,
    )
```

time: 759 us -> 220 us (0.29)
  waiting for transfers between devices: 513 us -> 70.4 us
  other arithmetic: 132 us -> 7.95 us
  matrix products: 52.5 us -> 0 us
  starting transfers between devices: 1.06 us -> 51.8 us
  Pallas kernels: 0 us -> 49.6 us
  blocking collectives: 0 us -> 23.1 us
  local copies, waits for them, and re-layouts: 35.5 us -> 15.5 us
  between operations: 17.2 us -> 0.38 us
    psum x6 -> x0, waiting for transfers between devices: 513 us -> none  [the longest x3 261 us: spread(): return lax.psum(jnp.where(mine, shard, jnp.zeros_like(shard)), axis)]
    another operation x18 -> x2, other arithmetic: 109 us -> 0.08 us  [the longest x1 0.08 us: body(): at = jnp.stack([prow, pcol, core]).astype(jnp.int32)]
    pallas_call x0 -> x8, Pallas kernels: none -> 49.6 us  [the longest x1 12.8 us: body(): call(mixer_kernel, [(square, VMEM)], [SMEM, top_spec, top_spec, VMEM, pl....]
    dot_general x10 -> x0, matrix products: 42.1 us -> none  [the longest x1 10.4 us: body(): jnp.dot(matrix, yc_flat, precision=hp, preferred_element_type=jnp.float32)]
    all_to_all x0 -> x6, waiting for transfers between devices: none -> 38.7 us  [the longest x3 33.7 us: share(): return lax.all_to_all(copies, axis, 0, 0, axis_index_groups=groups)]
    all_to_all x0 -> x6, starting transfers between devices: none -> 32 us  [the longest x3 19.9 us: share(): return lax.all_to_all(copies, axis, 0, 0, axis_index_groups=groups)]
    ppermute x0 -> x7, waiting for transfers between devices: none -> 31.8 us  [the longest x3 18.9 us: doubled(): return block + lax.ppermute(block, 'prow', pairs)]
    all_to_all x0 -> x1, blocking collectives: none -> 23.1 us  [share(): return lax.all_to_all(copies, axis, 0, 0, axis_index_groups=groups)]
  transfers between devices with their start and end apart: 6 -> 13, of which waited for: 6 -> 11; matrix products, arithmetic and copies ran while one was open for 1% -> 2% of each run, Pallas kernels for 0% -> 7%
where the time goes in v2:
time: 220 us; the launch traced here: 219 us
  waiting for transfers between devices  70.4 us (32%)
  starting transfers between devices  51.8 us (24%)
  Pallas kernels  49.6 us (23%)
  blocking collectives  23.1 us (10%)
  local copies, waits for them, and re-layouts  15.5 us (7%)
  other arithmetic  7.95 us (4%)
    all_to_all x3, waiting for transfers between devices, share(): return lax.all_to_all(copies, axis, 0, 0, axis_index_groups=groups)  33.7 us
    all_to_all x1, blocking collectives, share(): return lax.all_to_all(copies, axis, 0, 0, axis_index_groups=groups)  23.1 us
    all_to_all x3, starting transfers between devices, share(): return lax.all_to_all(copies, axis, 0, 0, axis_index_groups=groups)  19.9 us
    ppermute x3, waiting for transfers between devices, doubled(): return block + lax.ppermute(block, 'prow', pairs)  18.9 us
    pallas_call x1, Pallas kernels, body(): call(mixer_kernel, [(square, VMEM)], [SMEM, top_spec, top_spec, VMEM, pl....  12.8 us
    pallas_call x1, Pallas kernels, body(): call(factor_kernel, [(square, VMEM)] * 3, [SMEM, gram_spec, gram_spec], g...  10.5 us
    ppermute x3, starting transfers between devices, doubled(): return block + lax.ppermute(block, 'prow', pairs)  10.2 us
    unnamed x34, local copies, waits for them, and re-layouts  9.3 us
  transfers between devices with their start and end apart: 13, of which 11 were waited for; matrix products, arithmetic and copies ran while one was open for 2% of the time, Pallas kernels for 7%

profile of v2, /device:TPU:1, one launch (start us, length us, event | category | flops | bytes accessed | tf_op | source)
XLA Modules:
  0.0 218.8 jit_solution(11429649511494642640)
XLA Ops:
  0.1 2.2 copy-done
  2.3 4.6 %shard_map.17 = f32[2,16,9,8,256]{4,3,2,1,0:T(8,128)S(1)} custom-call(s32[3]{0:T(128)S(1)} %pad_add_fusion.at_ref, f32[8192,128]{1,0:T(8,128)S(1)} %bitcast.36), custom_call_target="tpu_custom_call" | custom-call | flops 1610612736 | bytes 6291456 | tf_op jit(solution)/shard_map/pallas_call | solution.py:327
  6.9 1.3 collective-permute-start.1
  8.2 5.7 %collective-permute-done.1 = f32[16,9,8,256]{3,2,1,0:T(8,128)} collective-permute-done((f32[16,9,8,256]{3,2,1,0:T(8,128)S(1)}, f32[16,9,8,256]{3,2,1,0:T(8,128)}, u32[]{:S(2)}, u32[]{:S(2)}) %collective-permute-start.1) | collective-permute-done | bytes 1179680 | tf_op jit(solution)/shard_map/ppermute | solution.py:337
  13.9 2.5 %fusion = f32[16,9,8,256]{3,2,1,0:T(8,128)} fusion(f32[16,9,8,256]{3,2,1,0:T(8,128)} %collective-permute-done.1, f32[2,16,9,8,256]{4,3,2,1,0:T(8,128)S(1)} %shard_map.17, pred[]{:T(512)S(6)} %eq.13), kind=kLoop, calls=%fused_computation.2 | loop fusion | flops 294912 | bytes 3538945 | tf_op jit(solution)/shard_map/jit(_where)/select_n | solution.py:338
  16.4 3.7 %all-to-all-start = ((f32[16,9,8,256]{3,2,1,0:T(8,128)}), f32[16,9,8,256]{3,2,1,0:T(8,128)S(1)}, u32[]{:S(2)}, u32[]{:S(2)}) async-start(f32[16,9,8,256]{3,2,1,0:T(8,128)} %fusion), calls=%async_computation | async-start | bytes 2359296 | tf_op jit(solution)/shard_map/all_to_all | solution.py:339
  20.3 1.2 slice.61
  21.8 7.6 %collective-permute-start = (f32[1024,128]{1,0:T(8,128)S(1)}, f32[1024,128]{1,0:T(8,128)S(1)}, u32[]{:S(2)}, u32[]{:S(2)}) collective-permute-start(f32[1024,128]{1,0:T(8,128)S(1)} %broadcast_select_fusion), channel_id=1, source_target_pairs={{0,128},{1,129},{2,130},{3,131},{4,132},{5,133},{6,134},{7,135},{8... | collective-permute-start | bytes 1572872 | tf_op jit(solution)/shard_map/ppermute | solution.py:301
  29.3 10.4 %collective-permute-done = f32[1024,128]{1,0:T(8,128)S(1)} collective-permute-done((f32[1024,128]{1,0:T(8,128)S(1)}, f32[1024,128]{1,0:T(8,128)S(1)}, u32[]{:S(2)}, u32[]{:S(2)}) %collective-permute-start) | collective-permute-done | bytes 524320 | tf_op jit(solution)/shard_map/ppermute | solution.py:301
  40.0 1.3 collective-permute-start.2
  42.0 7.4 %all-to-all-start.1 = ((f32[8,2,8,256]{3,2,1,0:T(8,128)}), f32[8,2,8,256]{3,2,1,0:T(8,128)S(1)}, u32[]{:S(2)}, u32[]{:S(2)}) async-start(f32[8,2,8,256]{3,2,1,0:T(8,128)} %broadcast_in_dim.48), calls=%async_computation.1 | async-start | bytes 262144 | tf_op jit(solution)/shard_map/all_to_all | solution.py:296
  49.8 10.3 %all-to-all-done.1 = f32[8,2,8,256]{3,2,1,0:T(8,128)S(1)} async-done(((f32[8,2,8,256]{3,2,1,0:T(8,128)}), f32[8,2,8,256]{3,2,1,0:T(8,128)S(1)}, u32[]{:S(2)}, u32[]{:S(2)}) %all-to-all-start.1) | async-done | bytes 131104 | tf_op jit(solution)/shard_map/all_to_all | solution.py:296
  60.2 1.2 broadcast_in_dim.50
  61.4 6.1 %all-to-all-start.2 = ((f32[16,10,8,256]{3,2,1,0:T(8,128)}), f32[16,10,8,256]{3,2,1,0:T(8,128)S(1)}, u32[]{:S(2)}, u32[]{:S(2)}) async-start(f32[16,10,8,256]{3,2,1,0:T(8,128)} %broadcast_in_dim.50), calls=%async_computation.2 | async-start | bytes 2621440 | tf_op jit(solution)/shard_map/all_to_all | solution.py:296
  67.5 1.3 collective-permute-start.3
  68.8 8.2 %collective-permute-done.3 = f32[1024,128]{1,0:T(8,128)S(1)} collective-permute-done((f32[1024,128]{1,0:T(8,128)S(1)}, f32[1024,128]{1,0:T(8,128)S(1)}, u32[]{:S(2)}, u32[]{:S(2)}) %collective-permute-start.3) | collective-permute-done | bytes 524320 | tf_op jit(solution)/shard_map/ppermute | solution.py:301
  77.0 0.9 add.39.top_ref
  77.8 6.5 %all-to-all-done.2.own_ref = f32[16,10,8,256]{3,2,1,0:T(8,128)S(1)} async-done(((f32[16,10,8,256]{3,2,1,0:T(8,128)}), f32[16,10,8,256]{3,2,1,0:T(8,128)S(1)}, u32[]{:S(2)}, u32[]{:S(2)}) %all-to-all-start.2) | async-done | bytes 1310752 | tf_op jit(solution)/shard_map/all_to_all | solution.py:296
  84.4 4.3 %collective-permute-start.4 = (f32[16,10,8,256]{3,2,1,0:T(8,128)S(1)}, f32[16,10,8,256]{3,2,1,0:T(8,128)S(1)}, u32[]{:S(2)}, u32[]{:S(2)}) collective-permute-start(f32[16,10,8,256]{3,2,1,0:T(8,128)S(1)} %all-to-all-done.2.own_ref), channel_id=1, source_target_pairs={{0,1},{1,0},{2,3},{3,2},{4,5},{5,4},{6,7},{7,6},{8,9},{9,8},{10,11... | collective-permute-start | bytes 3932168 | tf_op jit(solution)/shard_map/ppermute | solution.py:348
  88.6 2.7 %collective-permute-done.4.other_ref = f32[16,10,8,256]{3,2,1,0:T(8,128)S(1)} collective-permute-done((f32[16,10,8,256]{3,2,1,0:T(8,128)S(1)}, f32[16,10,8,256]{3,2,1,0:T(8,128)S(1)}, u32[]{:S(2)}, u32[]{:S(2)}) %collective-permute-start.4) | collective-permute-done | bytes 1310752 | tf_op jit(solution)/shard_map/ppermute | solution.py:348
  91.3 10.5 %shard_map.18 = (f32[256,256]{1,0:T(8,128)S(1)}, f32[256,256]{1,0:T(8,128)S(1)}, f32[256,256]{1,0:T(8,128)S(1)}) custom-call(s32[3]{0:T(128)S(1)} %pad_add_fusion.at_ref, f32[16,10,8,256]{3,2,1,0:T(8,128)S(1)} %all-to-all-done.2.own_ref, f32[16,10,8,256]{3,2,1,0:T(8,128)S(1)} %collective-permute-done.4.other_ref), custom_call_target="tpu_custom_call" | custom-call | flops 10000000000 | bytes 1048576 | tf_op jit(solution)/shard_map/pallas_call | solution.py:354
  103.2 7.8 %shard_map.19 = (f32[8,256,256]{2,1,0:T(8,128)S(1)}, f32[512,256]{1,0:T(8,128)S(1)}) custom-call(s32[3]{0:T(128)S(1)} %pad_add_fusion.at_ref, f32[8192,128]{1,0:T(8,128)S(1)} %bitcast.37, f32[16,10,8,256]{3,2,1,0:T(8,128)S(1)} %all-to-all-done.2.own_ref, f32[16,10,8,256]{3,2,1,0:T(8,128)S(1)} %collective-permute-done.4.other_ref, ...), custom_call_target="tpu_custom_call" | custom-call | flops 4831838208 | bytes 9437184 | tf_op jit(solution)/shard_map/pallas_call | solution.py:360
  111.1 0.8 copy-done.6
  111.9 4.3 %all-to-all-start.3 = ((f32[8,64,256]{2,1,0:T(8,128)}), f32[8,64,256]{2,1,0:T(8,128)}, u32[]{:S(2)}, u32[]{:S(2)}) async-start(f32[8,64,256]{2,1,0:T(8,128)} %bitcast.42), calls=%async_computation.3 | async-start | bytes 1048576 | tf_op jit(solution)/shard_map/all_to_all | solution.py:380
  116.2 1.1 copy-done.7
  117.3 1.3 copy-done.13
  118.6 0.9 copy-done.15
  119.5 12.8 %shard_map.20.mixer_ref = f32[256,256]{1,0:T(8,128)S(1)} custom-call(s32[3]{0:T(128)S(1)} %pad_add_fusion.at_ref, f32[16,10,8,256]{3,2,1,0:T(8,128)S(1)} %all-to-all-done.2.own_ref, f32[16,10,8,256]{3,2,1,0:T(8,128)S(1)} %copy-done.13, f32[256,256]{1,0:T(8,128)S(1)} %copy-done.15, f32[512,256]{1,0:T(8,128)S(1)} %copy-done.7), custom_call_target="tpu_custom_call" | custom-call | flops 10000000000 | bytes 1048576 | tf_op jit(solution)/shard_map/pallas_call | solution.py:370
  133.1 1.2 reduce_sum.30
  134.2 0.8 broadcast_in_dim.51
  135.1 6.4 %all-to-all-start.4 = ((f32[8,64,256]{2,1,0:T(8,128)}), f32[8,64,256]{2,1,0:T(8,128)}, u32[]{:S(2)}, u32[]{:S(2)}) async-start(f32[8,64,256]{2,1,0:T(8,128)} %broadcast_in_dim.51), calls=%async_computation.4 | async-start | bytes 1048576 | tf_op jit(solution)/shard_map/all_to_all | solution.py:296
  141.4 1.2 shard_map.21.y_ref
  142.6 16.9 %all-to-all-done.4 = f32[8,64,256]{2,1,0:T(8,128)} async-done(((f32[8,64,256]{2,1,0:T(8,128)}), f32[8,64,256]{2,1,0:T(8,128)}, u32[]{:S(2)}, u32[]{:S(2)}) %all-to-all-start.4) | async-done | bytes 524320 | tf_op jit(solution)/shard_map/all_to_all | solution.py:296
  159.5 1.7 shard_map.22
  161.8 1.5 collective-permute-done.5
  163.3 0.9 slice_add_fusion
  164.2 1.0 slice_select_fusion
  165.3 0.8 copy.10
  166.1 4.1 %all-to-all-start.5 = ((f32[4,3,32,256]{3,2,1,0:T(8,128)}), f32[4,3,32,256]{3,2,1,0:T(8,128)}, u32[]{:S(2)}, u32[]{:S(2)}) async-start(f32[4,3,32,256]{3,2,1,0:T(8,128)} %bitcast.34), calls=%async_computation.5 | async-start | bytes 786432 | tf_op jit(solution)/shard_map/all_to_all | solution.py:392
  170.2 2.1 shard_map.23
  172.3 0.8 copy-done.4
  173.1 4.9 %all-to-all-done.5 = f32[4,3,32,256]{3,2,1,0:T(8,128)} async-done(((f32[4,3,32,256]{3,2,1,0:T(8,128)}), f32[4,3,32,256]{3,2,1,0:T(8,128)}, u32[]{:S(2)}, u32[]{:S(2)}) %all-to-all-start.5) | async-done | bytes 393248 | tf_op jit(solution)/shard_map/all_to_all | solution.py:392
  178.1 0.9 slice_reduce_fusion
  179.0 1.0 slice.59
  180.3 23.1 %all_to_all.35 = f32[16,3,32,256]{3,2,1,0:T(8,128)S(1)} all-to-all(f32[16,3,32,256]{3,2,1,0:T(8,128)S(1)} %broadcast_in_dim.52), channel_id=1, replica_groups={{0,2,4,6,8,10,12,14,16,18,20,22,24,26,28,30},{1,3,5,7,9,11,13,15,17,19,..., dimensions={0} | all-to-all | bytes 3145728 | tf_op jit(solution)/shard_map/all_to_all | solution.py:296
  203.4 3.5 %collective-permute-start.6 = (f32[4,4,3,32,256]{4,3,2,1,0:T(8,128)S(1)}, f32[4,4,3,32,256]{4,3,2,1,0:T(8,128)S(1)}, u32[]{:S(2)}, u32[]{:S(2)}) collective-permute-start(f32[4,4,3,32,256]{4,3,2,1,0:T(8,128)S(1)} %bitcast.39), channel_id=1, source_target_pairs={{0,1},{1,0},{2,3},{3,2},{4,5},{5,4},{6,7},{7,6},{8,9},{9,8},{10,11... | collective-permute-start | bytes 4718600 | tf_op jit(solution)/shard_map/ppermute | solution.py:401
  206.9 3.0 %collective-permute-done.6.other_ref.other_proj_ref = f32[4,4,3,32,256]{4,3,2,1,0:T(8,128)S(1)} collective-permute-done((f32[4,4,3,32,256]{4,3,2,1,0:T(8,128)S(1)}, f32[4,4,3,32,256]{4,3,2,1,0:T(8,128)S(1)}, u32[]{:S(2)}, u32[]{:S(2)}) %collective-permute-start.6) | collective-permute-done | bytes 1572896 | tf_op jit(solution)/shard_map/ppermute | solution.py:401
  209.9 8.9 %shard_map.24 = f32[8192,128]{1,0:T(8,128)} custom-call(s32[3]{0:T(128)S(1)} %pad_add_fusion.at_ref, f32[8192,128]{1,0:T(8,128)S(1)} %bitcast.38, f32[8,256,256]{2,1,0:T(8,128)S(1)} %get-tuple-element.33.left_ref, f32[4,4,3,32,256]{4,3,2,1,0:T(8,128)S(1)} %bitcast.40, f32[4,4,3,32,256]{4,3,2,1,0:T(8,128)S(1)} %collective-permute-done.6.other_ref.other_proj_ref, ...), custom_call_target="tpu_custom_call" | custom-call | flops 3221225472 | bytes 12582912 | tf_op jit(solution)/shard_map/pallas_call | solution.py:404
  (52 shorter events, 4.9 us)
Async XLA Ops:
  0.1 2.2 %copy-start = (f32[8,256,2,256]{3,2,1,0:T(2,128)S(1)}, f32[8,256,2,256]{3,2,1,0:T(2,128)}, u32[]{:S(2)}) copy-start(f32[8,256,2,256]{3,2,1,0:T(2,128)} %param.1) | copy-start | bytes 12582916
  6.9 7.0 %collective-permute-start.1 = (f32[16,9,8,256]{3,2,1,0:T(8,128)S(1)}, f32[16,9,8,256]{3,2,1,0:T(8,128)}, u32[]{:S(2)}, u32[]{:S(2)}) collective-permute-start(f32[16,9,8,256]{3,2,1,0:T(8,128)S(1)} %slice_bitcast_fusion), channel_id=1, source_target_pairs={{0,1},{32,33},{64,65},{96,97},{128,129},{160,161},{192,193},{224,2... | collective-permute-start | bytes 3538952 | tf_op jit(solution)/shard_map/ppermute | solution.py:337
  16.4 23.5 %all-to-all-start = ((f32[16,9,8,256]{3,2,1,0:T(8,128)}), f32[16,9,8,256]{3,2,1,0:T(8,128)S(1)}, u32[]{:S(2)}, u32[]{:S(2)}) async-start(f32[16,9,8,256]{3,2,1,0:T(8,128)} %fusion), calls=%async_computation | async-start | bytes 2359296 | tf_op jit(solution)/shard_map/all_to_all | solution.py:339
  21.8 17.9 %collective-permute-start = (f32[1024,128]{1,0:T(8,128)S(1)}, f32[1024,128]{1,0:T(8,128)S(1)}, u32[]{:S(2)}, u32[]{:S(2)}) collective-permute-start(f32[1024,128]{1,0:T(8,128)S(1)} %broadcast_select_fusion), channel_id=1, source_target_pairs={{0,128},{1,129},{2,130},{3,131},{4,132},{5,133},{6,134},{7,135},{8... | collective-permute-start | bytes 1572872 | tf_op jit(solution)/shard_map/ppermute | solution.py:301
  40.0 9.8 %collective-permute-start.2 = (f32[1024,128]{1,0:T(8,128)S(1)}, f32[1024,128]{1,0:T(8,128)S(1)}, u32[]{:S(2)}, u32[]{:S(2)}) collective-permute-start(f32[1024,128]{1,0:T(8,128)S(1)} %fusion.2), channel_id=1, source_target_pairs={{0,64},{128,192},{1,65},{129,193},{2,66},{130,194},{3,67},{131,195... | collective-permute-start | bytes 1572872 | tf_op jit(solution)/shard_map/ppermute | solution.py:301
  42.0 18.2 %all-to-all-start.1 = ((f32[8,2,8,256]{3,2,1,0:T(8,128)}), f32[8,2,8,256]{3,2,1,0:T(8,128)S(1)}, u32[]{:S(2)}, u32[]{:S(2)}) async-start(f32[8,2,8,256]{3,2,1,0:T(8,128)} %broadcast_in_dim.48), calls=%async_computation.1 | async-start | bytes 262144 | tf_op jit(solution)/shard_map/all_to_all | solution.py:296
  61.4 23.0 %all-to-all-start.2 = ((f32[16,10,8,256]{3,2,1,0:T(8,128)}), f32[16,10,8,256]{3,2,1,0:T(8,128)S(1)}, u32[]{:S(2)}, u32[]{:S(2)}) async-start(f32[16,10,8,256]{3,2,1,0:T(8,128)} %broadcast_in_dim.50), calls=%async_computation.2 | async-start | bytes 2621440 | tf_op jit(solution)/shard_map/all_to_all | solution.py:296
  67.5 9.5 %collective-permute-start.3 = (f32[1024,128]{1,0:T(8,128)S(1)}, f32[1024,128]{1,0:T(8,128)S(1)}, u32[]{:S(2)}, u32[]{:S(2)}) collective-permute-start(f32[1024,128]{1,0:T(8,128)S(1)} %add.38), channel_id=1, source_target_pairs={{0,32},{64,96},{128,160},{192,224},{1,33},{65,97},{129,161},{193,2... | collective-permute-start | bytes 1572872 | tf_op jit(solution)/shard_map/ppermute | solution.py:301
  84.4 18.9 %copy-start.1 = (f32[8,256,2,256]{3,2,1,0:T(2,128)S(1)}, f32[8,256,2,256]{3,2,1,0:T(2,128)}, u32[]{:S(2)}) copy-start(f32[8,256,2,256]{3,2,1,0:T(2,128)} %param.1) | copy-start | bytes 12582916
  84.4 6.9 %collective-permute-start.4 = (f32[16,10,8,256]{3,2,1,0:T(8,128)S(1)}, f32[16,10,8,256]{3,2,1,0:T(8,128)S(1)}, u32[]{:S(2)}, u32[]{:S(2)}) collective-permute-start(f32[16,10,8,256]{3,2,1,0:T(8,128)S(1)} %all-to-all-done.2.own_ref), channel_id=1, source_target_pairs={{0,1},{1,0},{2,3},{3,2},{4,5},{5,4},{6,7},{7,6},{8,9},{9,8},{10,11... | collective-permute-start | bytes 3932168 | tf_op jit(solution)/shard_map/ppermute | solution.py:348
  91.3 11.9 %copy-start.12 = (f32[16,10,8,256]{3,2,1,0:T(8,128)}, f32[16,10,8,256]{3,2,1,0:T(8,128)S(1)}, u32[]{:S(2)}) copy-start(f32[16,10,8,256]{3,2,1,0:T(8,128)S(1)} %collective-permute-done.4.other_ref) | copy-start | bytes 3932164
  101.8 0.7 copy-start.8
  102.5 0.7 copy-start.14
  111.0 0.8 copy-start.6
  111.9 21.2 %all-to-all-start.3 = ((f32[8,64,256]{2,1,0:T(8,128)}), f32[8,64,256]{2,1,0:T(8,128)}, u32[]{:S(2)}, u32[]{:S(2)}) async-start(f32[8,64,256]{2,1,0:T(8,128)} %bitcast.42), calls=%async_computation.3 | async-start | bytes 1048576 | tf_op jit(solution)/shard_map/all_to_all | solution.py:380
  116.2 1.1 copy-start.7
  117.3 1.3 copy-start.13
  118.6 0.9 copy-start.15
  132.3 0.7 copy-start.10
  133.1 8.4 %copy-start.3 = (f32[1024,128]{1,0:T(8,128)S(1)}, f32[1024,128]{1,0:T(8,128)}, u32[]{:S(2)}) copy-start(f32[1024,128]{1,0:T(8,128)} %add.39.top_ref) | copy-start | bytes 1572868
  133.1 8.4 %copy-start.16 = (f32[256,256]{1,0:T(8,128)S(1)}, f32[256,256]{1,0:T(8,128)}, u32[]{:S(2)}) copy-start(f32[256,256]{1,0:T(8,128)} %copy-done.14) | copy-start | bytes 786436
  135.1 24.4 %all-to-all-start.4 = ((f32[8,64,256]{2,1,0:T(8,128)}), f32[8,64,256]{2,1,0:T(8,128)}, u32[]{:S(2)}, u32[]{:S(2)}) async-start(f32[8,64,256]{2,1,0:T(8,128)} %broadcast_in_dim.51), calls=%async_computation.4 | async-start | bytes 1048576 | tf_op jit(solution)/shard_map/all_to_all | solution.py:296
  161.2 2.1 collective-permute-start.5
  165.2 5.0 %copy-start.11 = (f32[256,256]{1,0:T(8,128)S(1)}, f32[256,256]{1,0:T(8,128)}, u32[]{:S(2)}) copy-start(f32[256,256]{1,0:T(8,128)} %copy-done.10) | copy-start | bytes 786436
  166.1 12.0 %all-to-all-start.5 = ((f32[4,3,32,256]{3,2,1,0:T(8,128)}), f32[4,3,32,256]{3,2,1,0:T(8,128)}, u32[]{:S(2)}, u32[]{:S(2)}) async-start(f32[4,3,32,256]{3,2,1,0:T(8,128)} %bitcast.34), calls=%async_computation.5 | async-start | bytes 786432 | tf_op jit(solution)/shard_map/all_to_all | solution.py:392
  172.3 0.8 copy-start.4
  179.0 30.9 %copy-start.9 = (f32[256,256]{1,0:T(8,128)S(1)}, f32[256,256]{1,0:T(8,128)}, u32[]{:S(2)}) copy-start(f32[256,256]{1,0:T(8,128)} %copy-done.8) | copy-start | bytes 786436
  180.1 29.9 %copy-start.2 = (f32[8,256,2,256]{3,2,1,0:T(2,128)S(1)}, f32[8,256,2,256]{3,2,1,0:T(2,128)}, u32[]{:S(2)}) copy-start(f32[8,256,2,256]{3,2,1,0:T(2,128)} %param.1) | copy-start | bytes 12582916
  180.2 29.7 %copy-start.5 = (f32[256,512]{1,0:T(8,128)S(1)}, f32[256,512]{1,0:T(8,128)}, u32[]{:S(2)}) copy-start(f32[256,512]{1,0:T(8,128)} %copy-done.4) | copy-start | bytes 1572868
  203.4 6.5 %collective-permute-start.6 = (f32[4,4,3,32,256]{4,3,2,1,0:T(8,128)S(1)}, f32[4,4,3,32,256]{4,3,2,1,0:T(8,128)S(1)}, u32[]{:S(2)}, u32[]{:S(2)}) collective-permute-start(f32[4,4,3,32,256]{4,3,2,1,0:T(8,128)S(1)} %bitcast.39), channel_id=1, source_target_pairs={{0,1},{1,0},{2,3},{3,2},{4,5},{5,4},{6,7},{7,6},{8,9},{9,8},{10,11... | collective-permute-start | bytes 4718600 | tf_op jit(solution)/shard_map/ppermute | solution.py:401

commit v3 on v2

v3 whole, which is shorter than its diff:
```python
import functools
import jax
import jax.numpy as jnp
from jax import lax
from jax.experimental import pallas as pl
from jax.experimental.pallas import tpu as pltpu
from jax.sharding import PartitionSpec as P

HP = lax.Precision.HIGHEST
XS, YS, CORES = 4, 4, 2
CHIPS = XS * YS
LANES = 128
BASE = 64
GROUP = 8
PLANE = [[q * CORES + k for q in range(CHIPS)] for k in range(CORES)]
LINE = YS * CORES
LINES = [[x * LINE + j for j in range(LINE)] for x in range(XS)]
SWAP = [(i, i ^ 1) for i in range(CHIPS * CORES)]
VMEM = pl.BlockSpec(memory_space=pltpu.VMEM)
SMEM = pl.BlockSpec(memory_space=pltpu.SMEM)


def mm(a, b):
    return jnp.dot(a, b, precision=HP, preferred_element_type=jnp.float32)


def mm_tn(a, b):
    return lax.dot_general(a, b, (((0,), (0,)), ((), ())), precision=HP, preferred_element_type=jnp.float32)


def mm_nt(a, b):
    return lax.dot_general(a, b, (((1,), (1,)), ((), ())), precision=HP, preferred_element_type=jnp.float32)


def eliminate(block, jordan):
    n = block.shape[0]
    eye = (lax.broadcasted_iota(jnp.int32, (n, n), 0) == lax.broadcasted_iota(jnp.int32, (n, n), 1))
    wide = jnp.concatenate([block, eye.astype(jnp.float32)], axis=1)
    shape = (GROUP, 2 * n)
    groups = n // GROUP
    at = lax.broadcasted_iota(jnp.int32, shape, 0)
    w = [wide[g * GROUP : (g + 1) * GROUP] for g in range(groups)]
    for p in range(groups):
        live = [g for g in range(groups) if jordan or g >= p]
        cols = {
            g: [
                jnp.broadcast_to(w[g][:, p * GROUP + b : p * GROUP + b + 1], shape)
                for b in range(GROUP)
            ]
            for g in live
        }
        for a in range(GROUP):
            inv = 1.0 / cols[p][a][a : a + 1]
            row = w[p][a : a + 1]
            heads = [cols[p][b][a : a + 1] for b in range(GROUP)]
            for g in live:
                m = cols[g][a] * inv
                if g == p:
                    m = jnp.where(at != a if jordan else at > a, m, 0.0)
                for b in range(a + 1, GROUP):
                    cols[g][b] = cols[g][b] - m * heads[b]
                w[g] = w[g] - m * row
    return jnp.concatenate(w, axis=0)


def diagonal(wide):
    n = wide.shape[0]
    shape = wide.shape
    eye = lax.broadcasted_iota(jnp.int32, shape, 0) == lax.broadcasted_iota(jnp.int32, shape, 1)
    return jnp.sum(jnp.where(eye, wide, 0.0), axis=1, keepdims=True)


def factor(a):
    n = a.shape[0]
    if n <= BASE:
        wide = eliminate(a, False)
        wide = wide * (1.0 / jnp.sqrt(diagonal(wide)))
        left = wide[:, :n]
        upper = lax.broadcasted_iota(jnp.int32, (n, n), 0) <= lax.broadcasted_iota(jnp.int32, (n, n), 1)
        return jnp.where(upper, left, 0.0), wide[:, n:]
    h = n // 2
    u11, i11 = factor(a[:h, :h])
    u12 = mm(i11, a[:h, h:])
    u22, i22 = factor(a[h:, h:] - mm_tn(u12, u12))
    i21 = -mm(i22, mm_tn(u12, i11))
    zero = jnp.zeros((h, h), jnp.float32)
    upper = jnp.concatenate([jnp.concatenate([u11, u12], 1), jnp.concatenate([zero, u22], 1)], 0)
    inv = jnp.concatenate([jnp.concatenate([i11, zero], 1), jnp.concatenate([i21, i22], 1)], 0)
    return upper, inv


def inverse(a):
    n = a.shape[0]
    if n <= BASE:
        wide = eliminate(a, True)
        return (wide * (1.0 / diagonal(wide)))[:, n:]
    h = n // 2
    i11 = inverse(a[:h, :h])
    x = mm(i11, a[:h, h:])
    y = mm(a[h:, :h], i11)
    s = inverse(a[h:, h:] - mm(a[h:, :h], x))
    xs = mm(x, s)
    top = jnp.concatenate([i11 + mm(xs, y), -xs], 1)
    return jnp.concatenate([top, jnp.concatenate([-mm(s, y), s], 1)], 0)


def split(a):
    high = a.astype(jnp.bfloat16)
    return high, (a - high.astype(jnp.float32)).astype(jnp.bfloat16)


def dot3(a, b, dims):
    one = functools.partial(
        lax.dot_general, dimension_numbers=(dims, ((), ())), preferred_element_type=jnp.float32
    )
    return one(a[0], b[0]) + (one(a[0], b[1]) + one(a[1], b[0]))


def identity(n):
    rows = lax.broadcasted_iota(jnp.int32, (n, n), 0)
    return (rows == lax.broadcasted_iota(jnp.int32, (n, n), 1)).astype(jnp.float32)


def tile(ref, m, t, nm, nt):
    return ref[pl.ds(t * nm + m, ref.shape[0] // (nm * nt), stride=nm * nt), :]


def in_order(at_ref, own, other):
    first = at_ref[2] == 0
    return jnp.concatenate([jnp.where(first, own, other), jnp.where(first, other, own)], axis=0)


def rows_of(ref):
    return ref[...].reshape(-1, ref.shape[-1])


def pack_kernel(nm, nt, at_ref, x_ref, packet_ref, gram_ref):
    step = pl.program_id(0)
    panel = jnp.concatenate([tile(x_ref, 0, t, nm, nt) for t in range(nt)], axis=1)
    panel = jnp.where((step == 0) & (at_ref[0] == 0), 0.0, panel)
    last = packet_ref.shape[2] - 1
    packet_ref[:, :, pl.ds(step, 1)] = panel.reshape(CORES, CHIPS, 1, *packet_ref.shape[3:])
    more = mm_tn(panel, panel)

    @pl.when(step == 0)
    def _():
        gram_ref[...] = more

    @pl.when(step > 0)
    def _():
        gram_ref[...] += more

    @pl.when(step == last - 1)
    def _():
        packet_ref[:, :, last] = gram_ref[...].reshape(CORES, CHIPS, *packet_ref.shape[3:])


def factor_kernel(at_ref, own_ref, other_ref, upper_ref, inv_ref, inv_t_ref):
    upper, inv = factor(in_order(at_ref, rows_of(own_ref), rows_of(other_ref)))
    upper_ref[...] = upper
    inv_ref[...] = inv
    inv_t_ref[...] = inv.T


def mixer_kernel(at_ref, own_ref, other_ref, inv_ref, after_ref, mixer_ref):
    top = in_order(at_ref, rows_of(own_ref), rows_of(other_ref))
    mixer_ref[...] = inverse(identity(top.shape[0]) + mm_nt(inv_ref[...], top))


def rows_kernel(at_ref, own_ref, other_ref, inv_t_ref, y_ref, slab_ref, flip_ref):
    y = mm(in_order(at_ref, rows_of(own_ref), rows_of(other_ref)), inv_t_ref[...])
    y += jnp.where((pl.program_id(0) == 0) & (at_ref[0] == 1), identity(y.shape[0]), 0.0)
    y_ref[0] = y
    flip_ref[...] = y.T
    deep = slab_ref.shape[0]
    slab_ref[...] = flip_ref[pl.ds(pl.multiple_of(at_ref[3] * deep, deep), deep), :]


def apply_kernel(
    nm, nt, at_ref, x_ref, top_ref, far_ref, more_ref, inv_ref, keep_ref, send_ref, y_ref, high_ref, low_ref
):
    step = pl.program_id(0)
    nb = inv_ref.shape[0]

    @pl.when(step == 0)
    def _():
        for m in range(nm):
            panel = jnp.concatenate(
                [
                    jnp.where(
                        at_ref[4] == 1,
                        tile(top_ref, m, t, nm, nt),
                        tile(far_ref, m, t, nm, nt) + tile(more_ref, m, t, nm, nt),
                    )
                    for t in range(nt)
                ],
                axis=1,
            )
            if m == 0:
                panel = jnp.where(at_ref[1] == 0, 0.0, panel)
            y = mm(inv_ref[...], panel)
            if m == 0:
                y += jnp.where(at_ref[1] == 1, identity(nb), 0.0)
            y_ref[:, m * nb : (m + 1) * nb] = y
            high_ref[m * nb : (m + 1) * nb], low_ref[m * nb : (m + 1) * nb] = split(y.T)

    block = jnp.concatenate(
        [tile(x_ref, m, t, nm, nt) for m in range(nm) for t in range(nt)], axis=1
    )
    part = dot3(split(block), (high_ref[...], low_ref[...]), ((1,), (0,)))
    part = jnp.where((step == 0) & (at_ref[0] == 0), 0.0, part)
    first = at_ref[2] == 0
    hb = nb // CORES
    keep_ref[...] = jnp.where(first, part[:hb], part[hb:]).reshape(keep_ref.shape)
    send_ref[...] = jnp.where(first, part[hb:], part[:hb]).reshape(send_ref.shape)


def proj_kernel(at_ref, slab_ref, own_ref, other_ref, copies_ref):
    step = pl.program_id(0)
    more = mm(slab_ref[...], in_order(at_ref, rows_of(own_ref), rows_of(other_ref)))

    @pl.when(step == 0)
    def _():
        copies_ref[0] = more

    @pl.when(step > 0)
    def _():
        copies_ref[0] += more

    @pl.when(step == pl.num_programs(0) - 1)
    def _():
        for i in range(1, copies_ref.shape[0]):
            copies_ref[i] = copies_ref[0]


def sides_kernel(at_ref, mixer_ref, y_ref, near_ref, far_ref, more_ref, z_ref, v_ref):
    mixer = mixer_ref[...]
    nb = mixer.shape[0]
    for m in range(y_ref.shape[1] // nb):
        halves = [
            jnp.where(at_ref[5] == 1, near_ref[h, :, m], far_ref[h, :, m] + more_ref[h, :, m])
            for h in range(CORES)
        ]
        ay = in_order(at_ref, *[half.reshape(nb // CORES, nb) for half in halves])
        z_ref[:, m * nb : (m + 1) * nb] = lax.dot_general(
            mixer, ay, (((0,), (1,)), ((), ())), precision=HP, preferred_element_type=jnp.float32
        )
    v_ref[...] = mm(mixer, y_ref[...])


def update_kernel(
    nm, nt, at_ref, x_ref, left_ref, own_ref, other_ref, proj_ref,
    mixer_ref, y_ref, z_ref, v_ref, upper_ref, out_ref, high_ref, low_ref,
):
    step = pl.program_id(0)
    nb = mixer_ref.shape[0]

    @pl.when(step == 0)
    def _():
        mixer = mixer_ref[...]
        core = mm(mm_tn(mixer, proj_ref[...]), mixer)
        w = split(z_ref[...] - mm_tn(core, y_ref[...]))
        v = split(v_ref[...])
        for i, ref in enumerate((high_ref, low_ref)):
            ref[:nb] = w[i]
            ref[nb:] = v[i]

    ay = in_order(at_ref, rows_of(own_ref), rows_of(other_ref))
    left = split(jnp.concatenate([left_ref[0], ay], axis=1))
    change = dot3(left, (high_ref[...], low_ref[...]), ((1,), (0,)))
    rows = nb
    for m in range(nm):
        for t in range(nt):
            at = m * nb + t * LANES
            out_ref[pl.ds(t * nm + m, rows, stride=nm * nt), :] = (
                tile(x_ref, m, t, nm, nt) - change[:, at : at + LANES]
            )

    @pl.when(at_ref[1] == 0)
    def _():
        keep = (step == 0) & (at_ref[0] == 0)
        band = jnp.where((step == 0) & (at_ref[0] == 1), -upper_ref[...], 0.0)
        for t in range(nt):
            old = tile(x_ref, 0, t, nm, nt)
            out_ref[pl.ds(t * nm, rows, stride=nm * nt), :] = jnp.where(
                keep, old, band[:, t * LANES : (t + 1) * LANES]
            )

    @pl.when((step == 0) & (at_ref[0] == 0))
    def _():
        band = jnp.where(at_ref[1] == 1, -upper_ref[...].T, 0.0)
        for m in range(nm):
            for t in range(nt):
                new = band[:, t * LANES : (t + 1) * LANES] if m == 0 else jnp.zeros((rows, LANES))
                if m == 0:
                    new = jnp.where(at_ref[1] == 0, tile(x_ref, m, t, nm, nt), new)
                out_ref[pl.ds(t * nm + m, rows, stride=nm * nt), :] = new


def call(kernel, outs, ins, grid=(), flops=0, moved=1 << 20, scratch=()):
    return pl.pallas_call(
        kernel,
        grid=grid,
        out_shape=[jax.ShapeDtypeStruct(s, jnp.float32) for s, _ in outs],
        in_specs=ins,
        out_specs=[spec for _, spec in outs],
        scratch_shapes=list(scratch),
        compiler_params=pltpu.CompilerParams(vmem_limit_bytes=40 << 20),
        cost_estimate=pl.CostEstimate(flops=flops, bytes_accessed=moved, transcendentals=0),
    )


def share(piece, axis, count, groups=None):
    copies = jnp.broadcast_to(piece[None], (count,) + piece.shape)
    return lax.all_to_all(copies, axis, 0, 0, axis_index_groups=groups)


def move(block, root, nz, hops):
    lines = CHIPS * CORES
    pairs = [
        ((root(c) + i) % nz * lines + c, (root(c) + j) % nz * lines + c)
        for c in range(lines)
        for i, j in hops
    ]
    return lax.ppermute(block, ("prow", "pcol"), pairs)


def near_moves(block, root, nz):
    return move(block, root, nz, [(0, 3)]), move(block, root, nz, [(0, 6)])


def far_moves(block, root, nz):
    return move(block, root, nz, [(0, 1), (3, 4)]), move(block, root, nz, [(0, 7), (3, 2), (6, 5)])


def body(hamiltonian):
    nl, nb, nm, _ = hamiltonian.shape
    nt = nb // LANES
    nz = lax.axis_size("prow")
    prow = lax.axis_index("prow")
    pcol = lax.axis_index("pcol")
    core = pcol % CORES
    sub = nb // (CHIPS * CORES)
    nc = nm * nb
    away = (prow + nz - pcol % nz) % nz
    relay = lambda d: (d == 0) | (d == 3) | (d == 6)
    at = jnp.stack([prow, pcol, core, pcol % LINE, relay(prow), relay(away)]).astype(jnp.int32)
    square, wide = (nb, nb), (nb, nc)
    whole = lambda shape: pl.BlockSpec(shape, lambda l: (0,) * len(shape))
    chunk = lambda index: pl.BlockSpec((CHIPS, 1, sub, nb), index)
    barrier = lax.optimization_barrier

    x = hamiltonian.reshape(nl, nb, nm, nt, LANES).transpose(0, 1, 3, 2, 4)
    x = x.reshape(nl * nb * nt * nm, LANES)
    x_rows = nb * nt * nm
    x_spec = pl.BlockSpec((x_rows, LANES), lambda l: (l, 0))

    root = lambda c: 0
    near = near_moves(x[:x_rows], root, nz)

    packet_shape = (CORES, CHIPS, nl + 1, sub, nb)
    packet = call(
        functools.partial(pack_kernel, nm, nt),
        [(packet_shape, whole(packet_shape))],
        [SMEM, x_spec],
        grid=(nl,),
        flops=2 * 10**10,
        moved=6 << 20,
        scratch=[pltpu.VMEM(square, jnp.float32)],
    )(at, x)[0]
    outgoing = jnp.where(core == 0, packet[0], lax.ppermute(packet[1], "pcol", [(0, 1)]))
    mine = lax.all_to_all(outgoing, "pcol", 0, 0, axis_index_groups=PLANE)[0]
    near, mine = barrier((near, mine))
    p_cols = jnp.where(prow == 0, x[:x_rows], near[0] + near[1])
    stacked = share(jnp.stack([mine[nl], mine[0]]), "prow", nz)
    summed = jnp.stack([jnp.sum(stacked[:, 0], axis=0), stacked[1, 1]])
    small = share(summed, "pcol", CHIPS, PLANE)
    p_cols, small, mine = barrier((p_cols, small, mine))
    far = far_moves(p_cols, root, nz)
    other_small = lax.ppermute(small, "pcol", SWAP)
    gram_spec = chunk(lambda l: (0, 0, 0, 0))
    upper, inv, inv_t = call(
        factor_kernel, [(square, VMEM)] * 3, [SMEM, gram_spec, gram_spec], grid=(1,), flops=10**10
    )(at, small, other_small)
    own_p = share(mine[:nl], "pcol", CHIPS, PLANE)
    far, inv, inv_t = barrier((far, inv, inv_t))

    half_shape = (CHIPS, nl, sub, nb)
    row_spec = chunk(lambda l: (0, l, 0, 0))
    keep, send, y_cols = call(
        functools.partial(apply_kernel, nm, nt),
        [(half_shape, row_spec), (half_shape, row_spec), (wide, whole(wide))],
        [SMEM, x_spec] + [whole((x_rows, LANES))] * 3 + [whole(square)],
        grid=(nl,),
        flops=12 * nl * nb**2 * nc,
        moved=9 << 20,
        scratch=[pltpu.VMEM((nc, nb), jnp.bfloat16)] * 2,
    )(at, x, p_cols, *far, inv)
    keep, send, own_p = barrier((keep, send, own_p))
    other_p = lax.ppermute(own_p, "pcol", SWAP)
    parts = keep + lax.ppermute(send, "pcol", SWAP)
    parts = lax.all_to_all(parts, "pcol", 0, 0, axis_index_groups=PLANE)
    slab_rows = nb // LINE
    y_rows, slab = call(
        rows_kernel,
        [((nl, nb, nb), pl.BlockSpec((1, nb, nb), lambda l: (l, 0, 0))),
         ((slab_rows, nl * nb), pl.BlockSpec((slab_rows, nb), lambda l: (0, l)))],
        [SMEM, row_spec, row_spec, whole(square)],
        grid=(nl,),
        flops=5 * 10**9,
        moved=6 << 20,
        scratch=[pltpu.VMEM(square, jnp.float32)],
    )(at, own_p, other_p, inv_t)
    parts, y_rows, slab = barrier((parts, y_rows, slab))
    own = share(jnp.sum(parts, axis=0), "pcol", CHIPS, PLANE)
    mixer = call(
        mixer_kernel,
        [(square, VMEM)],
        [SMEM] + [chunk(lambda l: (0, 1, 0, 0))] * 2 + [VMEM, pl.BlockSpec(memory_space=pl.ANY)],
        grid=(1,),
        flops=10**10,
    )(at, small, other_small, inv, parts)[0]
    own, mixer = barrier((own, mixer))
    other = lax.ppermute(own, "pcol", SWAP)

    picked = jnp.stack(
        [
            jnp.stack(
                [lax.dynamic_index_in_dim(a, m * XS + pcol // nz, 1, keepdims=False) for m in range(nm)], 1
            )
            for a in (own, other)
        ]
    )
    root = lambda c: c % nz
    near = near_moves(picked, root, nz)

    copies = call(
        proj_kernel,
        [((nz, slab_rows, nb), whole((nz, slab_rows, nb)))],
        [SMEM, pl.BlockSpec((slab_rows, nb), lambda l: (0, l)), row_spec, row_spec],
        grid=(nl,),
        flops=10**9,
        moved=4 << 20,
    )(at, slab, own, other)[0]
    pieces = lax.all_to_all(copies, "prow", 0, 0)
    near, pieces = barrier((near, pieces))
    ay_cols = jnp.where(away == 0, picked, near[0] + near[1])
    far = far_moves(ay_cols, root, nz)
    proj = share(jnp.sum(pieces, axis=0), "pcol", LINE, LINES).reshape(square)
    far, proj = barrier((far, proj))
    z_cols, v_cols = call(sides_kernel, [(wide, VMEM)] * 2, [SMEM] + [VMEM] * 5, flops=3 * 10**9)(
        at, mixer, y_cols, ay_cols, *far
    )

    out = call(
        functools.partial(update_kernel, nm, nt),
        [(x.shape, x_spec)],
        [SMEM, x_spec, pl.BlockSpec((1, nb, nb), lambda l: (l, 0, 0)), row_spec, row_spec]
        + [whole(s) for s in (square, square, wide, wide, wide, square)],
        grid=(nl,),
        flops=12 * nl * nb**2 * nc,
        moved=12 << 20,
        scratch=[pltpu.VMEM((2 * nb, nc), jnp.bfloat16)] * 2,
    )(at, x, y_rows, own, other, proj, mixer, y_cols, z_cols, v_cols, upper)[0]
    out = out.reshape(nl, nb, nt, nm, LANES).transpose(0, 1, 3, 2, 4)
    return out.reshape(hamiltonian.shape)


def solution(mesh):
    return jax.shard_map(
        body,
        mesh=mesh,
        in_specs=(P(None, "prow", None, "pcol"),),
        out_specs=P(None, "prow", None, "pcol"),
        check_vma=False,
    )
```

time: 220 us -> 208 us (0.945)
  waiting for transfers between devices: 70.4 us -> 37.1 us
  blocking collectives: 23.1 us -> 43.3 us
  Pallas kernels: 49.6 us -> 52.8 us
  other arithmetic: 7.95 us -> 4.96 us
  local copies, waits for them, and re-layouts: 15.5 us -> 17.8 us
    all_to_all x3, waiting for transfers between devices: 33.7 us -> 8.43 us  [share(): return lax.all_to_all(copies, axis, 0, 0, axis_index_groups=groups)]
    ppermute x6 -> x12, waiting for transfers between devices: 29.1 us -> 9.93 us  [the longest x1 5.69 us: body(): lax.ppermute(packet[1], 'pcol', [(0, 1)])]
    all_to_all x0 -> x1, blocking collectives: none -> 12.3 us  [body(): pieces = lax.all_to_all(copies, 'prow', 0, 0)]
    all_to_all x1, waiting for transfers between devices: 0.01 us -> 9.79 us  [body(): mine = lax.all_to_all(outgoing, 'pcol', 0, 0, axis_index_groups=PLANE)[0]]
    all_to_all x1 -> x2, blocking collectives: 23.1 us -> 31 us  [share(): return lax.all_to_all(copies, axis, 0, 0, axis_index_groups=groups)]
    all_to_all x3, starting transfers between devices: 19.9 us -> 14.9 us  [share(): return lax.all_to_all(copies, axis, 0, 0, axis_index_groups=groups)]
    ppermute x6 -> x12, starting transfers between devices: 15.6 us -> 20.4 us  [the longest x8 15 us: move(): return lax.ppermute(block, ('prow', 'pcol'), pairs)]
    unnamed x34 -> x48, local copies, waits for them, and re-layouts: 9.3 us -> 13.4 us
  transfers between devices with their start and end apart: 13 -> 18, of which waited for: 11 -> 9; matrix products, arithmetic and copies ran while one was open for 2% -> 2% of each run, Pallas kernels for 7% -> 18%
where the time goes in v3:
time: 208 us; the launch traced here: 207 us
  Pallas kernels  52.8 us (25%)
  starting transfers between devices  50.9 us (24%)
  blocking collectives  43.3 us (21%)
  waiting for transfers between devices  37.1 us (18%)
  local copies, waits for them, and re-layouts  17.8 us (9%)
  other arithmetic  4.96 us (2%)
    all_to_all x2, blocking collectives, share(): return lax.all_to_all(copies, axis, 0, 0, axis_index_groups=groups)  31 us
    ppermute x8, starting transfers between devices, move(): return lax.ppermute(block, ('prow', 'pcol'), pairs)  15 us
    all_to_all x3, starting transfers between devices, share(): return lax.all_to_all(copies, axis, 0, 0, axis_index_groups=groups)  14.9 us
    unnamed x48, local copies, waits for them, and re-layouts  13.4 us
    pallas_call x1, Pallas kernels, body(): call(mixer_kernel, [(square, VMEM)], [SMEM] + [chunk(lambda l: (0, 1, 0,...  12.8 us
    all_to_all x1, blocking collectives, body(): pieces = lax.all_to_all(copies, 'prow', 0, 0)  12.3 us
    pallas_call x1, Pallas kernels, body(): call(factor_kernel, [(square, VMEM)] * 3, [SMEM, gram_spec, gram_spec], g...  10.5 us
    all_to_all x1, waiting for transfers between devices, body(): mine = lax.all_to_all(outgoing, 'pcol', 0, 0, axis_index_groups=PLANE)[0]  9.79 us
  transfers between devices with their start and end apart: 18, of which 9 were waited for; matrix products, arithmetic and copies ran while one was open for 2% of the time, Pallas kernels for 18%

profile of v3, /device:TPU:1, one launch (start us, length us, event | category | flops | bytes accessed | tf_op | source)
XLA Modules:
  0.0 207.3 jit_solution(7592301986154056612)
XLA Ops:
  0.1 2.2 %copy-done = f32[8,256,2,256]{3,2,1,0:T(2,128)S(1)} copy-done((f32[8,256,2,256]{3,2,1,0:T(2,128)S(1)}, f32[8,256,2,256]{3,2,1,0:T(2,128)}, u32[]{:S(2)}) %copy-start) | copy-done | bytes 4194328
  2.3 4.3 %shard_map.17 = f32[2,16,9,8,256]{4,3,2,1,0:T(8,128)S(1)} custom-call(s32[6]{0:T(128)S(1)} %stack.63.at_ref, f32[8192,128]{1,0:T(8,128)S(1)} %bitcast.34), custom_call_target="tpu_custom_call" | custom-call | flops 20000000000 | bytes 6291456 | tf_op jit(solution)/shard_map/pallas_call | solution.py:362
  6.7 1.3 collective-permute-start.2
  8.0 5.7 %collective-permute-done.2 = f32[16,9,8,256]{3,2,1,0:T(8,128)} collective-permute-done((f32[16,9,8,256]{3,2,1,0:T(8,128)S(1)}, f32[16,9,8,256]{3,2,1,0:T(8,128)}, u32[]{:S(2)}, u32[]{:S(2)}) %collective-permute-start.2) | collective-permute-done | bytes 1179680 | tf_op jit(solution)/shard_map/ppermute | solution.py:371
  13.7 2.5 %fusion = f32[16,9,8,256]{3,2,1,0:T(8,128)} fusion(f32[16,9,8,256]{3,2,1,0:T(8,128)} %collective-permute-done.2, f32[2,16,9,8,256]{4,3,2,1,0:T(8,128)S(1)} %shard_map.17, pred[]{:T(512)S(6)} %eq.34), kind=kLoop, calls=%fused_computation.2 | loop fusion | flops 294912 | bytes 3538945 | tf_op jit(solution)/shard_map/jit(_where)/select_n | solution.py:371
  16.2 3.7 %all-to-all-start = ((f32[16,9,8,256]{3,2,1,0:T(8,128)}), f32[16,9,8,256]{3,2,1,0:T(8,128)S(1)}, u32[]{:S(2)}, u32[]{:S(2)}) async-start(f32[16,9,8,256]{3,2,1,0:T(8,128)} %fusion), calls=%async_computation | async-start | bytes 2359296 | tf_op jit(solution)/shard_map/all_to_all | solution.py:372
  19.9 1.2 slice.41
  21.1 6.7 %collective-permute-start.1 = (f32[1024,128]{1,0:T(8,128)S(1)}, f32[1024,128]{1,0:T(8,128)S(1)}, u32[]{:S(2)}, u32[]{:S(2)}) collective-permute-start(f32[1024,128]{1,0:T(8,128)S(1)} %bitcast.38), channel_id=1, source_target_pairs={{0,192},{1,193},{2,194},{3,195},{4,196},{5,197},{6,198},{7,199},{8... | collective-permute-start | bytes 1572872 | tf_op jit(solution)/shard_map/ppermute | solution.py:325
  27.8 1.3 collective-permute-start
  29.1 9.8 %all-to-all-done = f32[16,9,8,256]{3,2,1,0:T(8,128)S(1)} async-done(((f32[16,9,8,256]{3,2,1,0:T(8,128)}), f32[16,9,8,256]{3,2,1,0:T(8,128)S(1)}, u32[]{:S(2)}, u32[]{:S(2)}) %all-to-all-start) | async-done | bytes 1179680 | tf_op jit(solution)/shard_map/all_to_all | solution.py:372
  39.4 1.3 collective-permute-done
  40.8 13.2 %all_to_all.40 = f32[8,2,8,256]{3,2,1,0:T(8,128)S(1)} all-to-all(f32[8,2,8,256]{3,2,1,0:T(8,128)S(1)} %broadcast_in_dim.10), channel_id=1, replica_groups=mesh['prow'=8,'pcol'=32] {'prow'}, dimensions={0} | all-to-all | bytes 262144 | tf_op jit(solution)/shard_map/all_to_all | solution.py:315
  54.8 6.0 %all-to-all-start.2 = ((f32[16,2,8,256]{3,2,1,0:T(8,128)}), f32[16,2,8,256]{3,2,1,0:T(8,128)S(1)}, u32[]{:S(2)}, u32[]{:S(2)}) async-start(f32[16,2,8,256]{3,2,1,0:T(8,128)} %broadcast_in_dim.11), calls=%async_computation.2 | async-start | bytes 524288 | tf_op jit(solution)/shard_map/all_to_all | solution.py:315
  60.8 7.4 %all-to-all-done.2.own_ref = f32[16,2,8,256]{3,2,1,0:T(8,128)S(1)} async-done(((f32[16,2,8,256]{3,2,1,0:T(8,128)}), f32[16,2,8,256]{3,2,1,0:T(8,128)S(1)}, u32[]{:S(2)}, u32[]{:S(2)}) %all-to-all-start.2) | async-done | bytes 262176 | tf_op jit(solution)/shard_map/all_to_all | solution.py:315
  68.2 3.6 %collective-permute-start.5 = (f32[16,2,8,256]{3,2,1,0:T(8,128)S(1)}, f32[16,2,8,256]{3,2,1,0:T(8,128)S(1)}, u32[]{:S(2)}, u32[]{:S(2)}) collective-permute-start(f32[16,2,8,256]{3,2,1,0:T(8,128)S(1)} %all-to-all-done.2.own_ref), channel_id=1, source_target_pairs={{0,1},{1,0},{2,3},{3,2},{4,5},{5,4},{6,7},{7,6},{8,9},{9,8},{10,11... | collective-permute-start | bytes 786440 | tf_op jit(solution)/shard_map/ppermute | solution.py:380
  71.8 1.5 collective-permute-start.4
  73.3 1.3 collective-permute-start.3
  74.6 1.1 broadcast_in_dim.12
  75.7 3.7 %all-to-all-start.3 = ((f32[16,8,8,256]{3,2,1,0:T(8,128)}), f32[16,8,8,256]{3,2,1,0:T(8,128)S(1)}, u32[]{:S(2)}, u32[]{:S(2)}) async-start(f32[16,8,8,256]{3,2,1,0:T(8,128)} %broadcast_in_dim.12), calls=%async_computation.3 | async-start | bytes 2097152 | tf_op jit(solution)/shard_map/all_to_all | solution.py:315
  79.4 10.5 %shard_map.18 = (f32[256,256]{1,0:T(8,128)S(1)}, f32[256,256]{1,0:T(8,128)S(1)}, f32[256,256]{1,0:T(8,128)S(1)}) custom-call(s32[6]{0:T(128)S(1)} %stack.63.at_ref, f32[16,2,8,256]{3,2,1,0:T(8,128)S(1)} %all-to-all-done.2.own_ref, f32[16,2,8,256]{3,2,1,0:T(8,128)S(1)} %collective-permute-done.5.other_ref), custom_call_target="tpu_custom_call" | custom-call | flops 10000000000 | bytes 1048576 | tf_op jit(solution)/shard_map/pallas_call | solution.py:382
  90.6 0.8 copy-done.12
  91.5 0.8 copy-done.14
  92.3 1.0 copy-done.13
  93.3 1.0 copy-done.15
  94.4 4.7 %shard_map.19 = (f32[16,8,8,256]{3,2,1,0:T(8,128)S(1)}, f32[16,8,8,256]{3,2,1,0:T(8,128)S(1)}, f32[256,512]{1,0:T(8,128)S(1)}) custom-call(s32[6]{0:T(128)S(1)} %stack.63.at_ref, f32[8192,128]{1,0:T(8,128)S(1)} %bitcast.35, f32[1024,128]{1,0:T(8,128)S(1)} %add_select_fusion.1.top_ref, f32[1024,128]{1,0:T(8,128)S(1)} %copy-done.15, ...), custom_call_target="tpu_custom_call" | custom-call | flops 3221225472 | bytes 9437184 | tf_op jit(solution)/shard_map/pallas_call | solution.py:390
  99.0 0.8 copy-done.5
  99.8 1.0 copy-done.11
  102.0 2.4 %collective-permute-done.6 = f32[16,8,8,256]{3,2,1,0:T(8,128)S(1)} collective-permute-done((f32[16,8,8,256]{3,2,1,0:T(8,128)}, f32[16,8,8,256]{3,2,1,0:T(8,128)S(1)}, u32[]{:S(2)}, u32[]{:S(2)}) %collective-permute-start.6) | collective-permute-done | bytes 1048608 | tf_op jit(solution)/shard_map/ppermute | solution.py:401
  104.4 1.1 add.44
  105.5 8.5 %all-to-all-start.4 = ((f32[16,8,8,256]{3,2,1,0:T(8,128)}), f32[16,8,8,256]{3,2,1,0:T(8,128)S(1)}, u32[]{:S(2)}, u32[]{:S(2)}) async-start(f32[16,8,8,256]{3,2,1,0:T(8,128)} %add.44), calls=%async_computation.4 | async-start | bytes 2097152 | tf_op jit(solution)/shard_map/all_to_all | solution.py:402
  114.0 6.2 %shard_map.20 = (f32[8,256,256]{2,1,0:T(8,128)S(1)}, f32[32,2048]{1,0:T(8,128)S(1)}) custom-call(s32[6]{0:T(128)S(1)} %stack.63.at_ref, f32[16,8,8,256]{3,2,1,0:T(8,128)S(1)} %all-to-all-done.3.own_ref, f32[16,8,8,256]{3,2,1,0:T(8,128)} %collective-permute-done.7.other_ref, f32[256,256]{1,0:T(8,128)S(1)} %copy-done.23), custom_call_target="tpu_custom_call" | custom-call | flops 5000000000 | bytes 6291456 | tf_op jit(solution)/shard_map/pallas_call | solution.py:404
  120.2 1.3 copy-done.3
  122.3 6.7 %all-to-all-done.4.after_ref = f32[16,8,8,256]{3,2,1,0:T(8,128)S(1)} async-done(((f32[16,8,8,256]{3,2,1,0:T(8,128)}), f32[16,8,8,256]{3,2,1,0:T(8,128)S(1)}, u32[]{:S(2)}, u32[]{:S(2)}) %all-to-all-start.4) | async-done | bytes 1048608 | tf_op jit(solution)/shard_map/all_to_all | solution.py:402
  129.1 1.1 broadcast_in_dim.13
  130.2 5.3 %all-to-all-start.5 = ((f32[16,8,8,256]{3,2,1,0:T(8,128)}), f32[16,8,8,256]{3,2,1,0:T(8,128)S(1)}, u32[]{:S(2)}, u32[]{:S(2)}) async-start(f32[16,8,8,256]{3,2,1,0:T(8,128)} %broadcast_in_dim.13), calls=%async_computation.5 | async-start | bytes 2097152 | tf_op jit(solution)/shard_map/all_to_all | solution.py:315
  135.5 12.8 %shard_map.21.mixer_ref = f32[256,256]{1,0:T(8,128)S(1)} custom-call(s32[6]{0:T(128)S(1)} %stack.63.at_ref, f32[16,2,8,256]{3,2,1,0:T(8,128)S(1)} %copy-done.10, f32[16,2,8,256]{3,2,1,0:T(8,128)S(1)} %copy-done.17, f32[256,256]{1,0:T(8,128)S(1)} %copy-done.21, f32[16,8,8,256]{3,2,1,0:T(8,128)S(1)} %all-to-all-done.4.after_ref), custom_call_target="tpu_custom_call" | custom-call | flops 10000000000 | bytes 1048576 | tf_op jit(solution)/shard_map/pallas_call | solution.py:416
  149.0 1.1 all-to-all-done.5.own_ref
  150.0 3.5 %collective-permute-start.8 = (f32[16,8,8,256]{3,2,1,0:T(8,128)S(1)}, f32[16,8,8,256]{3,2,1,0:T(8,128)S(1)}, u32[]{:S(2)}, u32[]{:S(2)}) collective-permute-start(f32[16,8,8,256]{3,2,1,0:T(8,128)S(1)} %all-to-all-done.5.own_ref), channel_id=1, source_target_pairs={{0,1},{1,0},{2,3},{3,2},{4,5},{5,4},{6,7},{7,6},{8,9},{9,8},{10,11... | collective-permute-start | bytes 3145736 | tf_op jit(solution)/shard_map/ppermute | solution.py:424
  153.5 2.3 %collective-permute-done.8.other_ref = f32[16,8,8,256]{3,2,1,0:T(8,128)S(1)} collective-permute-done((f32[16,8,8,256]{3,2,1,0:T(8,128)S(1)}, f32[16,8,8,256]{3,2,1,0:T(8,128)S(1)}, u32[]{:S(2)}, u32[]{:S(2)}) %collective-permute-start.8) | collective-permute-done | bytes 1048608 | tf_op jit(solution)/shard_map/ppermute | solution.py:424
  157.3 2.9 %shard_map.22 = f32[8,32,256]{2,1,0:T(8,128)S(1)} custom-call(s32[6]{0:T(128)S(1)} %stack.63.at_ref, f32[32,2048]{1,0:T(8,128)S(1)} %copy-done.19, f32[16,8,8,256]{3,2,1,0:T(8,128)S(1)} %all-to-all-done.5.own_ref, f32[16,8,8,256]{3,2,1,0:T(8,128)S(1)} %collective-permute-done.8.other_ref), custom_call_target="tpu_custom_call" | custom-call | flops 1000000000 | bytes 4194304 | tf_op jit(solution)/shard_map/pallas_call | solution.py:437
  160.3 12.3 %all_to_all.41 = f32[8,32,256]{2,1,0:T(8,128)} all-to-all(f32[8,32,256]{2,1,0:T(8,128)S(1)} %shard_map.22), channel_id=1, replica_groups=mesh['prow'=8,'pcol'=32] {'prow'}, dimensions={0} | all-to-all | bytes 524288 | tf_op jit(solution)/shard_map/all_to_all | solution.py:445
  172.7 1.3 collective-permute-start.12
  174.0 1.5 collective-permute-start.11
  175.5 1.0 reduce_sum.29
  176.5 17.8 %all_to_all.42 = f32[8,32,256]{2,1,0:T(8,128)S(1)} all-to-all(f32[8,32,256]{2,1,0:T(8,128)S(1)} %broadcast_in_dim.14), channel_id=1, replica_groups={{0,1,2,3,4,5,6,7},{8,9,10,11,12,13,14,15},{16,17,18,19,20,21,22,23},{24..., dimensions={0} | all-to-all | bytes 524288 | tf_op jit(solution)/shard_map/all_to_all | solution.py:315
  194.3 0.9 copy-done.8
  195.2 2.6 %shard_map.23 = (f32[256,512]{1,0:T(8,128)S(1)}, f32[256,512]{1,0:T(8,128)S(1)}) custom-call(s32[6]{0:T(128)S(1)} %stack.63.at_ref, f32[256,256]{1,0:T(8,128)S(1)} %copy-done.8, f32[256,512]{1,0:T(8,128)S(1)} %copy-done.6, f32[2,16,2,8,256]{4,3,2,1,0:T(8,128)S(1)} %add_select_fusion.near_ref, f32[2,16,2,8,256]{4,3,2,1,0:T(8,128)} %collective-permute-done.11.far_ref, ...), custom_call_target="tpu_custom_call" | custom-call | flops 3000000000 | bytes 1048576 | tf_op jit(solution)/shard_map/pallas_call | solution.py:451
  198.4 8.8 %shard_map.24 = f32[8192,128]{1,0:T(8,128)} custom-call(s32[6]{0:T(128)S(1)} %stack.63.at_ref, f32[8192,128]{1,0:T(8,128)S(1)} %bitcast.36, f32[8,256,256]{2,1,0:T(8,128)S(1)} %copy-done.4, f32[16,8,8,256]{3,2,1,0:T(8,128)S(1)} %all-to-all-done.5.own_ref, f32[16,8,8,256]{3,2,1,0:T(8,128)S(1)} %collective-permute-done.8.other_ref, f32[256,256]{1,0:T(8,128)S(1)} %bitcast.37, ...), custom_call_target="tpu_custom_call" | custom-call | flops 3221225472 | bytes 12582912 | tf_op jit(solution)/shard_map/pallas_call | solution.py:455
  (72 shorter events, 7.3 us)
Async XLA Ops:
  0.1 2.2 %copy-start = (f32[8,256,2,256]{3,2,1,0:T(2,128)S(1)}, f32[8,256,2,256]{3,2,1,0:T(2,128)}, u32[]{:S(2)}) copy-start(f32[8,256,2,256]{3,2,1,0:T(2,128)} %param.1) | copy-start | bytes 12582916
  6.7 7.0 %collective-permute-start.2 = (f32[16,9,8,256]{3,2,1,0:T(8,128)S(1)}, f32[16,9,8,256]{3,2,1,0:T(8,128)}, u32[]{:S(2)}, u32[]{:S(2)}) collective-permute-start(f32[16,9,8,256]{3,2,1,0:T(8,128)S(1)} %slice_bitcast_fusion), channel_id=1, source_target_pairs={{0,1},{32,33},{64,65},{96,97},{128,129},{160,161},{192,193},{224,2... | collective-permute-start | bytes 3538952 | tf_op jit(solution)/shard_map/ppermute | solution.py:371
  16.2 22.7 %all-to-all-start = ((f32[16,9,8,256]{3,2,1,0:T(8,128)}), f32[16,9,8,256]{3,2,1,0:T(8,128)S(1)}, u32[]{:S(2)}, u32[]{:S(2)}) async-start(f32[16,9,8,256]{3,2,1,0:T(8,128)} %fusion), calls=%async_computation | async-start | bytes 2359296 | tf_op jit(solution)/shard_map/all_to_all | solution.py:372
  21.1 18.3 %collective-permute-start.1 = (f32[1024,128]{1,0:T(8,128)S(1)}, f32[1024,128]{1,0:T(8,128)S(1)}, u32[]{:S(2)}, u32[]{:S(2)}) collective-permute-start(f32[1024,128]{1,0:T(8,128)S(1)} %bitcast.38), channel_id=1, source_target_pairs={{0,192},{1,193},{2,194},{3,195},{4,196},{5,197},{6,198},{7,199},{8... | collective-permute-start | bytes 1572872 | tf_op jit(solution)/shard_map/ppermute | solution.py:325
  27.8 13.0 %collective-permute-start = (f32[1024,128]{1,0:T(8,128)S(1)}, f32[1024,128]{1,0:T(8,128)S(1)}, u32[]{:S(2)}, u32[]{:S(2)}) collective-permute-start(f32[1024,128]{1,0:T(8,128)S(1)} %bitcast.39), channel_id=1, source_target_pairs={{0,96},{1,97},{2,98},{3,99},{4,100},{5,101},{6,102},{7,103},{8,104... | collective-permute-start | bytes 1572872 | tf_op jit(solution)/shard_map/ppermute | solution.py:325
  54.8 13.4 %all-to-all-start.2 = ((f32[16,2,8,256]{3,2,1,0:T(8,128)}), f32[16,2,8,256]{3,2,1,0:T(8,128)S(1)}, u32[]{:S(2)}, u32[]{:S(2)}) async-start(f32[16,2,8,256]{3,2,1,0:T(8,128)} %broadcast_in_dim.11), calls=%async_computation.2 | async-start | bytes 524288 | tf_op jit(solution)/shard_map/all_to_all | solution.py:315
  68.2 11.2 %copy-start.9 = (f32[16,2,8,256]{3,2,1,0:T(8,128)}, f32[16,2,8,256]{3,2,1,0:T(8,128)S(1)}, u32[]{:S(2)}) copy-start(f32[16,2,8,256]{3,2,1,0:T(8,128)S(1)} %all-to-all-done.2.own_ref) | copy-start | bytes 786436
  68.2 11.2 %collective-permute-start.5 = (f32[16,2,8,256]{3,2,1,0:T(8,128)S(1)}, f32[16,2,8,256]{3,2,1,0:T(8,128)S(1)}, u32[]{:S(2)}, u32[]{:S(2)}) collective-permute-start(f32[16,2,8,256]{3,2,1,0:T(8,128)S(1)} %all-to-all-done.2.own_ref), channel_id=1, source_target_pairs={{0,1},{1,0},{2,3},{3,2},{4,5},{5,4},{6,7},{7,6},{8,9},{9,8},{10,11... | collective-permute-start | bytes 786440 | tf_op jit(solution)/shard_map/ppermute | solution.py:380
  71.8 18.9 %collective-permute-start.4 = (f32[1024,128]{1,0:T(8,128)S(1)}, f32[1024,128]{1,0:T(8,128)S(1)}, u32[]{:S(2)}, u32[]{:S(2)}) collective-permute-start(f32[1024,128]{1,0:T(8,128)S(1)} %add_select_fusion.1.top_ref), channel_id=1, source_target_pairs={{0,224},{96,64},{192,160},{1,225},{97,65},{193,161},{2,226},{98,66... | collective-permute-start | bytes 1572872 | tf_op jit(solution)/shard_map/ppermute | solution.py:325
  73.3 18.2 %collective-permute-start.3 = (f32[1024,128]{1,0:T(8,128)S(1)}, f32[1024,128]{1,0:T(8,128)S(1)}, u32[]{:S(2)}, u32[]{:S(2)}) collective-permute-start(f32[1024,128]{1,0:T(8,128)S(1)} %add_select_fusion.1.top_ref), channel_id=1, source_target_pairs={{0,32},{96,128},{1,33},{97,129},{2,34},{98,130},{3,35},{99,131},{4... | collective-permute-start | bytes 1572872 | tf_op jit(solution)/shard_map/ppermute | solution.py:325
  75.7 25.8 %all-to-all-start.3 = ((f32[16,8,8,256]{3,2,1,0:T(8,128)}), f32[16,8,8,256]{3,2,1,0:T(8,128)S(1)}, u32[]{:S(2)}, u32[]{:S(2)}) async-start(f32[16,8,8,256]{3,2,1,0:T(8,128)} %broadcast_in_dim.12), calls=%async_computation.3 | async-start | bytes 2097152 | tf_op jit(solution)/shard_map/all_to_all | solution.py:315
  79.4 12.9 %copy-start.1 = (f32[8,256,2,256]{3,2,1,0:T(2,128)S(1)}, f32[8,256,2,256]{3,2,1,0:T(2,128)}, u32[]{:S(2)}) copy-start(f32[8,256,2,256]{3,2,1,0:T(2,128)} %param.1) | copy-start | bytes 12582916
  79.4 10.5 %copy-start.16 = (f32[16,2,8,256]{3,2,1,0:T(8,128)}, f32[16,2,8,256]{3,2,1,0:T(8,128)S(1)}, u32[]{:S(2)}) copy-start(f32[16,2,8,256]{3,2,1,0:T(8,128)S(1)} %collective-permute-done.5.other_ref) | copy-start | bytes 786436
  89.9 0.7 copy-start.22
  90.6 0.8 copy-start.12
  91.5 0.8 copy-start.14
  92.3 1.0 copy-start.13
  93.3 1.0 copy-start.15
  99.0 0.8 copy-start.5
  99.8 1.0 copy-start.11
  100.8 0.7 copy-start.20
  101.5 2.9 %collective-permute-start.6 = (f32[16,8,8,256]{3,2,1,0:T(8,128)}, f32[16,8,8,256]{3,2,1,0:T(8,128)S(1)}, u32[]{:S(2)}, u32[]{:S(2)}) collective-permute-start(f32[16,8,8,256]{3,2,1,0:T(8,128)} %copy-done.11), channel_id=1, source_target_pairs={{0,1},{1,0},{2,3},{3,2},{4,5},{5,4},{6,7},{7,6},{8,9},{9,8},{10,11... | collective-permute-start | bytes 3145736 | tf_op jit(solution)/shard_map/ppermute | solution.py:401
  101.8 12.2 %collective-permute-start.7 = (f32[16,8,8,256]{3,2,1,0:T(8,128)S(1)}, f32[16,8,8,256]{3,2,1,0:T(8,128)}, u32[]{:S(2)}, u32[]{:S(2)}) collective-permute-start(f32[16,8,8,256]{3,2,1,0:T(8,128)S(1)} %all-to-all-done.3.own_ref), channel_id=1, source_target_pairs={{0,1},{1,0},{2,3},{3,2},{4,5},{5,4},{6,7},{7,6},{8,9},{9,8},{10,11... | collective-permute-start | bytes 3145736 | tf_op jit(solution)/shard_map/ppermute | solution.py:400
  105.5 8.5 %copy-start.23 = (f32[256,256]{1,0:T(8,128)S(1)}, f32[256,256]{1,0:T(8,128)}, u32[]{:S(2)}) copy-start(f32[256,256]{1,0:T(8,128)} %copy-done.22) | copy-start | bytes 786436
  105.5 23.5 %all-to-all-start.4 = ((f32[16,8,8,256]{3,2,1,0:T(8,128)}), f32[16,8,8,256]{3,2,1,0:T(8,128)S(1)}, u32[]{:S(2)}, u32[]{:S(2)}) async-start(f32[16,8,8,256]{3,2,1,0:T(8,128)} %add.44), calls=%async_computation.4 | async-start | bytes 2097152 | tf_op jit(solution)/shard_map/all_to_all | solution.py:402
  120.2 1.3 copy-start.3
  121.6 0.7 copy-start.18
  130.2 5.3 %copy-start.10 = (f32[16,2,8,256]{3,2,1,0:T(8,128)S(1)}, f32[16,2,8,256]{3,2,1,0:T(8,128)}, u32[]{:S(2)}) copy-start(f32[16,2,8,256]{3,2,1,0:T(8,128)} %copy-done.9) | copy-start | bytes 786436
  130.2 5.3 %copy-start.17 = (f32[16,2,8,256]{3,2,1,0:T(8,128)S(1)}, f32[16,2,8,256]{3,2,1,0:T(8,128)}, u32[]{:S(2)}) copy-start(f32[16,2,8,256]{3,2,1,0:T(8,128)} %copy-done.16) | copy-start | bytes 786436
  130.2 5.3 %copy-start.21 = (f32[256,256]{1,0:T(8,128)S(1)}, f32[256,256]{1,0:T(8,128)}, u32[]{:S(2)}) copy-start(f32[256,256]{1,0:T(8,128)} %copy-done.20) | copy-start | bytes 786436
  130.2 19.9 %all-to-all-start.5 = ((f32[16,8,8,256]{3,2,1,0:T(8,128)}), f32[16,8,8,256]{3,2,1,0:T(8,128)S(1)}, u32[]{:S(2)}, u32[]{:S(2)}) async-start(f32[16,8,8,256]{3,2,1,0:T(8,128)} %broadcast_in_dim.13), calls=%async_computation.5 | async-start | bytes 2097152 | tf_op jit(solution)/shard_map/all_to_all | solution.py:315
  148.3 0.7 copy-start.7
  150.0 5.7 %collective-permute-start.8 = (f32[16,8,8,256]{3,2,1,0:T(8,128)S(1)}, f32[16,8,8,256]{3,2,1,0:T(8,128)S(1)}, u32[]{:S(2)}, u32[]{:S(2)}) collective-permute-start(f32[16,8,8,256]{3,2,1,0:T(8,128)S(1)} %all-to-all-done.5.own_ref), channel_id=1, source_target_pairs={{0,1},{1,0},{2,3},{3,2},{4,5},{5,4},{6,7},{7,6},{8,9},{9,8},{10,11... | collective-permute-start | bytes 3145736 | tf_op jit(solution)/shard_map/ppermute | solution.py:424
  155.8 1.5 copy-start.19
  155.9 16.6 %collective-permute-start.10 = (f32[2,16,2,8,256]{4,3,2,1,0:T(8,128)S(1)}, f32[2,16,2,8,256]{4,3,2,1,0:T(8,128)S(1)}, u32[]{:S(2)}, u32[]{:S(2)}) collective-permute-start(f32[2,16,2,8,256]{4,3,2,1,0:T(8,128)S(1)} %pad_maximum_fusion), channel_id=1, source_target_pairs={{0,192},{33,225},{66,2},{99,35},{132,68},{165,101},{198,134},{231,... | collective-permute-start | bytes 1572872 | tf_op jit(solution)/shard_map/ppermute | solution.py:325
  156.6 15.9 %collective-permute-start.9 = (f32[2,16,2,8,256]{4,3,2,1,0:T(8,128)S(1)}, f32[2,16,2,8,256]{4,3,2,1,0:T(8,128)S(1)}, u32[]{:S(2)}, u32[]{:S(2)}) collective-permute-start(f32[2,16,2,8,256]{4,3,2,1,0:T(8,128)S(1)} %pad_maximum_fusion), channel_id=1, source_target_pairs={{0,96},{33,129},{66,162},{99,195},{132,228},{165,5},{198,38},{231,... | collective-permute-start | bytes 1572872 | tf_op jit(solution)/shard_map/ppermute | solution.py:325
  172.5 21.7 %copy-start.6 = (f32[256,512]{1,0:T(8,128)S(1)}, f32[256,512]{1,0:T(8,128)}, u32[]{:S(2)}) copy-start(f32[256,512]{1,0:T(8,128)} %copy-done.5) | copy-start | bytes 1572868
  172.7 21.6 %collective-permute-start.12 = (f32[2,16,2,8,256]{4,3,2,1,0:T(8,128)S(1)}, f32[2,16,2,8,256]{4,3,2,1,0:T(8,128)}, u32[]{:S(2)}, u32[]{:S(2)}) collective-permute-start(f32[2,16,2,8,256]{4,3,2,1,0:T(8,128)S(1)} %add_select_fusion.near_ref), channel_id=1, source_target_pairs={{0,224},{96,64},{192,160},{33,1},{129,97},{225,193},{66,34},{162,1... | collective-permute-start | bytes 1572872 | tf_op jit(solution)/shard_map/ppermute | solution.py:325
  174.0 20.3 %collective-permute-start.11 = (f32[2,16,2,8,256]{4,3,2,1,0:T(8,128)S(1)}, f32[2,16,2,8,256]{4,3,2,1,0:T(8,128)}, u32[]{:S(2)}, u32[]{:S(2)}) collective-permute-start(f32[2,16,2,8,256]{4,3,2,1,0:T(8,128)S(1)} %add_select_fusion.near_ref), channel_id=1, source_target_pairs={{0,32},{96,128},{33,65},{129,161},{66,98},{162,194},{99,131},{195,... | collective-permute-start | bytes 1572872 | tf_op jit(solution)/shard_map/ppermute | solution.py:325
  194.3 1.0 copy-start.8
  195.2 2.6 %copy-start.2 = (f32[8,256,2,256]{3,2,1,0:T(2,128)S(1)}, f32[8,256,2,256]{3,2,1,0:T(2,128)}, u32[]{:S(2)}) copy-start(f32[8,256,2,256]{3,2,1,0:T(2,128)} %param.1) | copy-start | bytes 12582916
  195.2 3.2 %copy-start.4 = (f32[8,256,256]{2,1,0:T(8,128)S(1)}, f32[8,256,256]{2,1,0:T(8,128)}, u32[]{:S(2)}) copy-start(f32[8,256,256]{2,1,0:T(8,128)} %copy-done.3) | copy-start | bytes 6291460

commit v4 on v3

--- a/solution.py
+++ b/solution.py
@@ -13,11 +13,10 @@
 BASE = 64
 GROUP = 8
 PLANE = [[q * CORES + k for q in range(CHIPS)] for k in range(CORES)]
-LINE = YS * CORES
-LINES = [[x * LINE + j for j in range(LINE)] for x in range(XS)]
 SWAP = [(i, i ^ 1) for i in range(CHIPS * CORES)]
 VMEM = pl.BlockSpec(memory_space=pltpu.VMEM)
 SMEM = pl.BlockSpec(memory_space=pltpu.SMEM)
+HBM = pl.BlockSpec(memory_space=pltpu.HBM)
 
 
 def mm(a, b):
@@ -104,16 +103,18 @@
     return jnp.concatenate([top, jnp.concatenate([-mm(s, y), s], 1)], 0)
 
 
-def split(a):
+def halves(a):
     high = a.astype(jnp.bfloat16)
     return high, (a - high.astype(jnp.float32)).astype(jnp.bfloat16)
 
 
-def dot3(a, b, dims):
-    one = functools.partial(
-        lax.dot_general, dimension_numbers=(dims, ((), ())), preferred_element_type=jnp.float32
-    )
-    return one(a[0], b[0]) + (one(a[0], b[1]) + one(a[1], b[0]))
+def thrice(a, left):
+    high, low = halves(a)
+    return jnp.concatenate([high, low, high] if left else [high, high, low], axis=1 if left else 0)
+
+
+def mm3(left, right):
+    return jnp.dot(left, right, preferred_element_type=jnp.float32)
 
 
 def identity(n):
@@ -125,6 +126,21 @@
     return ref[pl.ds(t * nm + m, ref.shape[0] // (nm * nt), stride=nm * nt), :]
 
 
+def fetched(step, x_ref, held_ref, sems):
+    rows = held_ref.shape[1]
+    copy = lambda i: pltpu.make_async_copy(
+        x_ref.at[pl.ds(pl.multiple_of(i * rows, rows), rows)], held_ref.at[i], sems.at[i]
+    )
+
+    @pl.when(step == 0)
+    def _():
+        for i in range(held_ref.shape[0]):
+            copy(i).start()
+
+    copy(step).wait()
+    return held_ref.at[step]
+
+
 def in_order(at_ref, own, other):
     first = at_ref[2] == 0
     return jnp.concatenate([jnp.where(first, own, other), jnp.where(first, other, own)], axis=0)
@@ -134,8 +150,9 @@
     return ref[...].reshape(-1, ref.shape[-1])
 
 
-def pack_kernel(nm, nt, at_ref, x_ref, packet_ref, gram_ref):
+def pack_kernel(nm, nt, at_ref, x_ref, packet_ref, gram_ref, held_ref, sems):
     step = pl.program_id(0)
+    x_ref = fetched(step, x_ref, held_ref, sems)
     panel = jnp.concatenate([tile(x_ref, 0, t, nm, nt) for t in range(nt)], axis=1)
     panel = jnp.where((step == 0) & (at_ref[0] == 0), 0.0, panel)
     last = packet_ref.shape[2] - 1
@@ -177,7 +194,8 @@
 
 
 def apply_kernel(
-    nm, nt, at_ref, x_ref, top_ref, far_ref, more_ref, inv_ref, keep_ref, send_ref, y_ref, high_ref, low_ref
+    nm, nt, at_ref, x_ref, top_ref, far_ref, more_ref, inv_ref, keep_ref, send_ref, y_ref,
+    right_ref,
 ):
     step = pl.program_id(0)
     nb = inv_ref.shape[0]
@@ -202,17 +220,17 @@
             if m == 0:
                 y += jnp.where(at_ref[1] == 1, identity(nb), 0.0)
             y_ref[:, m * nb : (m + 1) * nb] = y
-            high_ref[m * nb : (m + 1) * nb], low_ref[m * nb : (m + 1) * nb] = split(y.T)
+        right_ref[...] = thrice(y_ref[...].T, False)
 
     block = jnp.concatenate(
         [tile(x_ref, m, t, nm, nt) for m in range(nm) for t in range(nt)], axis=1
     )
-    part = dot3(split(block), (high_ref[...], low_ref[...]), ((1,), (0,)))
+    part = mm3(thrice(block, True), right_ref[...])
     part = jnp.where((step == 0) & (at_ref[0] == 0), 0.0, part)
     first = at_ref[2] == 0
     hb = nb // CORES
-    keep_ref[...] = jnp.where(first, part[:hb], part[hb:]).reshape(keep_ref.shape)
-    send_ref[...] = jnp.where(first, part[hb:], part[:hb]).reshape(send_ref.shape)
+    keep_ref[0] = jnp.where(first, part[:hb], part[hb:])
+    send_ref[0] = jnp.where(first, part[hb:], part[:hb])
 
 
 def proj_kernel(at_ref, slab_ref, own_ref, other_ref, copies_ref):
@@ -233,24 +251,52 @@
             copies_ref[i] = copies_ref[0]
 
 
-def sides_kernel(at_ref, mixer_ref, y_ref, near_ref, far_ref, more_ref, z_ref, v_ref):
+def route_kernel(nm, at_ref, four_ref, more_ref, pieces_ref, out_ref):
+    nz, sub, nb = pieces_ref.shape
+    total = jnp.sum(pieces_ref[...], axis=0)
+    deep = four_ref.shape[1] // nm
+    for z in range(nz):
+        bits = z ^ at_ref[0]
+        place = (bits & 2) | ((bits >> 2) & 1)
+
+        def put(ref):
+            for m in range(nm):
+                for i in range(deep):
+                    out_ref[i * nz + z, m] = ref[place, m * deep + i]
+
+        @pl.when((bits & 1) == 0)
+        def _():
+            put(four_ref)
+
+        @pl.when((bits & 1) == 1)
+        def _():
+            put(more_ref)
+
+    for i in range(out_ref.shape[0]):
+        out_ref[i, nm] = total
+
+
+def sides_kernel(mixer_ref, y_ref, rows_ref, z_ref, v_ref, proj_ref):
     mixer = mixer_ref[...]
     nb = mixer.shape[0]
-    for m in range(y_ref.shape[1] // nb):
-        halves = [
-            jnp.where(at_ref[5] == 1, near_ref[h, :, m], far_ref[h, :, m] + more_ref[h, :, m])
-            for h in range(CORES)
-        ]
-        ay = in_order(at_ref, *[half.reshape(nb // CORES, nb) for half in halves])
+    nm = y_ref.shape[1] // nb
+
+    def gathered(m):
+        return jnp.concatenate(
+            [rows_ref[:, k, m].reshape(nb // CORES, nb) for k in range(CORES)], axis=0
+        )
+
+    for m in range(nm):
         z_ref[:, m * nb : (m + 1) * nb] = lax.dot_general(
-            mixer, ay, (((0,), (1,)), ((), ())), precision=HP, preferred_element_type=jnp.float32
+            mixer, gathered(m), (((0,), (1,)), ((), ())), precision=HP, preferred_element_type=jnp.float32
         )
     v_ref[...] = mm(mixer, y_ref[...])
+    proj_ref[...] = gathered(nm)
 
 
 def update_kernel(
     nm, nt, at_ref, x_ref, left_ref, own_ref, other_ref, proj_ref,
-    mixer_ref, y_ref, z_ref, v_ref, upper_ref, out_ref, high_ref, low_ref,
+    mixer_ref, y_ref, z_ref, v_ref, upper_ref, out_ref, right_ref,
 ):
     step = pl.program_id(0)
     nb = mixer_ref.shape[0]
@@ -259,15 +305,11 @@
     def _():
         mixer = mixer_ref[...]
         core = mm(mm_tn(mixer, proj_ref[...]), mixer)
-        w = split(z_ref[...] - mm_tn(core, y_ref[...]))
-        v = split(v_ref[...])
-        for i, ref in enumerate((high_ref, low_ref)):
-            ref[:nb] = w[i]
-            ref[nb:] = v[i]
+        w = z_ref[...] - mm_tn(core, y_ref[...])
+        right_ref[...] = thrice(jnp.concatenate([w, v_ref[...]], axis=0), False)
 
     ay = in_order(at_ref, rows_of(own_ref), rows_of(other_ref))
-    left = split(jnp.concatenate([left_ref[0], ay], axis=1))
-    change = dot3(left, (high_ref[...], low_ref[...]), ((1,), (0,)))
+    change = mm3(thrice(jnp.concatenate([left_ref[0], ay], axis=1), True), right_ref[...])
     rows = nb
     for m in range(nm):
         for t in range(nt):
@@ -297,11 +339,11 @@
                 out_ref[pl.ds(t * nm + m, rows, stride=nm * nt), :] = new
 
 
-def call(kernel, outs, ins, grid=(), flops=0, moved=1 << 20, scratch=()):
+def call(kernel, outs, ins, grid=(), flops=0, moved=1 << 20, scratch=(), out=jax.ShapeDtypeStruct):
     return pl.pallas_call(
         kernel,
         grid=grid,
-        out_shape=[jax.ShapeDtypeStruct(s, jnp.float32) for s, _ in outs],
+        out_shape=[out(s, jnp.float32) for s, _ in outs],
         in_specs=ins,
         out_specs=[spec for _, spec in outs],
         scratch_shapes=list(scratch),
@@ -315,22 +357,20 @@
     return lax.all_to_all(copies, axis, 0, 0, axis_index_groups=groups)
 
 
-def move(block, root, nz, hops):
-    lines = CHIPS * CORES
-    pairs = [
-        ((root(c) + i) % nz * lines + c, (root(c) + j) % nz * lines + c)
-        for c in range(lines)
-        for i, j in hops
-    ]
-    return lax.ppermute(block, ("prow", "pcol"), pairs)
-
-
-def near_moves(block, root, nz):
-    return move(block, root, nz, [(0, 3)]), move(block, root, nz, [(0, 6)])
-
-
-def far_moves(block, root, nz):
-    return move(block, root, nz, [(0, 1), (3, 4)]), move(block, root, nz, [(0, 7), (3, 2), (6, 5)])
+def move(block, hops):
+    return lax.ppermute(block, "prow", hops)
+
+
+def near_moves(block):
+    return move(block, [(0, 3)]), move(block, [(0, 6)])
+
+
+def far_moves(block):
+    return move(block, [(0, 1), (3, 4)]), move(block, [(0, 7), (3, 2), (6, 5)])
+
+
+def doubled(block, reach, nz):
+    return jnp.concatenate([block, move(block, [(i, i ^ reach) for i in range(nz)])])
 
 
 def body(hamiltonian):
@@ -342,9 +382,8 @@
     core = pcol % CORES
     sub = nb // (CHIPS * CORES)
     nc = nm * nb
-    away = (prow + nz - pcol % nz) % nz
-    relay = lambda d: (d == 0) | (d == 3) | (d == 6)
-    at = jnp.stack([prow, pcol, core, pcol % LINE, relay(prow), relay(away)]).astype(jnp.int32)
+    relay = (prow == 0) | (prow == 3) | (prow == 6)
+    at = jnp.stack([prow, pcol, core, core * CHIPS + pcol // CORES, relay]).astype(jnp.int32)
     square, wide = (nb, nb), (nb, nc)
     whole = lambda shape: pl.BlockSpec(shape, lambda l: (0,) * len(shape))
     chunk = lambda index: pl.BlockSpec((CHIPS, 1, sub, nb), index)
@@ -355,56 +394,60 @@
     x_rows = nb * nt * nm
     x_spec = pl.BlockSpec((x_rows, LANES), lambda l: (l, 0))
 
-    root = lambda c: 0
-    near = near_moves(x[:x_rows], root, nz)
+    first_rows = x[:x_rows]
 
     packet_shape = (CORES, CHIPS, nl + 1, sub, nb)
     packet = call(
         functools.partial(pack_kernel, nm, nt),
         [(packet_shape, whole(packet_shape))],
-        [SMEM, x_spec],
+        [SMEM, HBM],
         grid=(nl,),
         flops=2 * 10**10,
         moved=6 << 20,
-        scratch=[pltpu.VMEM(square, jnp.float32)],
-    )(at, x)[0]
+        scratch=[
+            pltpu.VMEM(square, jnp.float32),
+            pltpu.VMEM((nl, x_rows, LANES), jnp.float32),
+            pltpu.SemaphoreType.DMA((nl,)),
+        ],
+    )(at, pltpu.with_memory_space_constraint(x, pltpu.HBM))[0]
     outgoing = jnp.where(core == 0, packet[0], lax.ppermute(packet[1], "pcol", [(0, 1)]))
+    near = near_moves(first_rows)
     mine = lax.all_to_all(outgoing, "pcol", 0, 0, axis_index_groups=PLANE)[0]
     near, mine = barrier((near, mine))
-    p_cols = jnp.where(prow == 0, x[:x_rows], near[0] + near[1])
+    p_cols = jnp.where(prow == 0, first_rows, near[0] + near[1])
     stacked = share(jnp.stack([mine[nl], mine[0]]), "prow", nz)
     summed = jnp.stack([jnp.sum(stacked[:, 0], axis=0), stacked[1, 1]])
     small = share(summed, "pcol", CHIPS, PLANE)
     p_cols, small, mine = barrier((p_cols, small, mine))
-    far = far_moves(p_cols, root, nz)
+    far = far_moves(p_cols)
     other_small = lax.ppermute(small, "pcol", SWAP)
     gram_spec = chunk(lambda l: (0, 0, 0, 0))
     upper, inv, inv_t = call(
         factor_kernel, [(square, VMEM)] * 3, [SMEM, gram_spec, gram_spec], grid=(1,), flops=10**10
     )(at, small, other_small)
     own_p = share(mine[:nl], "pcol", CHIPS, PLANE)
-    far, inv, inv_t = barrier((far, inv, inv_t))
-
-    half_shape = (CHIPS, nl, sub, nb)
+
+    half_shape = (nl, nb // CORES, nb)
+    half_spec = pl.BlockSpec((1,) + half_shape[1:], lambda l: (l, 0, 0))
     row_spec = chunk(lambda l: (0, l, 0, 0))
     keep, send, y_cols = call(
         functools.partial(apply_kernel, nm, nt),
-        [(half_shape, row_spec), (half_shape, row_spec), (wide, whole(wide))],
+        [(half_shape, half_spec), (half_shape, half_spec), (wide, whole(wide))],
         [SMEM, x_spec] + [whole((x_rows, LANES))] * 3 + [whole(square)],
         grid=(nl,),
         flops=12 * nl * nb**2 * nc,
         moved=9 << 20,
-        scratch=[pltpu.VMEM((nc, nb), jnp.bfloat16)] * 2,
-    )(at, x, p_cols, *far, inv)
+        scratch=[pltpu.VMEM((3 * nc, nb), jnp.bfloat16)],
+        out=pltpu.HBM,
+    )(at, x, *[pltpu.with_memory_space_constraint(a, pltpu.HBM) for a in (p_cols, *far)], inv)
     keep, send, own_p = barrier((keep, send, own_p))
     other_p = lax.ppermute(own_p, "pcol", SWAP)
-    parts = keep + lax.ppermute(send, "pcol", SWAP)
+    parts = (keep + lax.ppermute(send, "pcol", SWAP)).reshape(nl, CHIPS, sub, nb).transpose(1, 0, 2, 3)
     parts = lax.all_to_all(parts, "pcol", 0, 0, axis_index_groups=PLANE)
-    slab_rows = nb // LINE
     y_rows, slab = call(
         rows_kernel,
         [((nl, nb, nb), pl.BlockSpec((1, nb, nb), lambda l: (l, 0, 0))),
-         ((slab_rows, nl * nb), pl.BlockSpec((slab_rows, nb), lambda l: (0, l)))],
+         ((sub, nl * nb), pl.BlockSpec((sub, nb), lambda l: (0, l)))],
         [SMEM, row_spec, row_spec, whole(square)],
         grid=(nl,),
         flops=5 * 10**9,
@@ -412,7 +455,8 @@
         scratch=[pltpu.VMEM(square, jnp.float32)],
     )(at, own_p, other_p, inv_t)
     parts, y_rows, slab = barrier((parts, y_rows, slab))
-    own = share(jnp.sum(parts, axis=0), "pcol", CHIPS, PLANE)
+    piece = jnp.sum(parts, axis=0)
+    own = share(piece, "pcol", CHIPS, PLANE)
     mixer = call(
         mixer_kernel,
         [(square, VMEM)],
@@ -420,37 +464,32 @@
         grid=(1,),
         flops=10**10,
     )(at, small, other_small, inv, parts)[0]
-    own, mixer = barrier((own, mixer))
+    four = doubled(doubled(piece[None], 4, nz), 2, nz)
+    own, mixer, four = barrier((own, mixer, four))
     other = lax.ppermute(own, "pcol", SWAP)
-
-    picked = jnp.stack(
-        [
-            jnp.stack(
-                [lax.dynamic_index_in_dim(a, m * XS + pcol // nz, 1, keepdims=False) for m in range(nm)], 1
-            )
-            for a in (own, other)
-        ]
-    )
-    root = lambda c: c % nz
-    near = near_moves(picked, root, nz)
 
     copies = call(
         proj_kernel,
-        [((nz, slab_rows, nb), whole((nz, slab_rows, nb)))],
-        [SMEM, pl.BlockSpec((slab_rows, nb), lambda l: (0, l)), row_spec, row_spec],
+        [((nz, sub, nb), whole((nz, sub, nb)))],
+        [SMEM, pl.BlockSpec((sub, nb), lambda l: (0, l)), row_spec, row_spec],
         grid=(nl,),
         flops=10**9,
         moved=4 << 20,
     )(at, slab, own, other)[0]
     pieces = lax.all_to_all(copies, "prow", 0, 0)
-    near, pieces = barrier((near, pieces))
-    ay_cols = jnp.where(away == 0, picked, near[0] + near[1])
-    far = far_moves(ay_cols, root, nz)
-    proj = share(jnp.sum(pieces, axis=0), "pcol", LINE, LINES).reshape(square)
-    far, proj = barrier((far, proj))
-    z_cols, v_cols = call(sides_kernel, [(wide, VMEM)] * 2, [SMEM] + [VMEM] * 5, flops=3 * 10**9)(
-        at, mixer, y_cols, ay_cols, *far
-    )
+    more = move(four, [(i, i ^ 1) for i in range(nz)])
+    more, pieces = barrier((more, pieces))
+    lines = CHIPS * CORES
+    routed = call(
+        functools.partial(route_kernel, nm),
+        [((lines, nm + 1, sub, nb), VMEM)],
+        [SMEM] + [VMEM] * 3,
+        flops=10**8,
+    )(at, four, more, pieces)[0]
+    routed = lax.all_to_all(routed, "pcol", 0, 0)
+    z_cols, v_cols, proj = call(
+        sides_kernel, [(wide, VMEM), (wide, VMEM), (square, VMEM)], [VMEM] * 3, flops=3 * 10**9
+    )(mixer, y_cols, routed.reshape(CHIPS, CORES, nm + 1, sub, nb))
 
     out = call(
         functools.partial(update_kernel, nm, nt),
@@ -460,7 +499,7 @@
         grid=(nl,),
         flops=12 * nl * nb**2 * nc,
         moved=12 << 20,
-        scratch=[pltpu.VMEM((2 * nb, nc), jnp.bfloat16)] * 2,
+        scratch=[pltpu.VMEM((6 * nb, nc), jnp.bfloat16)],
     )(at, x, y_rows, own, other, proj, mixer, y_cols, z_cols, v_cols, upper)[0]
     out = out.reshape(nl, nb, nt, nm, LANES).transpose(0, 1, 3, 2, 4)
     return out.reshape(hamiltonian.shape)

time: 208 us -> 205 us (0.986)
  local copies, waits for them, and re-layouts: 17.8 us -> 8.78 us
  blocking collectives: 43.3 us -> 35 us
  waiting for transfers between devices: 37.1 us -> 43.2 us
  Pallas kernels: 52.8 us -> 56.3 us
  starting transfers between devices: 50.9 us -> 54.1 us
    all_to_all x2 -> x1, blocking collectives: 31 us -> 13.2 us  [share(): return lax.all_to_all(copies, axis, 0, 0, axis_index_groups=groups)]
    all_to_all x1, blocking collectives: 12.3 us -> 21.8 us  [body(): routed = lax.all_to_all(routed, 'pcol', 0, 0)]
    unnamed x48 -> x20, local copies, waits for them, and re-layouts: 13.4 us -> 4.5 us
    all_to_all x0 -> x1, waiting for transfers between devices: none -> 7.22 us  [body(): pieces = lax.all_to_all(copies, 'prow', 0, 0)]
    all_to_all x0 -> x1, starting transfers between devices: none -> 4.74 us  [body(): pieces = lax.all_to_all(copies, 'prow', 0, 0)]
    transpose x0 -> x1, other arithmetic: none -> 2.39 us  [body(): (keep + lax.ppermute(send, 'pcol', SWAP)).reshape(nl, CHIPS, sub, nb)]
    pallas_call x3 -> x4, Pallas kernels: 10.2 us -> 12.5 us  [the longest x1 7.06 us: body(): call(functools.partial(apply_kernel, nm, nt), [(half_shape, half_spec), (...]
    all_to_all x3, waiting for transfers between devices: 8.43 us -> 6.25 us  [share(): return lax.all_to_all(copies, axis, 0, 0, axis_index_groups=groups)]
  transfers between devices with their start and end apart: 18 -> 18, of which waited for: 9 -> 10; matrix products, arithmetic and copies ran while one was open for 2% -> 3% of each run, Pallas kernels for 18% -> 19%
where the time goes in v4:
time: 205 us; the launch traced here: 204 us
  Pallas kernels  56.3 us (27%)
  starting transfers between devices  54.1 us (26%)
  waiting for transfers between devices  43.2 us (21%)
  blocking collectives  35 us (17%)
  local copies, waits for them, and re-layouts  8.78 us (4%)
  other arithmetic  6.16 us (3%)
    all_to_all x1, blocking collectives, body(): routed = lax.all_to_all(routed, 'pcol', 0, 0)  21.8 us
    all_to_all x3, starting transfers between devices, share(): return lax.all_to_all(copies, axis, 0, 0, axis_index_groups=groups)  14.8 us
    ppermute x7, starting transfers between devices, move(): return lax.ppermute(block, 'prow', hops)  13.8 us
    all_to_all x1, blocking collectives, share(): return lax.all_to_all(copies, axis, 0, 0, axis_index_groups=groups)  13.2 us
    pallas_call x1, Pallas kernels, body(): call(mixer_kernel, [(square, VMEM)], [SMEM] + [chunk(lambda l: (0, 1, 0,...  12.8 us
    pallas_call x1, Pallas kernels, body(): call(factor_kernel, [(square, VMEM)] * 3, [SMEM, gram_spec, gram_spec], g...  10.5 us
    all_to_all x1, waiting for transfers between devices, body(): mine = lax.all_to_all(outgoing, 'pcol', 0, 0, axis_index_groups=PLANE)[0]  9.78 us
    pallas_call x1, Pallas kernels, body(): call(functools.partial(update_kernel, nm, nt), [(x.shape, x_spec)], [SMEM...  8.87 us
  transfers between devices with their start and end apart: 18, of which 10 were waited for; matrix products, arithmetic and copies ran while one was open for 3% of the time, Pallas kernels for 19%

profile of v4, /device:TPU:1, one launch (start us, length us, event | category | flops | bytes accessed | tf_op | source)
XLA Modules:
  0.0 203.9 jit_solution(10501238633550218937)
XLA Ops:
  0.1 5.5 %shard_map.17 = f32[2,16,9,8,256]{4,3,2,1,0:T(8,128)S(1)} custom-call(s32[5]{0:T(128)S(1)} %stack.36.at_ref, f32[8192,128]{1,0:T(8,128)} %bitcast.34), custom_call_target="tpu_custom_call" | custom-call | flops 20000000000 | bytes 6291456 | tf_op jit(solution)/shard_map/pallas_call | solution.py:400
  5.7 1.3 collective-permute-start.2
  7.0 5.7 %collective-permute-done.2 = f32[16,9,8,256]{3,2,1,0:T(8,128)} collective-permute-done((f32[16,9,8,256]{3,2,1,0:T(8,128)S(1)}, f32[16,9,8,256]{3,2,1,0:T(8,128)}, u32[]{:S(2)}, u32[]{:S(2)}) %collective-permute-start.2) | collective-permute-done | bytes 1179680 | tf_op jit(solution)/shard_map/ppermute | solution.py:413
  12.7 2.5 %fusion = f32[16,9,8,256]{3,2,1,0:T(8,128)} fusion(f32[16,9,8,256]{3,2,1,0:T(8,128)} %collective-permute-done.2, f32[2,16,9,8,256]{4,3,2,1,0:T(8,128)S(1)} %shard_map.17, pred[]{:T(512)S(6)} %eq.18), kind=kLoop, calls=%fused_computation.2 | loop fusion | flops 294912 | bytes 3538945 | tf_op jit(solution)/shard_map/jit(_where)/select_n | solution.py:413
  15.2 3.7 %all-to-all-start = ((f32[16,9,8,256]{3,2,1,0:T(8,128)}), f32[16,9,8,256]{3,2,1,0:T(8,128)S(1)}, u32[]{:S(2)}, u32[]{:S(2)}) async-start(f32[16,9,8,256]{3,2,1,0:T(8,128)} %fusion), calls=%async_computation | async-start | bytes 2359296 | tf_op jit(solution)/shard_map/all_to_all | solution.py:415
  18.9 1.2 slice.40
  20.1 6.7 %collective-permute-start.1 = (f32[1024,128]{1,0:T(8,128)S(1)}, f32[1024,128]{1,0:T(8,128)S(1)}, u32[]{:S(2)}, u32[]{:S(2)}) collective-permute-start(f32[1024,128]{1,0:T(8,128)S(1)} %bitcast.39), channel_id=1, source_target_pairs={{0,192},{1,193},{2,194},{3,195},{4,196},{5,197},{6,198},{7,199},{8... | collective-permute-start | bytes 1572872 | tf_op jit(solution)/shard_map/ppermute | solution.py:361
  26.8 1.3 collective-permute-start
  28.1 9.8 %all-to-all-done = f32[16,9,8,256]{3,2,1,0:T(8,128)S(1)} async-done(((f32[16,9,8,256]{3,2,1,0:T(8,128)}), f32[16,9,8,256]{3,2,1,0:T(8,128)S(1)}, u32[]{:S(2)}, u32[]{:S(2)}) %all-to-all-start) | async-done | bytes 1179680 | tf_op jit(solution)/shard_map/all_to_all | solution.py:415
  37.9 0.5 collective-permute-done.1
  38.4 1.3 collective-permute-done
  39.8 13.2 %all_to_all.40 = f32[8,2,8,256]{3,2,1,0:T(8,128)S(1)} all-to-all(f32[8,2,8,256]{3,2,1,0:T(8,128)S(1)} %broadcast_in_dim.10), channel_id=1, replica_groups=mesh['prow'=8,'pcol'=32] {'prow'}, dimensions={0} | all-to-all | bytes 262144 | tf_op jit(solution)/shard_map/all_to_all | solution.py:357
  53.0 0.7 broadcast_in_dim.11
  53.7 6.0 %all-to-all-start.2 = ((f32[16,2,8,256]{3,2,1,0:T(8,128)}), f32[16,2,8,256]{3,2,1,0:T(8,128)S(1)}, u32[]{:S(2)}, u32[]{:S(2)}) async-start(f32[16,2,8,256]{3,2,1,0:T(8,128)} %broadcast_in_dim.11), calls=%async_computation.2 | async-start | bytes 524288 | tf_op jit(solution)/shard_map/all_to_all | solution.py:357
  59.7 1.2 add_select_fusion.top_ref
  60.9 6.2 %all-to-all-done.2.own_ref = f32[16,2,8,256]{3,2,1,0:T(8,128)S(1)} async-done(((f32[16,2,8,256]{3,2,1,0:T(8,128)}), f32[16,2,8,256]{3,2,1,0:T(8,128)S(1)}, u32[]{:S(2)}, u32[]{:S(2)}) %all-to-all-start.2) | async-done | bytes 262176 | tf_op jit(solution)/shard_map/all_to_all | solution.py:357
  67.2 3.6 %collective-permute-start.5 = (f32[16,2,8,256]{3,2,1,0:T(8,128)S(1)}, f32[16,2,8,256]{3,2,1,0:T(8,128)S(1)}, u32[]{:S(2)}, u32[]{:S(2)}) collective-permute-start(f32[16,2,8,256]{3,2,1,0:T(8,128)S(1)} %all-to-all-done.2.own_ref), channel_id=1, source_target_pairs={{0,1},{1,0},{2,3},{3,2},{4,5},{5,4},{6,7},{7,6},{8,9},{9,8},{10,11... | collective-permute-start | bytes 786440 | tf_op jit(solution)/shard_map/ppermute | solution.py:423
  70.8 1.5 collective-permute-start.4
  72.3 2.1 %collective-permute-start.3 = (f32[1024,128]{1,0:T(8,128)S(1)}, f32[1024,128]{1,0:T(8,128)}, u32[]{:S(2)}, u32[]{:S(2)}) collective-permute-start(f32[1024,128]{1,0:T(8,128)S(1)} %add_select_fusion.top_ref), channel_id=1, source_target_pairs={{0,32},{96,128},{1,33},{97,129},{2,34},{98,130},{3,35},{99,131},{4... | collective-permute-start | bytes 1572872 | tf_op jit(solution)/shard_map/ppermute | solution.py:361
  74.4 1.1 broadcast_in_dim.12
  75.4 3.7 %all-to-all-start.3 = ((f32[16,8,8,256]{3,2,1,0:T(8,128)}), f32[16,8,8,256]{3,2,1,0:T(8,128)S(1)}, u32[]{:S(2)}, u32[]{:S(2)}) async-start(f32[16,8,8,256]{3,2,1,0:T(8,128)} %broadcast_in_dim.12), calls=%async_computation.3 | async-start | bytes 2097152 | tf_op jit(solution)/shard_map/all_to_all | solution.py:357
  79.1 10.5 %shard_map.18 = (f32[256,256]{1,0:T(8,128)S(1)}, f32[256,256]{1,0:T(8,128)S(1)}, f32[256,256]{1,0:T(8,128)S(1)}) custom-call(s32[5]{0:T(128)S(1)} %stack.36.at_ref, f32[16,2,8,256]{3,2,1,0:T(8,128)S(1)} %all-to-all-done.2.own_ref, f32[16,2,8,256]{3,2,1,0:T(8,128)S(1)} %collective-permute-done.5.other_ref), custom_call_target="tpu_custom_call" | custom-call | flops 10000000000 | bytes 1048576 | tf_op jit(solution)/shard_map/pallas_call | solution.py:425
  89.6 0.8 copy-done.9
  90.4 7.1 %shard_map.19 = (f32[8,128,256]{2,1,0:T(8,128)}, f32[8,128,256]{2,1,0:T(8,128)}, f32[256,512]{1,0:T(8,128)}) custom-call(s32[5]{0:T(128)S(1)} %stack.36.at_ref, f32[8192,128]{1,0:T(8,128)S(1)} %bitcast.36, f32[1024,128]{1,0:T(8,128)} %copy-done.5, f32[1024,128]{1,0:T(8,128)} %collective-permute-done.3.far_ref, f32[1024,128]{1,0:T(8,128)} %copy-done.9, ...), custom_call_target="tpu_custom_call" | custom-call | flops 3221225472 | bytes 9437184 | tf_op jit(solution)/shard_map/pallas_call | solution.py:433
  98.0 2.4 %collective-permute-done.6 = f32[8,128,256]{2,1,0:T(8,128)S(1)} collective-permute-done((f32[8,128,256]{2,1,0:T(8,128)}, f32[8,128,256]{2,1,0:T(8,128)S(1)}, u32[]{:S(2)}, u32[]{:S(2)}) %collective-permute-start.6) | collective-permute-done | bytes 1048608 | tf_op jit(solution)/shard_map/ppermute | solution.py:445
  100.4 2.4 %copy_bitcast_fusion = f32[16,8,8,256]{3,2,1,0:T(8,128)} fusion(f32[8,128,256]{2,1,0:T(8,128)} %get-tuple-element.42, f32[8,128,256]{2,1,0:T(8,128)S(1)} %collective-permute-done.6), kind=kLoop, calls=%fused_computation.3 | loop fusion | flops 262144 | bytes 3145728 | tf_op jit(solution)/shard_map/transpose | solution.py:445
  102.8 7.4 %all-to-all-start.4 = ((f32[16,8,8,256]{3,2,1,0:T(8,128)}), f32[16,8,8,256]{3,2,1,0:T(8,128)S(1)}, u32[]{:S(2)}, u32[]{:S(2)}) async-start(f32[16,8,8,256]{3,2,1,0:T(8,128)} %copy_bitcast_fusion), calls=%async_computation.4 | async-start | bytes 2097152 | tf_op jit(solution)/shard_map/all_to_all | solution.py:446
  110.2 6.2 %shard_map.20 = (f32[8,256,256]{2,1,0:T(8,128)S(1)}, f32[8,2048]{1,0:T(8,128)S(1)}) custom-call(s32[5]{0:T(128)S(1)} %stack.36.at_ref, f32[16,8,8,256]{3,2,1,0:T(8,128)S(1)} %all-to-all-done.3.own_ref, f32[16,8,8,256]{3,2,1,0:T(8,128)} %collective-permute-done.7.other_ref, f32[256,256]{1,0:T(8,128)S(1)} %get-tuple-element.45.inv_t_ref), custom_call_target="tpu_custom_call" | custom-call | flops 5000000000 | bytes 6291456 | tf_op jit(solution)/shard_map/pallas_call | solution.py:447
  116.4 1.3 copy-done.2
  117.7 7.5 %all-to-all-done.4.after_ref = f32[16,8,8,256]{3,2,1,0:T(8,128)S(1)} async-done(((f32[16,8,8,256]{3,2,1,0:T(8,128)}), f32[16,8,8,256]{3,2,1,0:T(8,128)S(1)}, u32[]{:S(2)}, u32[]{:S(2)}) %all-to-all-start.4) | async-done | bytes 1048608 | tf_op jit(solution)/shard_map/all_to_all | solution.py:446
  125.5 1.1 broadcast_in_dim.13
  126.6 5.1 %all-to-all-start.5 = ((f32[16,8,8,256]{3,2,1,0:T(8,128)}), f32[16,8,8,256]{3,2,1,0:T(8,128)S(1)}, u32[]{:S(2)}, u32[]{:S(2)}) async-start(f32[16,8,8,256]{3,2,1,0:T(8,128)} %broadcast_in_dim.13), calls=%async_computation.5 | async-start | bytes 2097152 | tf_op jit(solution)/shard_map/all_to_all | solution.py:357
  131.7 1.5 collective-permute-done.8
  133.3 0.6 copy-done.7
  133.9 0.7 collective-permute-start.9
  134.6 12.8 %shard_map.21.mixer_ref = f32[256,256]{1,0:T(8,128)S(1)} custom-call(s32[5]{0:T(128)S(1)} %stack.36.at_ref, f32[16,2,8,256]{3,2,1,0:T(8,128)S(1)} %all-to-all-done.2.own_ref, f32[16,2,8,256]{3,2,1,0:T(8,128)S(1)} %collective-permute-done.5.other_ref, f32[256,256]{1,0:T(8,128)S(1)} %get-tuple-element.38.inv_ref, f32[16,8,8,256]{3,2,1,0:T(8,128)S(1)} %all-to-all-done.4.after_ref), custom_call_target="tpu_custom_call" | custom-call | flops 10000000000 | bytes 1048576 | tf_op jit(solution)/shard_map/pallas_call | solution.py:460
  147.4 4.3 %collective-permute-start.10 = (f32[16,8,8,256]{3,2,1,0:T(8,128)S(1)}, f32[16,8,8,256]{3,2,1,0:T(8,128)S(1)}, u32[]{:S(2)}, u32[]{:S(2)}) collective-permute-start(f32[16,8,8,256]{3,2,1,0:T(8,128)S(1)} %all-to-all-done.5.own_ref), channel_id=1, source_target_pairs={{0,1},{1,0},{2,3},{3,2},{4,5},{5,4},{6,7},{7,6},{8,9},{9,8},{10,11... | collective-permute-start | bytes 3145736 | tf_op jit(solution)/shard_map/ppermute | solution.py:469
  151.7 1.3 collective-permute-start.11
  152.9 1.0 collective-permute-done.10.other_ref
  154.0 3.2 %shard_map.22 = f32[8,8,256]{2,1,0:T(8,128)} custom-call(s32[5]{0:T(128)S(1)} %stack.36.at_ref, f32[8,2048]{1,0:T(8,128)S(1)} %get-tuple-element.54.slab_ref, f32[16,8,8,256]{3,2,1,0:T(8,128)S(1)} %all-to-all-done.5.own_ref, f32[16,8,8,256]{3,2,1,0:T(8,128)S(1)} %collective-permute-done.10.other_ref), custom_call_target="tpu_custom_call" | custom-call | flops 1000000000 | bytes 4194304 | tf_op jit(solution)/shard_map/pallas_call | solution.py:471
  157.2 4.7 %all-to-all-start.6 = ((f32[8,8,256]{2,1,0:T(8,128)}), f32[8,8,256]{2,1,0:T(8,128)S(1)}, u32[]{:S(2)}, u32[]{:S(2)}) async-start(f32[8,8,256]{2,1,0:T(8,128)} %shard_map.22), calls=%async_computation.6 | async-start | bytes 131072 | tf_op jit(solution)/shard_map/all_to_all | solution.py:479
  161.9 7.2 %all-to-all-done.6.pieces_ref = f32[8,8,256]{2,1,0:T(8,128)S(1)} async-done(((f32[8,8,256]{2,1,0:T(8,128)}), f32[8,8,256]{2,1,0:T(8,128)S(1)}, u32[]{:S(2)}, u32[]{:S(2)}) %all-to-all-start.6) | async-done | bytes 65568 | tf_op jit(solution)/shard_map/all_to_all | solution.py:479
  169.2 1.1 shard_map.23
  170.3 21.8 %all_to_all.41 = f32[32,3,8,256]{3,2,1,0:T(8,128)S(1)} all-to-all(f32[32,3,8,256]{3,2,1,0:T(8,128)S(1)} %shard_map.23), channel_id=1, replica_groups=mesh['prow'=8,'pcol'=32] {'pcol'}, dimensions={0} | all-to-all | bytes 1572864 | tf_op jit(solution)/shard_map/all_to_all | solution.py:489
  192.1 1.1 shard_map.24
  193.2 1.1 copy-done.1
  194.3 0.7 copy-done.3
  195.0 8.9 %shard_map.25 = f32[8192,128]{1,0:T(8,128)} custom-call(s32[5]{0:T(128)S(1)} %stack.36.at_ref, f32[8192,128]{1,0:T(8,128)S(1)} %bitcast.37, f32[8,256,256]{2,1,0:T(8,128)S(1)} %copy-done.3, f32[16,8,8,256]{3,2,1,0:T(8,128)S(1)} %all-to-all-done.5.own_ref, f32[16,8,8,256]{3,2,1,0:T(8,128)S(1)} %collective-permute-done.10.other_ref, ...), custom_call_target="tpu_custom_call" | custom-call | flops 3221225472 | bytes 12582912 | tf_op jit(solution)/shard_map/pallas_call | solution.py:494
  (39 shorter events, 1.2 us)
Async XLA Ops:
  5.7 7.0 %collective-permute-start.2 = (f32[16,9,8,256]{3,2,1,0:T(8,128)S(1)}, f32[16,9,8,256]{3,2,1,0:T(8,128)}, u32[]{:S(2)}, u32[]{:S(2)}) collective-permute-start(f32[16,9,8,256]{3,2,1,0:T(8,128)S(1)} %slice_bitcast_fusion), channel_id=1, source_target_pairs={{0,1},{32,33},{64,65},{96,97},{128,129},{160,161},{192,193},{224,2... | collective-permute-start | bytes 3538952 | tf_op jit(solution)/shard_map/ppermute | solution.py:413
  15.2 22.7 %all-to-all-start = ((f32[16,9,8,256]{3,2,1,0:T(8,128)}), f32[16,9,8,256]{3,2,1,0:T(8,128)S(1)}, u32[]{:S(2)}, u32[]{:S(2)}) async-start(f32[16,9,8,256]{3,2,1,0:T(8,128)} %fusion), calls=%async_computation | async-start | bytes 2359296 | tf_op jit(solution)/shard_map/all_to_all | solution.py:415
  20.1 18.3 %collective-permute-start.1 = (f32[1024,128]{1,0:T(8,128)S(1)}, f32[1024,128]{1,0:T(8,128)S(1)}, u32[]{:S(2)}, u32[]{:S(2)}) collective-permute-start(f32[1024,128]{1,0:T(8,128)S(1)} %bitcast.39), channel_id=1, source_target_pairs={{0,192},{1,193},{2,194},{3,195},{4,196},{5,197},{6,198},{7,199},{8... | collective-permute-start | bytes 1572872 | tf_op jit(solution)/shard_map/ppermute | solution.py:361
  26.8 13.0 %collective-permute-start = (f32[1024,128]{1,0:T(8,128)S(1)}, f32[1024,128]{1,0:T(8,128)S(1)}, u32[]{:S(2)}, u32[]{:S(2)}) collective-permute-start(f32[1024,128]{1,0:T(8,128)S(1)} %bitcast.40), channel_id=1, source_target_pairs={{0,96},{1,97},{2,98},{3,99},{4,100},{5,101},{6,102},{7,103},{8,104... | collective-permute-start | bytes 1572872 | tf_op jit(solution)/shard_map/ppermute | solution.py:361
  39.8 14.0 %copy-start.6 = (f32[1024,128]{1,0:T(8,128)}, f32[1024,128]{1,0:T(8,128)S(1)}, u32[]{:S(2)}) copy-start(f32[1024,128]{1,0:T(8,128)S(1)} %collective-permute-done) | copy-start | bytes 1572868
  53.7 13.4 %all-to-all-start.2 = ((f32[16,2,8,256]{3,2,1,0:T(8,128)}), f32[16,2,8,256]{3,2,1,0:T(8,128)S(1)}, u32[]{:S(2)}, u32[]{:S(2)}) async-start(f32[16,2,8,256]{3,2,1,0:T(8,128)} %broadcast_in_dim.11), calls=%async_computation.2 | async-start | bytes 524288 | tf_op jit(solution)/shard_map/all_to_all | solution.py:357
  60.9 14.5 %copy-start.5 = (f32[1024,128]{1,0:T(8,128)}, f32[1024,128]{1,0:T(8,128)S(1)}, u32[]{:S(2)}) copy-start(f32[1024,128]{1,0:T(8,128)S(1)} %add_select_fusion.top_ref) | copy-start | bytes 1572868
  67.2 11.9 %collective-permute-start.5 = (f32[16,2,8,256]{3,2,1,0:T(8,128)S(1)}, f32[16,2,8,256]{3,2,1,0:T(8,128)S(1)}, u32[]{:S(2)}, u32[]{:S(2)}) collective-permute-start(f32[16,2,8,256]{3,2,1,0:T(8,128)S(1)} %all-to-all-done.2.own_ref), channel_id=1, source_target_pairs={{0,1},{1,0},{2,3},{3,2},{4,5},{5,4},{6,7},{7,6},{8,9},{9,8},{10,11... | collective-permute-start | bytes 786440 | tf_op jit(solution)/shard_map/ppermute | solution.py:423
  70.8 18.8 %collective-permute-start.4 = (f32[1024,128]{1,0:T(8,128)S(1)}, f32[1024,128]{1,0:T(8,128)S(1)}, u32[]{:S(2)}, u32[]{:S(2)}) collective-permute-start(f32[1024,128]{1,0:T(8,128)S(1)} %add_select_fusion.top_ref), channel_id=1, source_target_pairs={{0,224},{96,64},{192,160},{1,225},{97,65},{193,161},{2,226},{98,66... | collective-permute-start | bytes 1572872 | tf_op jit(solution)/shard_map/ppermute | solution.py:361
  72.3 17.4 %collective-permute-start.3 = (f32[1024,128]{1,0:T(8,128)S(1)}, f32[1024,128]{1,0:T(8,128)}, u32[]{:S(2)}, u32[]{:S(2)}) collective-permute-start(f32[1024,128]{1,0:T(8,128)S(1)} %add_select_fusion.top_ref), channel_id=1, source_target_pairs={{0,32},{96,128},{1,33},{97,129},{2,34},{98,130},{3,35},{99,131},{4... | collective-permute-start | bytes 1572872 | tf_op jit(solution)/shard_map/ppermute | solution.py:361
  75.4 22.0 %all-to-all-start.3 = ((f32[16,8,8,256]{3,2,1,0:T(8,128)}), f32[16,8,8,256]{3,2,1,0:T(8,128)S(1)}, u32[]{:S(2)}, u32[]{:S(2)}) async-start(f32[16,8,8,256]{3,2,1,0:T(8,128)} %broadcast_in_dim.12), calls=%async_computation.3 | async-start | bytes 2097152 | tf_op jit(solution)/shard_map/all_to_all | solution.py:357
  79.1 11.3 %copy-start = (f32[8,256,2,256]{3,2,1,0:T(2,128)S(1)}, f32[8,256,2,256]{3,2,1,0:T(2,128)}, u32[]{:S(2)}) copy-start(f32[8,256,2,256]{3,2,1,0:T(2,128)} %param.1) | copy-start | bytes 12582916
  89.6 0.8 copy-start.9
  97.5 2.9 %collective-permute-start.6 = (f32[8,128,256]{2,1,0:T(8,128)}, f32[8,128,256]{2,1,0:T(8,128)S(1)}, u32[]{:S(2)}, u32[]{:S(2)}) collective-permute-start(f32[8,128,256]{2,1,0:T(8,128)} %get-tuple-element.43), channel_id=1, source_target_pairs={{0,1},{1,0},{2,3},{3,2},{4,5},{5,4},{6,7},{7,6},{8,9},{9,8},{10,11... | collective-permute-start | bytes 3145736 | tf_op jit(solution)/shard_map/ppermute | solution.py:445
  97.8 12.3 %collective-permute-start.7 = (f32[16,8,8,256]{3,2,1,0:T(8,128)S(1)}, f32[16,8,8,256]{3,2,1,0:T(8,128)}, u32[]{:S(2)}, u32[]{:S(2)}) collective-permute-start(f32[16,8,8,256]{3,2,1,0:T(8,128)S(1)} %all-to-all-done.3.own_ref), channel_id=1, source_target_pairs={{0,1},{1,0},{2,3},{3,2},{4,5},{5,4},{6,7},{7,6},{8,9},{9,8},{10,11... | collective-permute-start | bytes 3145736 | tf_op jit(solution)/shard_map/ppermute | solution.py:444
  102.8 22.4 %all-to-all-start.4 = ((f32[16,8,8,256]{3,2,1,0:T(8,128)}), f32[16,8,8,256]{3,2,1,0:T(8,128)S(1)}, u32[]{:S(2)}, u32[]{:S(2)}) async-start(f32[16,8,8,256]{3,2,1,0:T(8,128)} %copy_bitcast_fusion), calls=%async_computation.4 | async-start | bytes 2097152 | tf_op jit(solution)/shard_map/all_to_all | solution.py:446
  116.3 1.3 copy-start.2
  125.2 8.0 %collective-permute-start.8 = (f32[1,8,8,256]{3,2,1,0:T(8,128)S(1)}, f32[1,8,8,256]{3,2,1,0:T(8,128)S(1)}, u32[]{:S(2)}, u32[]{:S(2)}) collective-permute-start(f32[1,8,8,256]{3,2,1,0:T(8,128)S(1)} %bitcast.42), channel_id=1, source_target_pairs={{0,128},{32,160},{64,192},{96,224},{128,0},{160,32},{192,64},{224,... | collective-permute-start | bytes 196616 | tf_op jit(solution)/shard_map/ppermute | solution.py:361
  126.6 20.8 %all-to-all-start.5 = ((f32[16,8,8,256]{3,2,1,0:T(8,128)}), f32[16,8,8,256]{3,2,1,0:T(8,128)S(1)}, u32[]{:S(2)}, u32[]{:S(2)}) async-start(f32[16,8,8,256]{3,2,1,0:T(8,128)} %broadcast_in_dim.13), calls=%async_computation.5 | async-start | bytes 2097152 | tf_op jit(solution)/shard_map/all_to_all | solution.py:357
  133.2 0.6 copy-start.7
  133.9 13.5 %collective-permute-start.9 = (f32[2,8,8,256]{3,2,1,0:T(8,128)S(1)}, f32[2,8,8,256]{3,2,1,0:T(8,128)S(1)}, u32[]{:S(2)}, u32[]{:S(2)}) collective-permute-start(f32[2,8,8,256]{3,2,1,0:T(8,128)S(1)} %pad_maximum_fusion.1), channel_id=1, source_target_pairs={{0,64},{32,96},{64,0},{96,32},{128,192},{160,224},{192,128},{224,1... | collective-permute-start | bytes 393224 | tf_op jit(solution)/shard_map/ppermute | solution.py:361
  134.6 12.8 %copy-start.8 = (f32[1,8,8,256]{3,2,1,0:T(8,128)S(1)}, f32[1,8,8,256]{3,2,1,0:T(8,128)}, u32[]{:S(2)}) copy-start(f32[1,8,8,256]{3,2,1,0:T(8,128)} %copy-done.7) | copy-start | bytes 196612
  147.4 6.5 %collective-permute-start.10 = (f32[16,8,8,256]{3,2,1,0:T(8,128)S(1)}, f32[16,8,8,256]{3,2,1,0:T(8,128)S(1)}, u32[]{:S(2)}, u32[]{:S(2)}) collective-permute-start(f32[16,8,8,256]{3,2,1,0:T(8,128)S(1)} %all-to-all-done.5.own_ref), channel_id=1, source_target_pairs={{0,1},{1,0},{2,3},{3,2},{4,5},{5,4},{6,7},{7,6},{8,9},{9,8},{10,11... | collective-permute-start | bytes 3145736 | tf_op jit(solution)/shard_map/ppermute | solution.py:469
  151.7 10.2 %collective-permute-start.11 = (f32[4,8,8,256]{3,2,1,0:T(8,128)S(1)}, f32[4,8,8,256]{3,2,1,0:T(8,128)}, u32[]{:S(2)}, u32[]{:S(2)}) collective-permute-start(f32[4,8,8,256]{3,2,1,0:T(8,128)S(1)} %pad_maximum_fusion.four_ref), channel_id=1, source_target_pairs={{0,32},{32,0},{64,96},{96,64},{128,160},{160,128},{192,224},{224,1... | collective-permute-start | bytes 786440 | tf_op jit(solution)/shard_map/ppermute | solution.py:361
  157.2 12.0 %all-to-all-start.6 = ((f32[8,8,256]{2,1,0:T(8,128)}), f32[8,8,256]{2,1,0:T(8,128)S(1)}, u32[]{:S(2)}, u32[]{:S(2)}) async-start(f32[8,8,256]{2,1,0:T(8,128)} %shard_map.22), calls=%async_computation.6 | async-start | bytes 131072 | tf_op jit(solution)/shard_map/all_to_all | solution.py:479
  161.9 30.2 %copy-start.4 = (f32[256,512]{1,0:T(8,128)S(1)}, f32[256,512]{1,0:T(8,128)}, u32[]{:S(2)}) copy-start(f32[256,512]{1,0:T(8,128)} %get-tuple-element.52.y_ref) | copy-start | bytes 1572868
  192.1 2.2 %copy-start.1 = (f32[8,256,2,256]{3,2,1,0:T(2,128)S(1)}, f32[8,256,2,256]{3,2,1,0:T(2,128)}, u32[]{:S(2)}) copy-start(f32[8,256,2,256]{3,2,1,0:T(2,128)} %param.1) | copy-start | bytes 12582916
  192.1 2.9 %copy-start.3 = (f32[8,256,256]{2,1,0:T(8,128)S(1)}, f32[8,256,256]{2,1,0:T(8,128)}, u32[]{:S(2)}) copy-start(f32[8,256,256]{2,1,0:T(8,128)} %copy-done.2) | copy-start | bytes 6291460

commit v5 on v4

--- a/solution.py
+++ b/solution.py
@@ -172,11 +172,23 @@
         packet_ref[:, :, last] = gram_ref[...].reshape(CORES, CHIPS, *packet_ref.shape[3:])
 
 
-def factor_kernel(at_ref, own_ref, other_ref, upper_ref, inv_ref, inv_t_ref):
+def factor_kernel(
+    at_ref, own_ref, other_ref, inv_ref, upper_hbm, inv_hbm, inv_t_hbm, upper_ref, inv_t_ref, sems
+):
     upper, inv = factor(in_order(at_ref, rows_of(own_ref), rows_of(other_ref)))
     upper_ref[...] = upper
     inv_ref[...] = inv
     inv_t_ref[...] = inv.T
+    stores = [
+        pltpu.make_async_copy(src, dst, sems.at[i])
+        for i, (src, dst) in enumerate(
+            ((upper_ref, upper_hbm), (inv_ref, inv_hbm), (inv_t_ref, inv_t_hbm))
+        )
+    ]
+    for store in stores:
+        store.start()
+    for store in stores:
+        store.wait()
 
 
 def mixer_kernel(at_ref, own_ref, other_ref, inv_ref, after_ref, mixer_ref):
@@ -194,61 +206,102 @@
 
 
 def apply_kernel(
-    nm, nt, at_ref, x_ref, top_ref, far_ref, more_ref, inv_ref, keep_ref, send_ref, y_ref,
-    right_ref,
+    nm, nt, at_ref, x_ref, top_hbm, far_hbm, more_hbm, inv_ref, keep_ref, send_hbm, y_hbm,
+    top_ref, far_ref, more_ref, y_ref, send_ref, in_sems, out_sem, send_sems,
 ):
-    step = pl.program_id(0)
-    nb = inv_ref.shape[0]
-
-    @pl.when(step == 0)
-    def _():
-        for m in range(nm):
-            panel = jnp.concatenate(
-                [
-                    jnp.where(
-                        at_ref[4] == 1,
-                        tile(top_ref, m, t, nm, nt),
-                        tile(far_ref, m, t, nm, nt) + tile(more_ref, m, t, nm, nt),
-                    )
-                    for t in range(nt)
-                ],
-                axis=1,
+    nl, hb, nb = keep_ref.shape
+    rows = nb * nt * nm
+    loads = [
+        pltpu.make_async_copy(src, dst, in_sems.at[i])
+        for i, (src, dst) in enumerate(
+            ((top_hbm, top_ref), (far_hbm, far_ref), (more_hbm, more_ref))
+        )
+    ]
+    for load in loads:
+        load.start()
+    for load in loads:
+        load.wait()
+    for m in range(nm):
+        panel = jnp.concatenate(
+            [
+                jnp.where(
+                    at_ref[4] == 1,
+                    tile(top_ref, m, t, nm, nt),
+                    tile(far_ref, m, t, nm, nt) + tile(more_ref, m, t, nm, nt),
+                )
+                for t in range(nt)
+            ],
+            axis=1,
+        )
+        if m == 0:
+            panel = jnp.where(at_ref[1] == 0, 0.0, panel)
+        y = mm(inv_ref[...], panel)
+        if m == 0:
+            y += jnp.where(at_ref[1] == 1, identity(nb), 0.0)
+        y_ref[:, m * nb : (m + 1) * nb] = y
+    store = pltpu.make_async_copy(y_ref, y_hbm, out_sem)
+    store.start()
+    right = thrice(y_ref[...].T, False)
+    first = at_ref[2] == 0
+    send = lambda step: pltpu.make_async_copy(send_ref.at[step], send_hbm.at[step], send_sems.at[step])
+
+    @pl.loop(0, nl // 2)
+    def _(pair):
+        blocks = []
+        for i in range(2):
+            step = pair * 2 + i
+            rows_ref = x_ref.at[pl.ds(pl.multiple_of(step * rows, rows), rows)]
+            blocks.append(
+                jnp.concatenate(
+                    [tile(rows_ref, m, t, nm, nt) for m in range(nm) for t in range(nt)], axis=1
+                )
             )
-            if m == 0:
-                panel = jnp.where(at_ref[1] == 0, 0.0, panel)
-            y = mm(inv_ref[...], panel)
-            if m == 0:
-                y += jnp.where(at_ref[1] == 1, identity(nb), 0.0)
-            y_ref[:, m * nb : (m + 1) * nb] = y
-        right_ref[...] = thrice(y_ref[...].T, False)
-
-    block = jnp.concatenate(
-        [tile(x_ref, m, t, nm, nt) for m in range(nm) for t in range(nt)], axis=1
+        both = mm3(thrice(jnp.concatenate(blocks, axis=0), True), right)
+        for i in range(2):
+            step = pair * 2 + i
+            part = both[i * nb : (i + 1) * nb]
+            if i == 0:
+                part = jnp.where((pair == 0) & (at_ref[0] == 0), 0.0, part)
+            keep_ref[step] = jnp.where(first, part[:hb], part[hb:])
+            send_ref[step] = jnp.where(first, part[hb:], part[:hb])
+            send(step).start()
+
+    for step in range(nl):
+        send(step).wait()
+    store.wait()
+
+
+def half_loads(pair, own_hbm, other_hbm, own_ref, other_ref, own_sems, other_sems):
+    two = pl.ds(pair * 2, 2)
+    return (
+        pltpu.make_async_copy(own_hbm.at[:, two], own_ref.at[:, two], own_sems.at[pair]),
+        pltpu.make_async_copy(other_hbm.at[:, two], other_ref.at[:, two], other_sems.at[pair]),
     )
-    part = mm3(thrice(block, True), right_ref[...])
-    part = jnp.where((step == 0) & (at_ref[0] == 0), 0.0, part)
-    first = at_ref[2] == 0
-    hb = nb // CORES
-    keep_ref[0] = jnp.where(first, part[:hb], part[hb:])
-    send_ref[0] = jnp.where(first, part[hb:], part[:hb])
-
-
-def proj_kernel(at_ref, slab_ref, own_ref, other_ref, copies_ref):
-    step = pl.program_id(0)
-    more = mm(slab_ref[...], in_order(at_ref, rows_of(own_ref), rows_of(other_ref)))
-
-    @pl.when(step == 0)
-    def _():
-        copies_ref[0] = more
-
-    @pl.when(step > 0)
-    def _():
-        copies_ref[0] += more
-
-    @pl.when(step == pl.num_programs(0) - 1)
-    def _():
-        for i in range(1, copies_ref.shape[0]):
-            copies_ref[i] = copies_ref[0]
+
+
+def proj_kernel(
+    at_ref, slab_ref, own_hbm, other_hbm, copies_ref, own_ref, other_ref, own_sems, other_sems
+):
+    nl = own_ref.shape[1]
+    nb = own_ref.shape[3]
+    loads = [
+        half_loads(p, own_hbm, other_hbm, own_ref, other_ref, own_sems, other_sems)
+        for p in range(nl // 2)
+    ]
+    for pair in loads:
+        for load in pair:
+            load.start()
+    total = jnp.zeros(copies_ref.shape[1:], jnp.float32)
+    for step in range(nl):
+        if step % 2 == 0:
+            for load in loads[step // 2]:
+                load.wait()
+        ay = in_order(
+            at_ref, *[ref[:, step].reshape(nb // CORES, nb) for ref in (own_ref, other_ref)]
+        )
+        total += mm(slab_ref[:, step * nb : (step + 1) * nb], ay)
+    for i in range(copies_ref.shape[0]):
+        copies_ref[i] = total
 
 
 def route_kernel(nm, at_ref, four_ref, more_ref, pieces_ref, out_ref):
@@ -276,78 +329,130 @@
         out_ref[i, nm] = total
 
 
-def sides_kernel(mixer_ref, y_ref, rows_ref, z_ref, v_ref, proj_ref):
+def update_kernel(
+    nm, nt, at_ref, x_hbm, left_hbm, own_hbm, other_hbm, rows_ref, mixer_ref, y_hbm, upper_hbm,
+    out_ref, right_ref, held_ref, y_ref, upper_ref, x_ref, left_ref, own_ref, other_ref,
+    sems, in_sems, x_sems, left_sems, own_sems, other_sems,
+):
+    nb = mixer_ref.shape[0]
+    nl = left_ref.shape[0]
+    rows = nb * nt * nm
+
+    def pair_loads(pair):
+        at = pl.ds(pl.multiple_of(pair * 2 * rows, 2 * rows), 2 * rows)
+        two = pl.ds(pair * 2, 2)
+        return (
+            pltpu.make_async_copy(x_hbm.at[at], x_ref.at[at], x_sems.at[pair]),
+            pltpu.make_async_copy(left_hbm.at[two], left_ref.at[two], left_sems.at[pair]),
+        ) + half_loads(pair, own_hbm, other_hbm, own_ref, other_ref, own_sems, other_sems)
+
+    loads = [
+        pltpu.make_async_copy(src, dst, in_sems.at[i])
+        for i, (src, dst) in enumerate(((y_hbm, y_ref), (upper_hbm, upper_ref)))
+    ]
+    for load in loads:
+        load.start()
+    for pair in range(nl // 2):
+        for load in pair_loads(pair):
+            load.start()
     mixer = mixer_ref[...]
-    nb = mixer.shape[0]
-    nm = y_ref.shape[1] // nb
 
     def gathered(m):
         return jnp.concatenate(
             [rows_ref[:, k, m].reshape(nb // CORES, nb) for k in range(CORES)], axis=0
         )
 
-    for m in range(nm):
-        z_ref[:, m * nb : (m + 1) * nb] = lax.dot_general(
-            mixer, gathered(m), (((0,), (1,)), ((), ())), precision=HP, preferred_element_type=jnp.float32
+    core = mm(mm_tn(mixer, gathered(nm)), mixer)
+    z = lax.dot_general(
+        mixer,
+        jnp.concatenate([gathered(m) for m in range(nm)], axis=0),
+        (((0,), (1,)), ((), ())),
+        precision=HP,
+        preferred_element_type=jnp.float32,
+    )
+    for load in loads:
+        load.wait()
+    y = y_ref[...]
+    right_ref[...] = thrice(jnp.concatenate([z - mm_tn(core, y), mm(mixer, y)], axis=0), False)
+
+    def copy(pair):
+        return pltpu.make_async_copy(
+            held_ref.at[pair % 2],
+            out_ref.at[pl.ds(pl.multiple_of(pair * 2 * rows, 2 * rows), 2 * rows)],
+            sems.at[pair % 2],
         )
-    v_ref[...] = mm(mixer, y_ref[...])
-    proj_ref[...] = gathered(nm)
-
-
-def update_kernel(
-    nm, nt, at_ref, x_ref, left_ref, own_ref, other_ref, proj_ref,
-    mixer_ref, y_ref, z_ref, v_ref, upper_ref, out_ref, right_ref,
-):
-    step = pl.program_id(0)
-    nb = mixer_ref.shape[0]
-
-    @pl.when(step == 0)
-    def _():
-        mixer = mixer_ref[...]
-        core = mm(mm_tn(mixer, proj_ref[...]), mixer)
-        w = z_ref[...] - mm_tn(core, y_ref[...])
-        right_ref[...] = thrice(jnp.concatenate([w, v_ref[...]], axis=0), False)
-
-    ay = in_order(at_ref, rows_of(own_ref), rows_of(other_ref))
-    change = mm3(thrice(jnp.concatenate([left_ref[0], ay], axis=1), True), right_ref[...])
-    rows = nb
-    for m in range(nm):
-        for t in range(nt):
-            at = m * nb + t * LANES
-            out_ref[pl.ds(t * nm + m, rows, stride=nm * nt), :] = (
-                tile(x_ref, m, t, nm, nt) - change[:, at : at + LANES]
+
+    @pl.loop(0, nl // 2)
+    def _(pair):
+        @pl.when(pair >= 2)
+        def _():
+            copy(pair - 2).wait()
+
+        for load in pair_loads(pair):
+            load.wait()
+        lefts = []
+        for i in range(2):
+            step = pair * 2 + i
+            ay = in_order(
+                at_ref, *[ref[:, step].reshape(nb // CORES, nb) for ref in (own_ref, other_ref)]
             )
-
-    @pl.when(at_ref[1] == 0)
-    def _():
-        keep = (step == 0) & (at_ref[0] == 0)
-        band = jnp.where((step == 0) & (at_ref[0] == 1), -upper_ref[...], 0.0)
-        for t in range(nt):
-            old = tile(x_ref, 0, t, nm, nt)
-            out_ref[pl.ds(t * nm, rows, stride=nm * nt), :] = jnp.where(
-                keep, old, band[:, t * LANES : (t + 1) * LANES]
-            )
-
-    @pl.when((step == 0) & (at_ref[0] == 0))
-    def _():
-        band = jnp.where(at_ref[1] == 1, -upper_ref[...].T, 0.0)
-        for m in range(nm):
-            for t in range(nt):
-                new = band[:, t * LANES : (t + 1) * LANES] if m == 0 else jnp.zeros((rows, LANES))
-                if m == 0:
-                    new = jnp.where(at_ref[1] == 0, tile(x_ref, m, t, nm, nt), new)
-                out_ref[pl.ds(t * nm + m, rows, stride=nm * nt), :] = new
-
-
-def call(kernel, outs, ins, grid=(), flops=0, moved=1 << 20, scratch=(), out=jax.ShapeDtypeStruct):
+            lefts.append(jnp.concatenate([left_ref[step], ay], axis=1))
+        change = mm3(thrice(jnp.concatenate(lefts, axis=0), True), right_ref[...])
+        for i in range(2):
+            old_ref = x_ref.at[pl.ds(pl.multiple_of((pair * 2 + i) * rows, rows), rows)]
+            new_ref = held_ref.at[pair % 2, pl.ds(i * rows, rows)]
+
+            def put(m, t, value):
+                new_ref[pl.ds(t * nm + m, nb, stride=nm * nt), :] = value
+
+            for m in range(nm):
+                for t in range(nt):
+                    at = m * nb + t * LANES
+                    put(
+                        m, t,
+                        tile(old_ref, m, t, nm, nt) - change[i * nb : (i + 1) * nb, at : at + LANES],
+                    )
+
+            @pl.when(at_ref[1] == 0)
+            def _():
+                band = jnp.zeros((nb, nb), jnp.float32)
+                if i == 0:
+                    band = jnp.where((pair == 0) & (at_ref[0] == 1), -upper_ref[...], band)
+                for t in range(nt):
+                    new = band[:, t * LANES : (t + 1) * LANES]
+                    if i == 0:
+                        keep = (pair == 0) & (at_ref[0] == 0)
+                        new = jnp.where(keep, tile(old_ref, 0, t, nm, nt), new)
+                    put(0, t, new)
+
+            if i == 0:
+
+                @pl.when((pair == 0) & (at_ref[0] == 0))
+                def _():
+                    band = jnp.where(at_ref[1] == 1, -upper_ref[...].T, 0.0)
+                    for m in range(nm):
+                        for t in range(nt):
+                            new = jnp.zeros((nb, LANES), jnp.float32)
+                            if m == 0:
+                                new = band[:, t * LANES : (t + 1) * LANES]
+                                new = jnp.where(at_ref[1] == 0, tile(old_ref, m, t, nm, nt), new)
+                            put(m, t, new)
+
+        copy(pair).start()
+
+    copy(nl // 2 - 2).wait()
+    copy(nl // 2 - 1).wait()
+
+
+def call(kernel, outs, ins, grid=(), flops=0, moved=1 << 20, scratch=(), out=None):
     return pl.pallas_call(
         kernel,
         grid=grid,
-        out_shape=[out(s, jnp.float32) for s, _ in outs],
+        out_shape=[o(s, jnp.float32) for o, (s, _) in zip(out or [jax.ShapeDtypeStruct] * len(outs), outs)],
         in_specs=ins,
         out_specs=[spec for _, spec in outs],
         scratch_shapes=list(scratch),
-        compiler_params=pltpu.CompilerParams(vmem_limit_bytes=40 << 20),
+        compiler_params=pltpu.CompilerParams(vmem_limit_bytes=24 << 20),
         cost_estimate=pl.CostEstimate(flops=flops, bytes_accessed=moved, transcendentals=0),
     )
 
@@ -421,24 +526,34 @@
     p_cols, small, mine = barrier((p_cols, small, mine))
     far = far_moves(p_cols)
     other_small = lax.ppermute(small, "pcol", SWAP)
-    gram_spec = chunk(lambda l: (0, 0, 0, 0))
-    upper, inv, inv_t = call(
-        factor_kernel, [(square, VMEM)] * 3, [SMEM, gram_spec, gram_spec], grid=(1,), flops=10**10
-    )(at, small, other_small)
+    small_half = lambda i: (small[:, i], other_small[:, i])
+    inv, upper, inv_kept, inv_t = call(
+        factor_kernel,
+        [(square, VMEM)] + [(square, HBM)] * 3,
+        [SMEM, VMEM, VMEM],
+        flops=10**10,
+        out=[jax.ShapeDtypeStruct] + [pltpu.HBM] * 3,
+        scratch=[pltpu.VMEM(square, jnp.float32)] * 2 + [pltpu.SemaphoreType.DMA((3,))],
+    )(at, *small_half(0))
     own_p = share(mine[:nl], "pcol", CHIPS, PLANE)
 
     half_shape = (nl, nb // CORES, nb)
-    half_spec = pl.BlockSpec((1,) + half_shape[1:], lambda l: (l, 0, 0))
     row_spec = chunk(lambda l: (0, l, 0, 0))
     keep, send, y_cols = call(
         functools.partial(apply_kernel, nm, nt),
-        [(half_shape, half_spec), (half_shape, half_spec), (wide, whole(wide))],
-        [SMEM, x_spec] + [whole((x_rows, LANES))] * 3 + [whole(square)],
-        grid=(nl,),
+        [(half_shape, VMEM), (half_shape, HBM), (wide, HBM)],
+        [SMEM, VMEM, HBM, HBM, HBM, VMEM],
+        out=[jax.ShapeDtypeStruct, pltpu.HBM, pltpu.HBM],
+        scratch=[pltpu.VMEM((x_rows, LANES), jnp.float32)] * 3
+        + [
+            pltpu.VMEM(wide, jnp.float32),
+            pltpu.VMEM(half_shape, jnp.float32),
+            pltpu.SemaphoreType.DMA((3,)),
+            pltpu.SemaphoreType.DMA,
+            pltpu.SemaphoreType.DMA((nl,)),
+        ],
         flops=12 * nl * nb**2 * nc,
         moved=9 << 20,
-        scratch=[pltpu.VMEM((3 * nc, nb), jnp.bfloat16)],
-        out=pltpu.HBM,
     )(at, x, *[pltpu.with_memory_space_constraint(a, pltpu.HBM) for a in (p_cols, *far)], inv)
     keep, send, own_p = barrier((keep, send, own_p))
     other_p = lax.ppermute(own_p, "pcol", SWAP)
@@ -453,8 +568,9 @@
         flops=5 * 10**9,
         moved=6 << 20,
         scratch=[pltpu.VMEM(square, jnp.float32)],
+        out=[pltpu.HBM, jax.ShapeDtypeStruct],
     )(at, own_p, other_p, inv_t)
-    parts, y_rows, slab = barrier((parts, y_rows, slab))
+    parts, slab = barrier((parts, slab))
     piece = jnp.sum(parts, axis=0)
     own = share(piece, "pcol", CHIPS, PLANE)
     mixer = call(
@@ -463,19 +579,21 @@
         [SMEM] + [chunk(lambda l: (0, 1, 0, 0))] * 2 + [VMEM, pl.BlockSpec(memory_space=pl.ANY)],
         grid=(1,),
         flops=10**10,
-    )(at, small, other_small, inv, parts)[0]
+    )(at, small, other_small, inv_kept, parts)[0]
     four = doubled(doubled(piece[None], 4, nz), 2, nz)
     own, mixer, four = barrier((own, mixer, four))
     other = lax.ppermute(own, "pcol", SWAP)
 
+    ay_halves = [pltpu.with_memory_space_constraint(a, pltpu.HBM) for a in (own, other)]
+
     copies = call(
         proj_kernel,
-        [((nz, sub, nb), whole((nz, sub, nb)))],
-        [SMEM, pl.BlockSpec((sub, nb), lambda l: (0, l)), row_spec, row_spec],
-        grid=(nl,),
+        [((nz, sub, nb), VMEM)],
+        [SMEM, VMEM, HBM, HBM],
+        scratch=[pltpu.VMEM(own.shape, jnp.float32)] * 2 + [pltpu.SemaphoreType.DMA((nl // 2,))] * 2,
         flops=10**9,
         moved=4 << 20,
-    )(at, slab, own, other)[0]
+    )(at, slab, *ay_halves)[0]
     pieces = lax.all_to_all(copies, "prow", 0, 0)
     more = move(four, [(i, i ^ 1) for i in range(nz)])
     more, pieces = barrier((more, pieces))
@@ -487,20 +605,26 @@
         flops=10**8,
     )(at, four, more, pieces)[0]
     routed = lax.all_to_all(routed, "pcol", 0, 0)
-    z_cols, v_cols, proj = call(
-        sides_kernel, [(wide, VMEM), (wide, VMEM), (square, VMEM)], [VMEM] * 3, flops=3 * 10**9
-    )(mixer, y_cols, routed.reshape(CHIPS, CORES, nm + 1, sub, nb))
-
     out = call(
         functools.partial(update_kernel, nm, nt),
-        [(x.shape, x_spec)],
-        [SMEM, x_spec, pl.BlockSpec((1, nb, nb), lambda l: (l, 0, 0)), row_spec, row_spec]
-        + [whole(s) for s in (square, square, wide, wide, wide, square)],
-        grid=(nl,),
+        [(x.shape, HBM)],
+        [SMEM] + [HBM] * 4 + [VMEM] * 2 + [HBM] * 2,
         flops=12 * nl * nb**2 * nc,
         moved=12 << 20,
-        scratch=[pltpu.VMEM((6 * nb, nc), jnp.bfloat16)],
-    )(at, x, y_rows, own, other, proj, mixer, y_cols, z_cols, v_cols, upper)[0]
+        scratch=[
+            pltpu.VMEM((6 * nb, nc), jnp.bfloat16),
+            pltpu.VMEM((2, 2 * x_rows, LANES), jnp.float32),
+            pltpu.VMEM(wide, jnp.float32),
+            pltpu.VMEM(square, jnp.float32),
+            pltpu.VMEM(x.shape, jnp.float32),
+            pltpu.VMEM((nl, nb, nb), jnp.float32),
+            pltpu.VMEM(own.shape, jnp.float32),
+            pltpu.VMEM(own.shape, jnp.float32),
+            pltpu.SemaphoreType.DMA((2,)),
+            pltpu.SemaphoreType.DMA((2,)),
+        ]
+        + [pltpu.SemaphoreType.DMA((nl // 2,))] * 4,
+    )(at, pltpu.with_memory_space_constraint(x, pltpu.HBM), y_rows, *ay_halves, routed.reshape(CHIPS, CORES, nm + 1, sub, nb), mixer, y_cols, upper)[0]
     out = out.reshape(nl, nb, nt, nm, LANES).transpose(0, 1, 3, 2, 4)
     return out.reshape(hamiltonian.shape)
 

time: 205 us -> 203 us (level)
    unnamed x20 -> x22, local copies, waits for them, and re-layouts: 4.5 us -> 2.56 us
    pallas_call x5 -> x4, Pallas kernels: 30.7 us -> 30.2 us  [the longest x1 11.2 us: body(): call(factor_kernel, [(square, VMEM)] + [(square, HBM)] * 3, [SMEM, VMEM,...]
  transfers between devices with their start and end apart: 18 -> 18, of which waited for: 10 -> 10; matrix products, arithmetic and copies ran while one was open for 3% -> 3% of each run, Pallas kernels for 19% -> 20%
where the time goes in v5:
time: 203 us; the launch traced here: 202 us
  Pallas kernels  56.6 us (28%)
  starting transfers between devices  54.5 us (27%)
  waiting for transfers between devices  43.8 us (22%)
  blocking collectives  34.8 us (17%)
  local copies, waits for them, and re-layouts  6.86 us (3%)
  other arithmetic  4.89 us (2%)
    all_to_all x1, blocking collectives, body(): routed = lax.all_to_all(routed, 'pcol', 0, 0)  21.6 us
    all_to_all x3, starting transfers between devices, share(): return lax.all_to_all(copies, axis, 0, 0, axis_index_groups=groups)  15 us
    all_to_all x1, blocking collectives, share(): return lax.all_to_all(copies, axis, 0, 0, axis_index_groups=groups)  13.2 us
    ppermute x7, starting transfers between devices, move(): return lax.ppermute(block, 'prow', hops)  13.1 us
    pallas_call x1, Pallas kernels, body(): call(mixer_kernel, [(square, VMEM)], [SMEM] + [chunk(lambda l: (0, 1, 0,...  12.8 us
    pallas_call x1, Pallas kernels, body(): call(factor_kernel, [(square, VMEM)] + [(square, HBM)] * 3, [SMEM, VMEM,...  11.2 us
    all_to_all x1, waiting for transfers between devices, body(): mine = lax.all_to_all(outgoing, 'pcol', 0, 0, axis_index_groups=PLANE)[0]  9.78 us
    pallas_call x1, Pallas kernels, body(): call(functools.partial(update_kernel, nm, nt), [(x.shape, HBM)], [SMEM] +...  8.95 us
  transfers between devices with their start and end apart: 18, of which 10 were waited for; matrix products, arithmetic and copies ran while one was open for 3% of the time, Pallas kernels for 20%

profile of v5, /device:TPU:1, one launch (start us, length us, event | category | flops | bytes accessed | tf_op | source)
XLA Modules:
  0.0 202.0 jit_solution(17970506460507266195)
XLA Ops:
  0.1 5.5 %shard_map.17 = f32[2,16,9,8,256]{4,3,2,1,0:T(8,128)S(1)} custom-call(s32[5]{0:T(128)S(1)} %stack.36.at_ref, f32[8192,128]{1,0:T(8,128)} %bitcast.38), custom_call_target="tpu_custom_call" | custom-call | flops 20000000000 | bytes 6291456 | tf_op jit(solution)/shard_map/pallas_call | solution.py:505
  5.7 1.3 collective-permute-start.2
  7.0 5.7 %collective-permute-done.2 = f32[16,9,8,256]{3,2,1,0:T(8,128)} collective-permute-done((f32[16,9,8,256]{3,2,1,0:T(8,128)S(1)}, f32[16,9,8,256]{3,2,1,0:T(8,128)}, u32[]{:S(2)}, u32[]{:S(2)}) %collective-permute-start.2) | collective-permute-done | bytes 1179680 | tf_op jit(solution)/shard_map/ppermute | solution.py:518
  12.7 2.5 %fusion = f32[16,9,8,256]{3,2,1,0:T(8,128)} fusion(f32[16,9,8,256]{3,2,1,0:T(8,128)} %collective-permute-done.2, f32[2,16,9,8,256]{4,3,2,1,0:T(8,128)S(1)} %shard_map.17, pred[]{:T(512)S(6)} %eq.18), kind=kLoop, calls=%fused_computation.2 | loop fusion | flops 294912 | bytes 3538945 | tf_op jit(solution)/shard_map/jit(_where)/select_n | solution.py:518
  15.2 3.7 %all-to-all-start = ((f32[16,9,8,256]{3,2,1,0:T(8,128)}), f32[16,9,8,256]{3,2,1,0:T(8,128)S(1)}, u32[]{:S(2)}, u32[]{:S(2)}) async-start(f32[16,9,8,256]{3,2,1,0:T(8,128)} %fusion), calls=%async_computation | async-start | bytes 2359296 | tf_op jit(solution)/shard_map/all_to_all | solution.py:520
  18.9 1.2 slice.48
  20.1 6.7 %collective-permute-start.1 = (f32[1024,128]{1,0:T(8,128)S(1)}, f32[1024,128]{1,0:T(8,128)S(1)}, u32[]{:S(2)}, u32[]{:S(2)}) collective-permute-start(f32[1024,128]{1,0:T(8,128)S(1)} %bitcast.43), channel_id=1, source_target_pairs={{0,192},{1,193},{2,194},{3,195},{4,196},{5,197},{6,198},{7,199},{8... | collective-permute-start | bytes 1572872 | tf_op jit(solution)/shard_map/ppermute | solution.py:466
  26.8 1.3 collective-permute-start
  28.1 9.8 %all-to-all-done = f32[16,9,8,256]{3,2,1,0:T(8,128)S(1)} async-done(((f32[16,9,8,256]{3,2,1,0:T(8,128)}), f32[16,9,8,256]{3,2,1,0:T(8,128)S(1)}, u32[]{:S(2)}, u32[]{:S(2)}) %all-to-all-start) | async-done | bytes 1179680 | tf_op jit(solution)/shard_map/all_to_all | solution.py:520
  37.9 0.5 collective-permute-done.1
  38.4 1.3 collective-permute-done
  39.8 13.2 %all_to_all.40 = f32[8,2,8,256]{3,2,1,0:T(8,128)S(1)} all-to-all(f32[8,2,8,256]{3,2,1,0:T(8,128)S(1)} %broadcast_in_dim.10), channel_id=1, replica_groups=mesh['prow'=8,'pcol'=32] {'prow'}, dimensions={0} | all-to-all | bytes 262144 | tf_op jit(solution)/shard_map/all_to_all | solution.py:462
  53.0 0.7 broadcast_in_dim.11
  53.7 6.0 %all-to-all-start.2 = ((f32[16,2,8,256]{3,2,1,0:T(8,128)}), f32[16,2,8,256]{3,2,1,0:T(8,128)S(1)}, u32[]{:S(2)}, u32[]{:S(2)}) async-start(f32[16,2,8,256]{3,2,1,0:T(8,128)} %broadcast_in_dim.11), calls=%async_computation.2 | async-start | bytes 524288 | tf_op jit(solution)/shard_map/all_to_all | solution.py:462
  59.7 1.2 add_select_fusion.top_hbm
  60.9 6.2 %all-to-all-done.2.own_ref = f32[16,2,8,256]{3,2,1,0:T(8,128)S(1)} async-done(((f32[16,2,8,256]{3,2,1,0:T(8,128)}), f32[16,2,8,256]{3,2,1,0:T(8,128)S(1)}, u32[]{:S(2)}, u32[]{:S(2)}) %all-to-all-start.2) | async-done | bytes 262176 | tf_op jit(solution)/shard_map/all_to_all | solution.py:462
  67.2 3.6 %collective-permute-start.5 = (f32[16,2,8,256]{3,2,1,0:T(8,128)S(1)}, f32[16,2,8,256]{3,2,1,0:T(8,128)S(1)}, u32[]{:S(2)}, u32[]{:S(2)}) collective-permute-start(f32[16,2,8,256]{3,2,1,0:T(8,128)S(1)} %all-to-all-done.2.own_ref), channel_id=1, source_target_pairs={{0,1},{1,0},{2,3},{3,2},{4,5},{5,4},{6,7},{7,6},{8,9},{9,8},{10,11... | collective-permute-start | bytes 786440 | tf_op jit(solution)/shard_map/ppermute | solution.py:528
  70.8 1.5 collective-permute-start.4
  72.3 1.3 collective-permute-start.3
  73.6 1.1 broadcast_in_dim.12
  74.7 3.7 %all-to-all-start.3 = ((f32[16,8,8,256]{3,2,1,0:T(8,128)}), f32[16,8,8,256]{3,2,1,0:T(8,128)S(1)}, u32[]{:S(2)}, u32[]{:S(2)}) async-start(f32[16,8,8,256]{3,2,1,0:T(8,128)} %broadcast_in_dim.12), calls=%async_computation.3 | async-start | bytes 2097152 | tf_op jit(solution)/shard_map/all_to_all | solution.py:462
  78.4 11.2 %shard_map.18 = (f32[256,256]{1,0:T(8,128)S(1)}, f32[256,256]{1,0:T(8,128)}, f32[256,256]{1,0:T(8,128)}, f32[256,256]{1,0:T(8,128)}) custom-call(s32[5]{0:T(128)S(1)} %stack.36.at_ref, f32[16,8,256]{2,1,0:T(8,128)S(1)} %slice_bitcast_fusion.3.own_ref, f32[16,8,256]{2,1,0:T(8,128)S(1)} %slice_bitcast_fusion.2.other_ref), custom_call_target="tpu_custom_call" | custom-call | flops 10000000000 | bytes 1048576 | tf_op jit(solution)/shard_map/pallas_call | solution.py:530
  89.7 0.8 copy-done.9
  90.4 0.8 copy-done.10
  91.2 5.8 %shard_map.19 = (f32[8,128,256]{2,1,0:T(8,128)S(1)}, f32[8,128,256]{2,1,0:T(8,128)}, f32[256,512]{1,0:T(8,128)}) custom-call(s32[5]{0:T(128)S(1)} %stack.36.at_ref, f32[8192,128]{1,0:T(8,128)S(1)} %bitcast.41, f32[1024,128]{1,0:T(8,128)} %copy-done.7, f32[1024,128]{1,0:T(8,128)} %copy-done.10, f32[1024,128]{1,0:T(8,128)} %copy-done.9, ...), custom_call_target="tpu_custom_call" | custom-call | flops 3221225472 | bytes 9437184 | tf_op jit(solution)/shard_map/pallas_call | solution.py:542
  97.1 0.4 collective-permute-start.7
  97.5 0.2 collective-permute-start.6
  97.7 2.4 %collective-permute-done.7 = f32[8,128,256]{2,1,0:T(8,128)S(1)} collective-permute-done((f32[8,128,256]{2,1,0:T(8,128)}, f32[8,128,256]{2,1,0:T(8,128)S(1)}, u32[]{:S(2)}, u32[]{:S(2)}) %collective-permute-start.7) | collective-permute-done | bytes 1048608 | tf_op jit(solution)/shard_map/ppermute | solution.py:560
  100.0 1.1 copy_bitcast_fusion
  101.2 7.5 %all-to-all-start.4 = ((f32[16,8,8,256]{3,2,1,0:T(8,128)}), f32[16,8,8,256]{3,2,1,0:T(8,128)S(1)}, u32[]{:S(2)}, u32[]{:S(2)}) async-start(f32[16,8,8,256]{3,2,1,0:T(8,128)} %copy_bitcast_fusion), calls=%async_computation.4 | async-start | bytes 2097152 | tf_op jit(solution)/shard_map/all_to_all | solution.py:561
  108.7 7.0 %shard_map.20 = (f32[8,256,256]{2,1,0:T(8,128)}, f32[8,2048]{1,0:T(8,128)S(1)}) custom-call(s32[5]{0:T(128)S(1)} %stack.36.at_ref, f32[16,8,8,256]{3,2,1,0:T(8,128)S(1)} %all-to-all-done.3.own_ref, f32[16,8,8,256]{3,2,1,0:T(8,128)} %collective-permute-done.6.other_ref, f32[256,256]{1,0:T(8,128)S(1)} %copy-done.4), custom_call_target="tpu_custom_call" | custom-call | flops 5000000000 | bytes 6291456 | tf_op jit(solution)/shard_map/pallas_call | solution.py:562
  115.6 8.0 %all-to-all-done.4.after_ref = f32[16,8,8,256]{3,2,1,0:T(8,128)S(1)} async-done(((f32[16,8,8,256]{3,2,1,0:T(8,128)}), f32[16,8,8,256]{3,2,1,0:T(8,128)S(1)}, u32[]{:S(2)}, u32[]{:S(2)}) %all-to-all-start.4) | async-done | bytes 1048608 | tf_op jit(solution)/shard_map/all_to_all | solution.py:561
  123.7 0.1 collective-permute-start.8
  123.8 1.1 broadcast_in_dim.13
  124.9 5.3 %all-to-all-start.5 = ((f32[16,8,8,256]{3,2,1,0:T(8,128)}), f32[16,8,8,256]{3,2,1,0:T(8,128)}, u32[]{:S(2)}, u32[]{:S(2)}) async-start(f32[16,8,8,256]{3,2,1,0:T(8,128)} %broadcast_in_dim.13), calls=%async_computation.5 | async-start | bytes 2097152 | tf_op jit(solution)/shard_map/all_to_all | solution.py:462
  130.2 1.3 collective-permute-done.8
  131.6 1.0 collective-permute-start.9
  132.6 12.8 %shard_map.21.mixer_ref = f32[256,256]{1,0:T(8,128)S(1)} custom-call(s32[5]{0:T(128)S(1)} %stack.36.at_ref, f32[16,2,8,256]{3,2,1,0:T(8,128)S(1)} %all-to-all-done.2.own_ref, f32[16,2,8,256]{3,2,1,0:T(8,128)S(1)} %collective-permute-done.5.other_ref, f32[256,256]{1,0:T(8,128)S(1)} %copy-done.5, f32[16,8,8,256]{3,2,1,0:T(8,128)S(1)} %all-to-all-done.4.after_ref), custom_call_target="tpu_custom_call" | custom-call | flops 10000000000 | bytes 1048576 | tf_op jit(solution)/shard_map/pallas_call | solution.py:576
  145.4 4.1 %collective-permute-start.10 = (f32[16,8,8,256]{3,2,1,0:T(8,128)}, f32[16,8,8,256]{3,2,1,0:T(8,128)S(1)}, u32[]{:S(2)}, u32[]{:S(2)}) collective-permute-start(f32[16,8,8,256]{3,2,1,0:T(8,128)} %all-to-all-done.5.own_hbm), channel_id=1, source_target_pairs={{0,1},{1,0},{2,3},{3,2},{4,5},{5,4},{6,7},{7,6},{8,9},{9,8},{10,11... | collective-permute-start | bytes 3145736 | tf_op jit(solution)/shard_map/ppermute | solution.py:585
  149.5 1.2 collective-permute-start.11
  150.7 1.3 collective-permute-done.10.other_hbm
  152.0 1.0 copy-done.6
  153.0 4.2 %shard_map.22 = f32[8,8,256]{2,1,0:T(8,128)} custom-call(s32[5]{0:T(128)S(1)} %stack.36.at_ref, f32[8,2048]{1,0:T(8,128)S(1)} %get-tuple-element.49.slab_ref, f32[16,8,8,256]{3,2,1,0:T(8,128)} %all-to-all-done.5.own_hbm, f32[16,8,8,256]{3,2,1,0:T(8,128)} %copy-done.6), custom_call_target="tpu_custom_call" | custom-call | flops 1000000000 | bytes 4194304 | tf_op jit(solution)/shard_map/pallas_call | solution.py:589
  157.2 5.7 %all-to-all-start.6 = ((f32[8,8,256]{2,1,0:T(8,128)}), f32[8,8,256]{2,1,0:T(8,128)S(1)}, u32[]{:S(2)}, u32[]{:S(2)}) async-start(f32[8,8,256]{2,1,0:T(8,128)} %shard_map.22), calls=%async_computation.6 | async-start | bytes 131072 | tf_op jit(solution)/shard_map/all_to_all | solution.py:597
  162.9 7.2 %all-to-all-done.6.pieces_ref = f32[8,8,256]{2,1,0:T(8,128)S(1)} async-done(((f32[8,8,256]{2,1,0:T(8,128)}), f32[8,8,256]{2,1,0:T(8,128)S(1)}, u32[]{:S(2)}, u32[]{:S(2)}) %all-to-all-start.6) | async-done | bytes 65568 | tf_op jit(solution)/shard_map/all_to_all | solution.py:597
  170.1 1.1 shard_map.23
  171.2 21.6 %all_to_all.41 = f32[32,3,8,256]{3,2,1,0:T(8,128)S(1)} all-to-all(f32[32,3,8,256]{3,2,1,0:T(8,128)S(1)} %shard_map.23), channel_id=1, replica_groups=mesh['prow'=8,'pcol'=32] {'pcol'}, dimensions={0} | all-to-all | bytes 1572864 | tf_op jit(solution)/shard_map/all_to_all | solution.py:607
  192.9 8.9 %shard_map.24 = f32[8192,128]{1,0:T(8,128)} custom-call(s32[5]{0:T(128)S(1)} %stack.36.at_ref, f32[8192,128]{1,0:T(8,128)} %bitcast.40, f32[8,256,256]{2,1,0:T(8,128)S(1)} %copy-done.1, f32[16,8,8,256]{3,2,1,0:T(8,128)} %all-to-all-done.5.own_hbm, f32[16,8,8,256]{3,2,1,0:T(8,128)} %copy-done.6, f32[16,2,3,8,256]{4,3,2,1,0:T(8,128)S(1)} %bitcast.42, ...), custom_call_target="tpu_custom_call" | custom-call | flops 3221225472 | bytes 12582912 | tf_op jit(solution)/shard_map/pallas_call | solution.py:608
  (42 shorter events, 0.4 us)
Async XLA Ops:
  5.7 7.0 %collective-permute-start.2 = (f32[16,9,8,256]{3,2,1,0:T(8,128)S(1)}, f32[16,9,8,256]{3,2,1,0:T(8,128)}, u32[]{:S(2)}, u32[]{:S(2)}) collective-permute-start(f32[16,9,8,256]{3,2,1,0:T(8,128)S(1)} %slice_bitcast_fusion), channel_id=1, source_target_pairs={{0,1},{32,33},{64,65},{96,97},{128,129},{160,161},{192,193},{224,2... | collective-permute-start | bytes 3538952 | tf_op jit(solution)/shard_map/ppermute | solution.py:518
  15.2 22.7 %all-to-all-start = ((f32[16,9,8,256]{3,2,1,0:T(8,128)}), f32[16,9,8,256]{3,2,1,0:T(8,128)S(1)}, u32[]{:S(2)}, u32[]{:S(2)}) async-start(f32[16,9,8,256]{3,2,1,0:T(8,128)} %fusion), calls=%async_computation | async-start | bytes 2359296 | tf_op jit(solution)/shard_map/all_to_all | solution.py:520
  20.1 18.3 %collective-permute-start.1 = (f32[1024,128]{1,0:T(8,128)S(1)}, f32[1024,128]{1,0:T(8,128)S(1)}, u32[]{:S(2)}, u32[]{:S(2)}) collective-permute-start(f32[1024,128]{1,0:T(8,128)S(1)} %bitcast.43), channel_id=1, source_target_pairs={{0,192},{1,193},{2,194},{3,195},{4,196},{5,197},{6,198},{7,199},{8... | collective-permute-start | bytes 1572872 | tf_op jit(solution)/shard_map/ppermute | solution.py:466
  26.8 13.0 %collective-permute-start = (f32[1024,128]{1,0:T(8,128)S(1)}, f32[1024,128]{1,0:T(8,128)S(1)}, u32[]{:S(2)}, u32[]{:S(2)}) collective-permute-start(f32[1024,128]{1,0:T(8,128)S(1)} %bitcast.44), channel_id=1, source_target_pairs={{0,96},{1,97},{2,98},{3,99},{4,100},{5,101},{6,102},{7,103},{8,104... | collective-permute-start | bytes 1572872 | tf_op jit(solution)/shard_map/ppermute | solution.py:466
  39.8 14.0 %copy-start.8 = (f32[1024,128]{1,0:T(8,128)}, f32[1024,128]{1,0:T(8,128)S(1)}, u32[]{:S(2)}) copy-start(f32[1024,128]{1,0:T(8,128)S(1)} %collective-permute-done) | copy-start | bytes 1572868
  53.7 13.4 %all-to-all-start.2 = ((f32[16,2,8,256]{3,2,1,0:T(8,128)}), f32[16,2,8,256]{3,2,1,0:T(8,128)S(1)}, u32[]{:S(2)}, u32[]{:S(2)}) async-start(f32[16,2,8,256]{3,2,1,0:T(8,128)} %broadcast_in_dim.11), calls=%async_computation.2 | async-start | bytes 524288 | tf_op jit(solution)/shard_map/all_to_all | solution.py:462
  60.9 13.8 %copy-start.7 = (f32[1024,128]{1,0:T(8,128)}, f32[1024,128]{1,0:T(8,128)S(1)}, u32[]{:S(2)}) copy-start(f32[1024,128]{1,0:T(8,128)S(1)} %add_select_fusion.top_hbm) | copy-start | bytes 1572868
  67.2 11.2 %collective-permute-start.5 = (f32[16,2,8,256]{3,2,1,0:T(8,128)S(1)}, f32[16,2,8,256]{3,2,1,0:T(8,128)S(1)}, u32[]{:S(2)}, u32[]{:S(2)}) collective-permute-start(f32[16,2,8,256]{3,2,1,0:T(8,128)S(1)} %all-to-all-done.2.own_ref), channel_id=1, source_target_pairs={{0,1},{1,0},{2,3},{3,2},{4,5},{5,4},{6,7},{7,6},{8,9},{9,8},{10,11... | collective-permute-start | bytes 786440 | tf_op jit(solution)/shard_map/ppermute | solution.py:528
  70.8 18.9 %collective-permute-start.4 = (f32[1024,128]{1,0:T(8,128)S(1)}, f32[1024,128]{1,0:T(8,128)S(1)}, u32[]{:S(2)}, u32[]{:S(2)}) collective-permute-start(f32[1024,128]{1,0:T(8,128)S(1)} %add_select_fusion.top_hbm), channel_id=1, source_target_pairs={{0,224},{96,64},{192,160},{1,225},{97,65},{193,161},{2,226},{98,66... | collective-permute-start | bytes 1572872 | tf_op jit(solution)/shard_map/ppermute | solution.py:466
  72.3 17.4 %collective-permute-start.3 = (f32[1024,128]{1,0:T(8,128)S(1)}, f32[1024,128]{1,0:T(8,128)S(1)}, u32[]{:S(2)}, u32[]{:S(2)}) collective-permute-start(f32[1024,128]{1,0:T(8,128)S(1)} %add_select_fusion.top_hbm), channel_id=1, source_target_pairs={{0,32},{96,128},{1,33},{97,129},{2,34},{98,130},{3,35},{99,131},{4... | collective-permute-start | bytes 1572872 | tf_op jit(solution)/shard_map/ppermute | solution.py:466
  74.7 22.4 %all-to-all-start.3 = ((f32[16,8,8,256]{3,2,1,0:T(8,128)}), f32[16,8,8,256]{3,2,1,0:T(8,128)S(1)}, u32[]{:S(2)}, u32[]{:S(2)}) async-start(f32[16,8,8,256]{3,2,1,0:T(8,128)} %broadcast_in_dim.12), calls=%async_computation.3 | async-start | bytes 2097152 | tf_op jit(solution)/shard_map/all_to_all | solution.py:462
  78.4 12.8 %copy-start = (f32[8,256,2,256]{3,2,1,0:T(2,128)S(1)}, f32[8,256,2,256]{3,2,1,0:T(2,128)}, u32[]{:S(2)}) copy-start(f32[8,256,2,256]{3,2,1,0:T(2,128)} %param.1) | copy-start | bytes 12582916
  89.7 0.8 copy-start.9
  90.4 0.8 copy-start.10
  97.1 3.0 %collective-permute-start.7 = (f32[8,128,256]{2,1,0:T(8,128)}, f32[8,128,256]{2,1,0:T(8,128)S(1)}, u32[]{:S(2)}, u32[]{:S(2)}) collective-permute-start(f32[8,128,256]{2,1,0:T(8,128)} %get-tuple-element.43), channel_id=1, source_target_pairs={{0,1},{1,0},{2,3},{3,2},{4,5},{5,4},{6,7},{7,6},{8,9},{9,8},{10,11... | collective-permute-start | bytes 3145736 | tf_op jit(solution)/shard_map/ppermute | solution.py:560
  97.5 11.2 %collective-permute-start.6 = (f32[16,8,8,256]{3,2,1,0:T(8,128)S(1)}, f32[16,8,8,256]{3,2,1,0:T(8,128)}, u32[]{:S(2)}, u32[]{:S(2)}) collective-permute-start(f32[16,8,8,256]{3,2,1,0:T(8,128)S(1)} %all-to-all-done.3.own_ref), channel_id=1, source_target_pairs={{0,1},{1,0},{2,3},{3,2},{4,5},{5,4},{6,7},{7,6},{8,9},{9,8},{10,11... | collective-permute-start | bytes 3145736 | tf_op jit(solution)/shard_map/ppermute | solution.py:559
  101.2 7.5 %copy-start.4 = (f32[256,256]{1,0:T(8,128)S(1)}, f32[256,256]{1,0:T(8,128)}, u32[]{:S(2)}) copy-start(f32[256,256]{1,0:T(8,128)} %get-tuple-element.40.inv_t_ref) | copy-start | bytes 786436
  101.2 22.5 %all-to-all-start.4 = ((f32[16,8,8,256]{3,2,1,0:T(8,128)}), f32[16,8,8,256]{3,2,1,0:T(8,128)S(1)}, u32[]{:S(2)}, u32[]{:S(2)}) async-start(f32[16,8,8,256]{3,2,1,0:T(8,128)} %copy_bitcast_fusion), calls=%async_computation.4 | async-start | bytes 2097152 | tf_op jit(solution)/shard_map/all_to_all | solution.py:561
  123.7 7.8 %collective-permute-start.8 = (f32[1,8,8,256]{3,2,1,0:T(8,128)S(1)}, f32[1,8,8,256]{3,2,1,0:T(8,128)S(1)}, u32[]{:S(2)}, u32[]{:S(2)}) collective-permute-start(f32[1,8,8,256]{3,2,1,0:T(8,128)S(1)} %bitcast.46), channel_id=1, source_target_pairs={{0,128},{32,160},{64,192},{96,224},{128,0},{160,32},{192,64},{224,... | collective-permute-start | bytes 196616 | tf_op jit(solution)/shard_map/ppermute | solution.py:466
  124.9 7.6 %copy-start.5 = (f32[256,256]{1,0:T(8,128)S(1)}, f32[256,256]{1,0:T(8,128)}, u32[]{:S(2)}) copy-start(f32[256,256]{1,0:T(8,128)} %get-tuple-element.46.inv_ref) | copy-start | bytes 786436
  124.9 20.5 %all-to-all-start.5 = ((f32[16,8,8,256]{3,2,1,0:T(8,128)}), f32[16,8,8,256]{3,2,1,0:T(8,128)}, u32[]{:S(2)}, u32[]{:S(2)}) async-start(f32[16,8,8,256]{3,2,1,0:T(8,128)} %broadcast_in_dim.13), calls=%async_computation.5 | async-start | bytes 2097152 | tf_op jit(solution)/shard_map/all_to_all | solution.py:462
  131.6 13.8 %collective-permute-start.9 = (f32[2,8,8,256]{3,2,1,0:T(8,128)S(1)}, f32[2,8,8,256]{3,2,1,0:T(8,128)S(1)}, u32[]{:S(2)}, u32[]{:S(2)}) collective-permute-start(f32[2,8,8,256]{3,2,1,0:T(8,128)S(1)} %pad_maximum_fusion.1), channel_id=1, source_target_pairs={{0,64},{32,96},{64,0},{96,32},{128,192},{160,224},{192,128},{224,1... | collective-permute-start | bytes 393224 | tf_op jit(solution)/shard_map/ppermute | solution.py:466
  145.4 6.6 %collective-permute-start.10 = (f32[16,8,8,256]{3,2,1,0:T(8,128)}, f32[16,8,8,256]{3,2,1,0:T(8,128)S(1)}, u32[]{:S(2)}, u32[]{:S(2)}) collective-permute-start(f32[16,8,8,256]{3,2,1,0:T(8,128)} %all-to-all-done.5.own_hbm), channel_id=1, source_target_pairs={{0,1},{1,0},{2,3},{3,2},{4,5},{5,4},{6,7},{7,6},{8,9},{9,8},{10,11... | collective-permute-start | bytes 3145736 | tf_op jit(solution)/shard_map/ppermute | solution.py:585
  149.5 13.4 %collective-permute-start.11 = (f32[4,8,8,256]{3,2,1,0:T(8,128)S(1)}, f32[4,8,8,256]{3,2,1,0:T(8,128)}, u32[]{:S(2)}, u32[]{:S(2)}) collective-permute-start(f32[4,8,8,256]{3,2,1,0:T(8,128)S(1)} %pad_maximum_fusion.four_ref), channel_id=1, source_target_pairs={{0,32},{32,0},{64,96},{96,64},{128,160},{160,128},{192,224},{224,1... | collective-permute-start | bytes 786440 | tf_op jit(solution)/shard_map/ppermute | solution.py:466
  152.0 1.0 copy-start.6
  157.2 12.9 %all-to-all-start.6 = ((f32[8,8,256]{2,1,0:T(8,128)}), f32[8,8,256]{2,1,0:T(8,128)S(1)}, u32[]{:S(2)}, u32[]{:S(2)}) async-start(f32[8,8,256]{2,1,0:T(8,128)} %shard_map.22), calls=%async_computation.6 | async-start | bytes 131072 | tf_op jit(solution)/shard_map/all_to_all | solution.py:597
  162.9 30.0 %copy-start.1 = (f32[8,256,256]{2,1,0:T(8,128)S(1)}, f32[8,256,256]{2,1,0:T(8,128)}, u32[]{:S(2)}) copy-start(f32[8,256,256]{2,1,0:T(8,128)} %get-tuple-element.41.left_hbm) | copy-start | bytes 6291460
  162.9 30.0 %copy-start.2 = (f32[256,512]{1,0:T(8,128)S(1)}, f32[256,512]{1,0:T(8,128)}, u32[]{:S(2)}) copy-start(f32[256,512]{1,0:T(8,128)} %get-tuple-element.53.y_hbm) | copy-start | bytes 1572868
  162.9 30.0 %copy-start.3 = (f32[256,256]{1,0:T(8,128)S(1)}, f32[256,256]{1,0:T(8,128)}, u32[]{:S(2)}) copy-start(f32[256,256]{1,0:T(8,128)} %get-tuple-element.54.upper_hbm) | copy-start | bytes 786436

commit v6 on v5

--- a/solution.py
+++ b/solution.py
@@ -556,8 +556,9 @@
         moved=9 << 20,
     )(at, x, *[pltpu.with_memory_space_constraint(a, pltpu.HBM) for a in (p_cols, *far)], inv)
     keep, send, own_p = barrier((keep, send, own_p))
+    parts = (keep + lax.ppermute(send, "pcol", SWAP)).reshape(nl, CHIPS, sub, nb).transpose(1, 0, 2, 3)
+    parts, own_p = barrier((parts, own_p))
     other_p = lax.ppermute(own_p, "pcol", SWAP)
-    parts = (keep + lax.ppermute(send, "pcol", SWAP)).reshape(nl, CHIPS, sub, nb).transpose(1, 0, 2, 3)
     parts = lax.all_to_all(parts, "pcol", 0, 0, axis_index_groups=PLANE)
     y_rows, slab = call(
         rows_kernel,

time: 203 us -> 203 us (level)
  starting transfers between devices: 54.5 us -> 52.4 us
  transfers between devices with their start and end apart: 18 -> 18, of which waited for: 10 -> 10; matrix products, arithmetic and copies ran while one was open for 3% -> 2% of each run, Pallas kernels for 20% -> 20%
where the time goes in v6:
time: 203 us; the launch traced here: 202 us
  Pallas kernels  56.6 us (28%)
  starting transfers between devices  52.4 us (26%)
  waiting for transfers between devices  45.8 us (23%)
  blocking collectives  34.7 us (17%)
  local copies, waits for them, and re-layouts  6.86 us (3%)
  other arithmetic  4.89 us (2%)
    all_to_all x1, blocking collectives, body(): routed = lax.all_to_all(routed, 'pcol', 0, 0)  21.5 us
    all_to_all x3, starting transfers between devices, share(): return lax.all_to_all(copies, axis, 0, 0, axis_index_groups=groups)  14.2 us
    all_to_all x1, blocking collectives, share(): return lax.all_to_all(copies, axis, 0, 0, axis_index_groups=groups)  13.2 us
    pallas_call x1, Pallas kernels, body(): call(mixer_kernel, [(square, VMEM)], [SMEM] + [chunk(lambda l: (0, 1, 0,...  12.8 us
    ppermute x7, starting transfers between devices, move(): return lax.ppermute(block, 'prow', hops)  12.4 us
    pallas_call x1, Pallas kernels, body(): call(factor_kernel, [(square, VMEM)] + [(square, HBM)] * 3, [SMEM, VMEM,...  11.2 us
    all_to_all x1, waiting for transfers between devices, body(): mine = lax.all_to_all(outgoing, 'pcol', 0, 0, axis_index_groups=PLANE)[0]  9.78 us
    all_to_all x1, waiting for transfers between devices, body(): parts = lax.all_to_all(parts, 'pcol', 0, 0, axis_index_groups=PLANE)  9.05 us
  transfers between devices with their start and end apart: 18, of which 10 were waited for; matrix products, arithmetic and copies ran while one was open for 2% of the time, Pallas kernels for 20%

profile of v6, /device:TPU:1, one launch (start us, length us, event | category | flops | bytes accessed | tf_op | source)
XLA Modules:
  0.0 201.7 jit_solution(17588962736433672766)
XLA Ops:
  0.1 5.5 %shard_map.17 = f32[2,16,9,8,256]{4,3,2,1,0:T(8,128)S(1)} custom-call(s32[5]{0:T(128)S(1)} %stack.36.at_ref, f32[8192,128]{1,0:T(8,128)} %bitcast.38), custom_call_target="tpu_custom_call" | custom-call | flops 20000000000 | bytes 6291456 | tf_op jit(solution)/shard_map/pallas_call | solution.py:505
  5.7 1.3 collective-permute-start.2
  7.0 5.7 %collective-permute-done.2 = f32[16,9,8,256]{3,2,1,0:T(8,128)} collective-permute-done((f32[16,9,8,256]{3,2,1,0:T(8,128)S(1)}, f32[16,9,8,256]{3,2,1,0:T(8,128)}, u32[]{:S(2)}, u32[]{:S(2)}) %collective-permute-start.2) | collective-permute-done | bytes 1179680 | tf_op jit(solution)/shard_map/ppermute | solution.py:518
  12.7 2.5 %fusion = f32[16,9,8,256]{3,2,1,0:T(8,128)} fusion(f32[16,9,8,256]{3,2,1,0:T(8,128)} %collective-permute-done.2, f32[2,16,9,8,256]{4,3,2,1,0:T(8,128)S(1)} %shard_map.17, pred[]{:T(512)S(6)} %eq.18), kind=kLoop, calls=%fused_computation.2 | loop fusion | flops 294912 | bytes 3538945 | tf_op jit(solution)/shard_map/jit(_where)/select_n | solution.py:518
  15.2 3.7 %all-to-all-start = ((f32[16,9,8,256]{3,2,1,0:T(8,128)}), f32[16,9,8,256]{3,2,1,0:T(8,128)S(1)}, u32[]{:S(2)}, u32[]{:S(2)}) async-start(f32[16,9,8,256]{3,2,1,0:T(8,128)} %fusion), calls=%async_computation | async-start | bytes 2359296 | tf_op jit(solution)/shard_map/all_to_all | solution.py:520
  18.9 1.2 slice.48
  20.1 6.7 %collective-permute-start.1 = (f32[1024,128]{1,0:T(8,128)S(1)}, f32[1024,128]{1,0:T(8,128)S(1)}, u32[]{:S(2)}, u32[]{:S(2)}) collective-permute-start(f32[1024,128]{1,0:T(8,128)S(1)} %bitcast.43), channel_id=1, source_target_pairs={{0,192},{1,193},{2,194},{3,195},{4,196},{5,197},{6,198},{7,199},{8... | collective-permute-start | bytes 1572872 | tf_op jit(solution)/shard_map/ppermute | solution.py:466
  26.8 1.3 collective-permute-start
  28.1 9.8 %all-to-all-done = f32[16,9,8,256]{3,2,1,0:T(8,128)S(1)} async-done(((f32[16,9,8,256]{3,2,1,0:T(8,128)}), f32[16,9,8,256]{3,2,1,0:T(8,128)S(1)}, u32[]{:S(2)}, u32[]{:S(2)}) %all-to-all-start) | async-done | bytes 1179680 | tf_op jit(solution)/shard_map/all_to_all | solution.py:520
  37.9 0.5 collective-permute-done.1
  38.4 1.3 collective-permute-done
  39.8 13.2 %all_to_all.40 = f32[8,2,8,256]{3,2,1,0:T(8,128)S(1)} all-to-all(f32[8,2,8,256]{3,2,1,0:T(8,128)S(1)} %broadcast_in_dim.10), channel_id=1, replica_groups=mesh['prow'=8,'pcol'=32] {'prow'}, dimensions={0} | all-to-all | bytes 262144 | tf_op jit(solution)/shard_map/all_to_all | solution.py:462
  53.0 0.7 broadcast_in_dim.11
  53.7 6.0 %all-to-all-start.2 = ((f32[16,2,8,256]{3,2,1,0:T(8,128)}), f32[16,2,8,256]{3,2,1,0:T(8,128)S(1)}, u32[]{:S(2)}, u32[]{:S(2)}) async-start(f32[16,2,8,256]{3,2,1,0:T(8,128)} %broadcast_in_dim.11), calls=%async_computation.2 | async-start | bytes 524288 | tf_op jit(solution)/shard_map/all_to_all | solution.py:462
  59.7 1.2 add_select_fusion.top_hbm
  60.9 6.2 %all-to-all-done.2.own_ref = f32[16,2,8,256]{3,2,1,0:T(8,128)S(1)} async-done(((f32[16,2,8,256]{3,2,1,0:T(8,128)}), f32[16,2,8,256]{3,2,1,0:T(8,128)S(1)}, u32[]{:S(2)}, u32[]{:S(2)}) %all-to-all-start.2) | async-done | bytes 262176 | tf_op jit(solution)/shard_map/all_to_all | solution.py:462
  67.2 3.6 %collective-permute-start.5 = (f32[16,2,8,256]{3,2,1,0:T(8,128)S(1)}, f32[16,2,8,256]{3,2,1,0:T(8,128)S(1)}, u32[]{:S(2)}, u32[]{:S(2)}) collective-permute-start(f32[16,2,8,256]{3,2,1,0:T(8,128)S(1)} %all-to-all-done.2.own_ref), channel_id=1, source_target_pairs={{0,1},{1,0},{2,3},{3,2},{4,5},{5,4},{6,7},{7,6},{8,9},{9,8},{10,11... | collective-permute-start | bytes 786440 | tf_op jit(solution)/shard_map/ppermute | solution.py:528
  70.8 1.5 collective-permute-start.4
  72.3 1.3 collective-permute-start.3
  73.6 1.1 broadcast_in_dim.12
  74.7 3.7 %all-to-all-start.3 = ((f32[16,8,8,256]{3,2,1,0:T(8,128)}), f32[16,8,8,256]{3,2,1,0:T(8,128)S(1)}, u32[]{:S(2)}, u32[]{:S(2)}) async-start(f32[16,8,8,256]{3,2,1,0:T(8,128)} %broadcast_in_dim.12), calls=%async_computation.3 | async-start | bytes 2097152 | tf_op jit(solution)/shard_map/all_to_all | solution.py:462
  78.4 11.2 %shard_map.18 = (f32[256,256]{1,0:T(8,128)S(1)}, f32[256,256]{1,0:T(8,128)}, f32[256,256]{1,0:T(8,128)}, f32[256,256]{1,0:T(8,128)}) custom-call(s32[5]{0:T(128)S(1)} %stack.36.at_ref, f32[16,8,256]{2,1,0:T(8,128)S(1)} %slice_bitcast_fusion.3.own_ref, f32[16,8,256]{2,1,0:T(8,128)S(1)} %slice_bitcast_fusion.2.other_ref), custom_call_target="tpu_custom_call" | custom-call | flops 10000000000 | bytes 1048576 | tf_op jit(solution)/shard_map/pallas_call | solution.py:530
  89.7 0.8 copy-done.9
  90.4 0.8 copy-done.10
  91.2 5.8 %shard_map.19 = (f32[8,128,256]{2,1,0:T(8,128)S(1)}, f32[8,128,256]{2,1,0:T(8,128)}, f32[256,512]{1,0:T(8,128)}) custom-call(s32[5]{0:T(128)S(1)} %stack.36.at_ref, f32[8192,128]{1,0:T(8,128)S(1)} %bitcast.41, f32[1024,128]{1,0:T(8,128)} %copy-done.7, f32[1024,128]{1,0:T(8,128)} %copy-done.10, f32[1024,128]{1,0:T(8,128)} %copy-done.9, ...), custom_call_target="tpu_custom_call" | custom-call | flops 3221225472 | bytes 9437184 | tf_op jit(solution)/shard_map/pallas_call | solution.py:542
  97.1 0.4 collective-permute-start.6
  97.5 2.6 %collective-permute-done.6 = f32[8,128,256]{2,1,0:T(8,128)S(1)} collective-permute-done((f32[8,128,256]{2,1,0:T(8,128)}, f32[8,128,256]{2,1,0:T(8,128)S(1)}, u32[]{:S(2)}, u32[]{:S(2)}) %collective-permute-start.6) | collective-permute-done | bytes 1048608 | tf_op jit(solution)/shard_map/ppermute | solution.py:559
  100.0 1.1 copy_bitcast_fusion
  101.2 0.3 collective-permute-start.7
  101.5 6.9 %all-to-all-start.4 = ((f32[16,8,8,256]{3,2,1,0:T(8,128)}), f32[16,8,8,256]{3,2,1,0:T(8,128)S(1)}, u32[]{:S(2)}, u32[]{:S(2)}) async-start(f32[16,8,8,256]{3,2,1,0:T(8,128)} %copy_bitcast_fusion), calls=%async_computation.4 | async-start | bytes 2097152 | tf_op jit(solution)/shard_map/all_to_all | solution.py:562
  108.4 7.0 %shard_map.20 = (f32[8,256,256]{2,1,0:T(8,128)}, f32[8,2048]{1,0:T(8,128)S(1)}) custom-call(s32[5]{0:T(128)S(1)} %stack.36.at_ref, f32[16,8,8,256]{3,2,1,0:T(8,128)S(1)} %all-to-all-done.3.own_ref, f32[16,8,8,256]{3,2,1,0:T(8,128)} %collective-permute-done.7.other_ref, f32[256,256]{1,0:T(8,128)S(1)} %copy-done.4), custom_call_target="tpu_custom_call" | custom-call | flops 5000000000 | bytes 6291456 | tf_op jit(solution)/shard_map/pallas_call | solution.py:563
  115.4 9.1 %all-to-all-done.4.after_ref = f32[16,8,8,256]{3,2,1,0:T(8,128)S(1)} async-done(((f32[16,8,8,256]{3,2,1,0:T(8,128)}), f32[16,8,8,256]{3,2,1,0:T(8,128)S(1)}, u32[]{:S(2)}, u32[]{:S(2)}) %all-to-all-start.4) | async-done | bytes 1048608 | tf_op jit(solution)/shard_map/all_to_all | solution.py:562
  124.5 0.1 collective-permute-start.8
  124.6 1.1 broadcast_in_dim.13
  125.7 4.6 %all-to-all-start.5 = ((f32[16,8,8,256]{3,2,1,0:T(8,128)}), f32[16,8,8,256]{3,2,1,0:T(8,128)}, u32[]{:S(2)}, u32[]{:S(2)}) async-start(f32[16,8,8,256]{3,2,1,0:T(8,128)} %broadcast_in_dim.13), calls=%async_computation.5 | async-start | bytes 2097152 | tf_op jit(solution)/shard_map/all_to_all | solution.py:462
  130.3 2.0 %collective-permute-done.8 = f32[1,8,8,256]{3,2,1,0:T(8,128)S(1)} collective-permute-done((f32[1,8,8,256]{3,2,1,0:T(8,128)S(1)}, f32[1,8,8,256]{3,2,1,0:T(8,128)S(1)}, u32[]{:S(2)}, u32[]{:S(2)}) %collective-permute-start.8) | collective-permute-done | bytes 65568 | tf_op jit(solution)/shard_map/ppermute | solution.py:466
  132.3 0.3 collective-permute-start.9
  132.6 12.8 %shard_map.21.mixer_ref = f32[256,256]{1,0:T(8,128)S(1)} custom-call(s32[5]{0:T(128)S(1)} %stack.36.at_ref, f32[16,2,8,256]{3,2,1,0:T(8,128)S(1)} %all-to-all-done.2.own_ref, f32[16,2,8,256]{3,2,1,0:T(8,128)S(1)} %collective-permute-done.5.other_ref, f32[256,256]{1,0:T(8,128)S(1)} %copy-done.5, f32[16,8,8,256]{3,2,1,0:T(8,128)S(1)} %all-to-all-done.4.after_ref), custom_call_target="tpu_custom_call" | custom-call | flops 10000000000 | bytes 1048576 | tf_op jit(solution)/shard_map/pallas_call | solution.py:577
  145.5 3.8 %collective-permute-start.10 = (f32[16,8,8,256]{3,2,1,0:T(8,128)}, f32[16,8,8,256]{3,2,1,0:T(8,128)S(1)}, u32[]{:S(2)}, u32[]{:S(2)}) collective-permute-start(f32[16,8,8,256]{3,2,1,0:T(8,128)} %all-to-all-done.5.own_hbm), channel_id=1, source_target_pairs={{0,1},{1,0},{2,3},{3,2},{4,5},{5,4},{6,7},{7,6},{8,9},{9,8},{10,11... | collective-permute-start | bytes 3145736 | tf_op jit(solution)/shard_map/ppermute | solution.py:586
  149.2 1.2 collective-permute-start.11
  150.4 1.3 collective-permute-done.10.other_hbm
  151.7 1.0 copy-done.6
  152.7 4.2 %shard_map.22 = f32[8,8,256]{2,1,0:T(8,128)} custom-call(s32[5]{0:T(128)S(1)} %stack.36.at_ref, f32[8,2048]{1,0:T(8,128)S(1)} %get-tuple-element.53.slab_ref, f32[16,8,8,256]{3,2,1,0:T(8,128)} %all-to-all-done.5.own_hbm, f32[16,8,8,256]{3,2,1,0:T(8,128)} %copy-done.6), custom_call_target="tpu_custom_call" | custom-call | flops 1000000000 | bytes 4194304 | tf_op jit(solution)/shard_map/pallas_call | solution.py:590
  156.9 5.8 %all-to-all-start.6 = ((f32[8,8,256]{2,1,0:T(8,128)}), f32[8,8,256]{2,1,0:T(8,128)S(1)}, u32[]{:S(2)}, u32[]{:S(2)}) async-start(f32[8,8,256]{2,1,0:T(8,128)} %shard_map.22), calls=%async_computation.6 | async-start | bytes 131072 | tf_op jit(solution)/shard_map/all_to_all | solution.py:598
  162.8 7.2 %all-to-all-done.6.pieces_ref = f32[8,8,256]{2,1,0:T(8,128)S(1)} async-done(((f32[8,8,256]{2,1,0:T(8,128)}), f32[8,8,256]{2,1,0:T(8,128)S(1)}, u32[]{:S(2)}, u32[]{:S(2)}) %all-to-all-start.6) | async-done | bytes 65568 | tf_op jit(solution)/shard_map/all_to_all | solution.py:598
  170.0 1.1 shard_map.23
  171.1 21.5 %all_to_all.41 = f32[32,3,8,256]{3,2,1,0:T(8,128)S(1)} all-to-all(f32[32,3,8,256]{3,2,1,0:T(8,128)S(1)} %shard_map.23), channel_id=1, replica_groups=mesh['prow'=8,'pcol'=32] {'pcol'}, dimensions={0} | all-to-all | bytes 1572864 | tf_op jit(solution)/shard_map/all_to_all | solution.py:608
  192.6 9.0 %shard_map.24 = f32[8192,128]{1,0:T(8,128)} custom-call(s32[5]{0:T(128)S(1)} %stack.36.at_ref, f32[8192,128]{1,0:T(8,128)} %bitcast.40, f32[8,256,256]{2,1,0:T(8,128)S(1)} %copy-done.1, f32[16,8,8,256]{3,2,1,0:T(8,128)} %all-to-all-done.5.own_hbm, f32[16,8,8,256]{3,2,1,0:T(8,128)} %copy-done.6, f32[16,2,3,8,256]{4,3,2,1,0:T(8,128)S(1)} %bitcast.42, ...), custom_call_target="tpu_custom_call" | custom-call | flops 3221225472 | bytes 12582912 | tf_op jit(solution)/shard_map/pallas_call | solution.py:609
  (42 shorter events, 0.4 us)
Async XLA Ops:
  5.7 7.0 %collective-permute-start.2 = (f32[16,9,8,256]{3,2,1,0:T(8,128)S(1)}, f32[16,9,8,256]{3,2,1,0:T(8,128)}, u32[]{:S(2)}, u32[]{:S(2)}) collective-permute-start(f32[16,9,8,256]{3,2,1,0:T(8,128)S(1)} %slice_bitcast_fusion), channel_id=1, source_target_pairs={{0,1},{32,33},{64,65},{96,97},{128,129},{160,161},{192,193},{224,2... | collective-permute-start | bytes 3538952 | tf_op jit(solution)/shard_map/ppermute | solution.py:518
  15.2 22.7 %all-to-all-start = ((f32[16,9,8,256]{3,2,1,0:T(8,128)}), f32[16,9,8,256]{3,2,1,0:T(8,128)S(1)}, u32[]{:S(2)}, u32[]{:S(2)}) async-start(f32[16,9,8,256]{3,2,1,0:T(8,128)} %fusion), calls=%async_computation | async-start | bytes 2359296 | tf_op jit(solution)/shard_map/all_to_all | solution.py:520
  20.1 18.3 %collective-permute-start.1 = (f32[1024,128]{1,0:T(8,128)S(1)}, f32[1024,128]{1,0:T(8,128)S(1)}, u32[]{:S(2)}, u32[]{:S(2)}) collective-permute-start(f32[1024,128]{1,0:T(8,128)S(1)} %bitcast.43), channel_id=1, source_target_pairs={{0,192},{1,193},{2,194},{3,195},{4,196},{5,197},{6,198},{7,199},{8... | collective-permute-start | bytes 1572872 | tf_op jit(solution)/shard_map/ppermute | solution.py:466
  26.8 13.0 %collective-permute-start = (f32[1024,128]{1,0:T(8,128)S(1)}, f32[1024,128]{1,0:T(8,128)S(1)}, u32[]{:S(2)}, u32[]{:S(2)}) collective-permute-start(f32[1024,128]{1,0:T(8,128)S(1)} %bitcast.44), channel_id=1, source_target_pairs={{0,96},{1,97},{2,98},{3,99},{4,100},{5,101},{6,102},{7,103},{8,104... | collective-permute-start | bytes 1572872 | tf_op jit(solution)/shard_map/ppermute | solution.py:466
  39.8 14.0 %copy-start.8 = (f32[1024,128]{1,0:T(8,128)}, f32[1024,128]{1,0:T(8,128)S(1)}, u32[]{:S(2)}) copy-start(f32[1024,128]{1,0:T(8,128)S(1)} %collective-permute-done) | copy-start | bytes 1572868
  53.7 13.4 %all-to-all-start.2 = ((f32[16,2,8,256]{3,2,1,0:T(8,128)}), f32[16,2,8,256]{3,2,1,0:T(8,128)S(1)}, u32[]{:S(2)}, u32[]{:S(2)}) async-start(f32[16,2,8,256]{3,2,1,0:T(8,128)} %broadcast_in_dim.11), calls=%async_computation.2 | async-start | bytes 524288 | tf_op jit(solution)/shard_map/all_to_all | solution.py:462
  60.9 13.8 %copy-start.7 = (f32[1024,128]{1,0:T(8,128)}, f32[1024,128]{1,0:T(8,128)S(1)}, u32[]{:S(2)}) copy-start(f32[1024,128]{1,0:T(8,128)S(1)} %add_select_fusion.top_hbm) | copy-start | bytes 1572868
  67.2 11.2 %collective-permute-start.5 = (f32[16,2,8,256]{3,2,1,0:T(8,128)S(1)}, f32[16,2,8,256]{3,2,1,0:T(8,128)S(1)}, u32[]{:S(2)}, u32[]{:S(2)}) collective-permute-start(f32[16,2,8,256]{3,2,1,0:T(8,128)S(1)} %all-to-all-done.2.own_ref), channel_id=1, source_target_pairs={{0,1},{1,0},{2,3},{3,2},{4,5},{5,4},{6,7},{7,6},{8,9},{9,8},{10,11... | collective-permute-start | bytes 786440 | tf_op jit(solution)/shard_map/ppermute | solution.py:528
  70.8 18.9 %collective-permute-start.4 = (f32[1024,128]{1,0:T(8,128)S(1)}, f32[1024,128]{1,0:T(8,128)S(1)}, u32[]{:S(2)}, u32[]{:S(2)}) collective-permute-start(f32[1024,128]{1,0:T(8,128)S(1)} %add_select_fusion.top_hbm), channel_id=1, source_target_pairs={{0,224},{96,64},{192,160},{1,225},{97,65},{193,161},{2,226},{98,66... | collective-permute-start | bytes 1572872 | tf_op jit(solution)/shard_map/ppermute | solution.py:466
  72.3 17.4 %collective-permute-start.3 = (f32[1024,128]{1,0:T(8,128)S(1)}, f32[1024,128]{1,0:T(8,128)S(1)}, u32[]{:S(2)}, u32[]{:S(2)}) collective-permute-start(f32[1024,128]{1,0:T(8,128)S(1)} %add_select_fusion.top_hbm), channel_id=1, source_target_pairs={{0,32},{96,128},{1,33},{97,129},{2,34},{98,130},{3,35},{99,131},{4... | collective-permute-start | bytes 1572872 | tf_op jit(solution)/shard_map/ppermute | solution.py:466
  74.7 22.4 %all-to-all-start.3 = ((f32[16,8,8,256]{3,2,1,0:T(8,128)}), f32[16,8,8,256]{3,2,1,0:T(8,128)S(1)}, u32[]{:S(2)}, u32[]{:S(2)}) async-start(f32[16,8,8,256]{3,2,1,0:T(8,128)} %broadcast_in_dim.12), calls=%async_computation.3 | async-start | bytes 2097152 | tf_op jit(solution)/shard_map/all_to_all | solution.py:462
  78.4 12.8 %copy-start = (f32[8,256,2,256]{3,2,1,0:T(2,128)S(1)}, f32[8,256,2,256]{3,2,1,0:T(2,128)}, u32[]{:S(2)}) copy-start(f32[8,256,2,256]{3,2,1,0:T(2,128)} %param.1) | copy-start | bytes 12582916
  89.7 0.8 copy-start.9
  90.4 0.8 copy-start.10
  97.1 3.0 %collective-permute-start.6 = (f32[8,128,256]{2,1,0:T(8,128)}, f32[8,128,256]{2,1,0:T(8,128)S(1)}, u32[]{:S(2)}, u32[]{:S(2)}) collective-permute-start(f32[8,128,256]{2,1,0:T(8,128)} %get-tuple-element.42), channel_id=1, source_target_pairs={{0,1},{1,0},{2,3},{3,2},{4,5},{5,4},{6,7},{7,6},{8,9},{9,8},{10,11... | collective-permute-start | bytes 3145736 | tf_op jit(solution)/shard_map/ppermute | solution.py:559
  101.2 7.3 %copy-start.4 = (f32[256,256]{1,0:T(8,128)S(1)}, f32[256,256]{1,0:T(8,128)}, u32[]{:S(2)}) copy-start(f32[256,256]{1,0:T(8,128)} %get-tuple-element.45.inv_t_ref) | copy-start | bytes 786436
  101.2 7.3 %collective-permute-start.7 = (f32[16,8,8,256]{3,2,1,0:T(8,128)S(1)}, f32[16,8,8,256]{3,2,1,0:T(8,128)}, u32[]{:S(2)}, u32[]{:S(2)}) collective-permute-start(f32[16,8,8,256]{3,2,1,0:T(8,128)S(1)} %all-to-all-done.3.own_ref), channel_id=1, source_target_pairs={{0,1},{1,0},{2,3},{3,2},{4,5},{5,4},{6,7},{7,6},{8,9},{9,8},{10,11... | collective-permute-start | bytes 3145736 | tf_op jit(solution)/shard_map/ppermute | solution.py:561
  101.5 23.0 %all-to-all-start.4 = ((f32[16,8,8,256]{3,2,1,0:T(8,128)}), f32[16,8,8,256]{3,2,1,0:T(8,128)S(1)}, u32[]{:S(2)}, u32[]{:S(2)}) async-start(f32[16,8,8,256]{3,2,1,0:T(8,128)} %copy_bitcast_fusion), calls=%async_computation.4 | async-start | bytes 2097152 | tf_op jit(solution)/shard_map/all_to_all | solution.py:562
  124.5 7.8 %collective-permute-start.8 = (f32[1,8,8,256]{3,2,1,0:T(8,128)S(1)}, f32[1,8,8,256]{3,2,1,0:T(8,128)S(1)}, u32[]{:S(2)}, u32[]{:S(2)}) collective-permute-start(f32[1,8,8,256]{3,2,1,0:T(8,128)S(1)} %bitcast.46), channel_id=1, source_target_pairs={{0,128},{32,160},{64,192},{96,224},{128,0},{160,32},{192,64},{224,... | collective-permute-start | bytes 196616 | tf_op jit(solution)/shard_map/ppermute | solution.py:466
  125.7 6.9 %copy-start.5 = (f32[256,256]{1,0:T(8,128)S(1)}, f32[256,256]{1,0:T(8,128)}, u32[]{:S(2)}) copy-start(f32[256,256]{1,0:T(8,128)} %get-tuple-element.50.inv_ref) | copy-start | bytes 786436
  125.7 19.8 %all-to-all-start.5 = ((f32[16,8,8,256]{3,2,1,0:T(8,128)}), f32[16,8,8,256]{3,2,1,0:T(8,128)}, u32[]{:S(2)}, u32[]{:S(2)}) async-start(f32[16,8,8,256]{3,2,1,0:T(8,128)} %broadcast_in_dim.13), calls=%async_computation.5 | async-start | bytes 2097152 | tf_op jit(solution)/shard_map/all_to_all | solution.py:462
  132.3 13.1 %collective-permute-start.9 = (f32[2,8,8,256]{3,2,1,0:T(8,128)S(1)}, f32[2,8,8,256]{3,2,1,0:T(8,128)S(1)}, u32[]{:S(2)}, u32[]{:S(2)}) collective-permute-start(f32[2,8,8,256]{3,2,1,0:T(8,128)S(1)} %pad_maximum_fusion.1), channel_id=1, source_target_pairs={{0,64},{32,96},{64,0},{96,32},{128,192},{160,224},{192,128},{224,1... | collective-permute-start | bytes 393224 | tf_op jit(solution)/shard_map/ppermute | solution.py:466
  145.5 6.3 %collective-permute-start.10 = (f32[16,8,8,256]{3,2,1,0:T(8,128)}, f32[16,8,8,256]{3,2,1,0:T(8,128)S(1)}, u32[]{:S(2)}, u32[]{:S(2)}) collective-permute-start(f32[16,8,8,256]{3,2,1,0:T(8,128)} %all-to-all-done.5.own_hbm), channel_id=1, source_target_pairs={{0,1},{1,0},{2,3},{3,2},{4,5},{5,4},{6,7},{7,6},{8,9},{9,8},{10,11... | collective-permute-start | bytes 3145736 | tf_op jit(solution)/shard_map/ppermute | solution.py:586
  149.2 13.5 %collective-permute-start.11 = (f32[4,8,8,256]{3,2,1,0:T(8,128)S(1)}, f32[4,8,8,256]{3,2,1,0:T(8,128)}, u32[]{:S(2)}, u32[]{:S(2)}) collective-permute-start(f32[4,8,8,256]{3,2,1,0:T(8,128)S(1)} %pad_maximum_fusion.four_ref), channel_id=1, source_target_pairs={{0,32},{32,0},{64,96},{96,64},{128,160},{160,128},{192,224},{224,1... | collective-permute-start | bytes 786440 | tf_op jit(solution)/shard_map/ppermute | solution.py:466
  151.7 1.0 copy-start.6
  156.9 13.1 %all-to-all-start.6 = ((f32[8,8,256]{2,1,0:T(8,128)}), f32[8,8,256]{2,1,0:T(8,128)S(1)}, u32[]{:S(2)}, u32[]{:S(2)}) async-start(f32[8,8,256]{2,1,0:T(8,128)} %shard_map.22), calls=%async_computation.6 | async-start | bytes 131072 | tf_op jit(solution)/shard_map/all_to_all | solution.py:598
  162.7 29.9 %copy-start.1 = (f32[8,256,256]{2,1,0:T(8,128)S(1)}, f32[8,256,256]{2,1,0:T(8,128)}, u32[]{:S(2)}) copy-start(f32[8,256,256]{2,1,0:T(8,128)} %get-tuple-element.46.left_hbm) | copy-start | bytes 6291460
  162.7 29.9 %copy-start.2 = (f32[256,512]{1,0:T(8,128)S(1)}, f32[256,512]{1,0:T(8,128)}, u32[]{:S(2)}) copy-start(f32[256,512]{1,0:T(8,128)} %get-tuple-element.57.y_hbm) | copy-start | bytes 1572868
  162.8 29.8 %copy-start.3 = (f32[256,256]{1,0:T(8,128)S(1)}, f32[256,256]{1,0:T(8,128)}, u32[]{:S(2)}) copy-start(f32[256,256]{1,0:T(8,128)} %get-tuple-element.58.upper_hbm) | copy-start | bytes 786436
